TPU v7x, 32 devices: a whole 2x2x4 slice. The times are simulated.
32 devices in a mesh: grp: 8 (over z, x), exp: 4 (over y, core).
Axes of the slice: x: 2, y: 2, z: 4, core: 2. Of those that a mesh axis runs over, the one named last changes fastest.
Arguments:
- layer_input: bfloat16 [4096, 2048], P(('grp', 'exp')), may hold values from -6 to 6
- out_grad: bfloat16 [4096, 2048], P(('grp', 'exp')), may hold values from -6 to 6
- doc_lengths: int32 [8, 2], P('grp'), may hold values from 64 to 448, as said below
- block_order: int32 [8, 8], P('grp'), may hold values from 0 to 7, as said below
- attn_route: int32 [4096, 2], P('grp'), may hold values from 0 to 3, all different within a row; in each aligned block of 128 rows (0 to 127, 128 to 255, ...) at most 96 rows name the same one
- ffn_route: int32 [4096, 2], P('grp'), may hold values from 0 to 3, all different within a row; in each aligned block of 128 rows (0 to 127, 128 to 255, ...) at most 96 rows name the same one
- norm_gains: float32 [2048, 2], P(('grp', 'exp')), may hold values from 0.5 to 1.5
- kv_master: float32 [2048, 4096], P(('grp', 'exp')), may hold values from -0.125 to 0.125
- router_master: float32 [2048, 8], P(('grp', 'exp')), may hold values from -0.09375 to 0.09375
- query_master: float32 [4, 2048, 2048], P('exp', 'grp'), may hold values from -0.125 to 0.125
- output_master: float32 [4, 2048, 2048], P('exp', 'grp'), may hold values from -1 to 1
- gate_up_master: float32 [4, 5632, 2, 2048], P('exp', 'grp'), may hold values from -0.125 to 0.125
- down_master: float32 [4, 5632, 2048], P('exp', 'grp'), may hold values from -0.109375 to 0.109375
Outputs:
- layer_output: bfloat16 [4096, 2048], P(('grp', 'exp'))
- input_grad: float32 [4096, 2048], P(('grp', 'exp'))
- gain_grad: float32 [2048, 2], P(('grp', 'exp'))
- kv_grad: float32 [2048, 4096], P(('grp', 'exp'))
- router_grad: float32 [2048, 8], P(('grp', 'exp'))
- query_grad: float32 [4, 2048, 2048], P('exp', 'grp')
- output_grad: float32 [4, 2048, 2048], P('exp', 'grp')
- gate_up_grad: float32 [4, 5632, 2, 2048], P('exp', 'grp')
- down_grad: float32 [4, 5632, 2048], P('exp', 'grp')
Inputs may be any that keep to these rules, and one draw needn't show every extreme that they name: `doc_lengths`: each row: the lengths of the group's two documents in stream order, summing to 512. In every draw some group has one document of exactly 64 tokens and one of 448. `block_order`: each row names every block once; the two dealt blocks of one device are b and 7 - b. `attn_route`: A row names two different experts. Among the 128 rows of one device no expert is named by more than 96 rows, a bound that some block reaches. `ffn_route`: A row names two different experts. Among the 128 rows of one device no expert is named by more than 96 rows, a bound that some block reaches.
All inputs are finite; a program needn't handle non-finite values.
Results may differ from a plain program's by a relative error of at most 0.02.
Values may be sent and summed in bfloat16 or wider, within the bound.
A program may use at most 384 MiB of HBM per device.

v0:
```python
import math

import jax
import jax.numpy as jnp
from jax import lax
from jax.sharding import PartitionSpec as P

HEADS = 16


epsilon = 1e-05
negative = -1e30
highest = lax.Precision.HIGHEST


def rotate(values, positions, sign, heads):
    count = values.shape[0]
    head_size = values.shape[1] // heads
    half = head_size // 2
    split = values.reshape(count, heads, head_size)
    freq = jnp.exp(jnp.arange(half, dtype=jnp.float32) * (-2.0 * math.log(10000.0) / head_size))
    angle = positions.astype(jnp.float32)[:, None] * freq[None, :]
    cosine = jnp.cos(angle)[:, None, :]
    sine = sign * jnp.sin(angle)[:, None, :]
    first = split[:, :, :half]
    second = split[:, :, half:]
    turned = jnp.concatenate(
        [first * cosine - second * sine, second * cosine + first * sine], axis=2
    )
    return turned.reshape(count, heads * head_size)


def layout(lengths, order, group_rows, block):
    places = jnp.arange(group_rows, dtype=jnp.int32)
    anchor = order[places // block] * block + places % block
    first = lengths[0]
    doc = (anchor >= first).astype(jnp.int32)
    return (anchor, doc, anchor - doc * first)


def destinations(routes, members, experts, capacity):
    local_rows = routes.shape[0] // members
    flat = routes.reshape(members, local_rows * 2)
    onehot = (flat[:, :, None] == jnp.arange(experts, dtype=jnp.int32)[None, None, :]).astype(
        jnp.int32
    )
    before = jnp.cumsum(onehot, axis=1) - onehot
    slot = jnp.sum(before * onehot, axis=2)
    return (flat * capacity + slot).reshape(members, local_rows, 2)


def dispatch_pair(dest, slots):
    targets = jnp.arange(slots, dtype=jnp.int32)[:, None]
    first = (dest[None, :, 0] == targets).astype(jnp.bfloat16)
    second = (dest[None, :, 1] == targets).astype(jnp.bfloat16)
    return (first, second)


def arrivals(dest_all, anchor, doc, place, member, local_slots):
    members = dest_all.shape[0]
    local_rows = dest_all.shape[1]
    targets = member * local_slots + jnp.arange(local_slots, dtype=jnp.int32)
    hits = jnp.sum(
        (dest_all[:, None, :, :] == targets[None, :, None, None]).astype(jnp.int32), axis=3
    )
    filled = jnp.sum(hits, axis=2)

    def pulled(values):
        return jnp.sum(hits * values.reshape(members, 1, local_rows), axis=2)

    return (pulled(anchor), jnp.where(filled > 0, pulled(doc), -1), pulled(place))


def slot_values(values, per_device, index):
    return values.reshape(values.shape[0], per_device, -1)[:, index].reshape(-1)


def expert_rows(buffer, sources, per_device, index):
    capacity = buffer.shape[1]
    width = buffer.shape[2]
    return buffer.reshape(sources, per_device, capacity, width)[:, index].reshape(
        sources * capacity, width
    )


def expert_buffer(pieces, sources, capacity):
    shaped = [piece.reshape(sources, 1, capacity, piece.shape[-1]) for piece in pieces]
    joined = shaped[0]
    return joined.reshape(sources * len(pieces), capacity, joined.shape[-1])


def pick_gates(logits, routes, experts):
    chosen = (routes[:, :, None] == jnp.arange(experts, dtype=jnp.int32)[None, None, :]).astype(
        jnp.float32
    )
    picked = jnp.sum(chosen * logits[:, None, :], axis=2)
    return (chosen, jax.nn.softmax(picked, axis=1))


def logit_grad(chosen, gates, gate_grad):
    inner = jnp.sum(gates * gate_grad, axis=1, keepdims=True)
    picked_grad = gates * (gate_grad - inner)
    return jnp.sum(chosen * picked_grad[:, :, None], axis=1)


def norm_back(grad_hidden, normed, inverse, gain):
    grad_normed = grad_hidden * gain
    gain_grad = jnp.sum(grad_hidden * normed, axis=0)
    mean_term = jnp.mean(grad_normed * normed, axis=1, keepdims=True)
    return (inverse * (grad_normed - normed * mean_term), gain_grad)


def block_scores(query_heads, key_part, key_anchor, key_doc, query_anchor, query_doc, scale):
    key_heads = key_part.reshape(key_part.shape[0], query_heads.shape[1], query_heads.shape[2])
    scores = (
        jnp.einsum("qhd,khd->hqk", query_heads, key_heads, preferred_element_type=jnp.float32)
        * scale
    )
    allowed = (query_doc[:, None] == key_doc[None, :]) & (
        key_anchor[None, :] <= query_anchor[:, None]
    )
    return jnp.where(allowed[None], scores, negative)


def key_parts(full_kv, key_anchor, key_doc, key_block):
    blocks = full_kv.shape[0] // key_block
    return (
        full_kv.reshape(blocks, key_block, full_kv.shape[1]),
        key_anchor.reshape(blocks, key_block),
        key_doc.reshape(blocks, key_block),
    )


def attend_forward(query, full_kv, query_anchor, query_doc, key_anchor, key_doc, heads, key_block):
    count, width = query.shape
    head_size = width // heads
    scale = 1.0 / math.sqrt(head_size)
    query_heads = query.reshape(count, heads, head_size)
    parts = key_parts(full_kv, key_anchor, key_doc, key_block)

    def measure(carry, part):
        running, total = carry
        scores = block_scores(
            query_heads, part[0][:, :width], part[1], part[2], query_anchor, query_doc, scale
        )
        raised = jnp.maximum(running, jnp.max(scores, axis=2))
        total = total * jnp.exp(running - raised) + jnp.sum(
            jnp.exp(scores - raised[:, :, None]), axis=2
        )
        return ((raised, total), None)

    start = (
        jnp.full((heads, count), negative, jnp.float32),
        jnp.zeros((heads, count), jnp.float32),
    )
    (running, total), _ = lax.scan(measure, start, parts)
    log_total = running + jnp.log(total)

    def collect(accum, part):
        scores = block_scores(
            query_heads, part[0][:, :width], part[1], part[2], query_anchor, query_doc, scale
        )
        weights = jnp.exp(scores - log_total[:, :, None]).astype(jnp.bfloat16)
        value_heads = part[0][:, width:].reshape(key_block, heads, head_size)
        return (
            accum
            + jnp.einsum("hqk,khd->qhd", weights, value_heads, preferred_element_type=jnp.float32),
            None,
        )

    attended, _ = lax.scan(collect, jnp.zeros((count, heads, head_size), jnp.float32), parts)
    return (attended.reshape(count, width), log_total)


def attend_backward(
    query,
    full_kv,
    attended_grad,
    attended,
    log_total,
    query_anchor,
    query_doc,
    key_anchor,
    key_doc,
    heads,
    key_block,
):
    count, width = query.shape
    head_size = width // heads
    scale = 1.0 / math.sqrt(head_size)
    query_heads = query.reshape(count, heads, head_size)
    grad_heads = attended_grad.reshape(count, heads, head_size)
    delta = jnp.sum(
        (attended_grad.astype(jnp.float32) * attended).reshape(count, heads, head_size), axis=2
    ).T
    parts = key_parts(full_kv, key_anchor, key_doc, key_block)

    def sweep(query_grad, part):
        key_part = part[0][:, :width]
        key_heads = key_part.reshape(key_block, heads, head_size)
        value_heads = part[0][:, width:].reshape(key_block, heads, head_size)
        scores = block_scores(
            query_heads, key_part, part[1], part[2], query_anchor, query_doc, scale
        )
        probs = jnp.exp(scores - log_total[:, :, None])
        prob_grad = jnp.einsum(
            "qhd,khd->hqk", grad_heads, value_heads, preferred_element_type=jnp.float32
        )
        score_grad = (probs * (prob_grad - delta[:, :, None])).astype(jnp.bfloat16)
        query_grad = query_grad + jnp.einsum(
            "hqk,khd->qhd", score_grad, key_heads, preferred_element_type=jnp.float32
        )
        key_grad = (
            jnp.einsum("hqk,qhd->khd", score_grad, query_heads, preferred_element_type=jnp.float32)
            * scale
        )
        value_grad = jnp.einsum(
            "hqk,qhd->khd",
            probs.astype(jnp.bfloat16),
            grad_heads,
            preferred_element_type=jnp.float32,
        )
        joined = jnp.concatenate(
            [key_grad.reshape(key_block, width), value_grad.reshape(key_block, width)], axis=1
        )
        return (query_grad, joined)

    query_grad, kv_grad = lax.scan(sweep, jnp.zeros((count, heads, head_size), jnp.float32), parts)
    return (query_grad.reshape(count, width) * scale, kv_grad.reshape(full_kv.shape[0], 2 * width))


def expert_ffn(routed, routed_grad, gate_up, down):
    gate = jnp.einsum("td,fd->tf", routed, gate_up[:, 0, :], preferred_element_type=jnp.float32)
    up = jnp.einsum("td,fd->tf", routed, gate_up[:, 1, :], preferred_element_type=jnp.float32)
    sigmoid = jax.nn.sigmoid(gate)
    act = (gate * sigmoid * up).astype(jnp.bfloat16)
    produced = jnp.dot(act, down, preferred_element_type=jnp.float32)
    act_grad = jnp.einsum("td,fd->tf", routed_grad, down, preferred_element_type=jnp.float32)
    gate_grad = (act_grad * up * sigmoid * (1.0 + gate * (1.0 - sigmoid))).astype(jnp.bfloat16)
    up_grad = (act_grad * gate * sigmoid).astype(jnp.bfloat16)
    sent_back = jnp.dot(gate_grad, gate_up[:, 0, :], preferred_element_type=jnp.float32)
    sent_back = sent_back + jnp.dot(up_grad, gate_up[:, 1, :], preferred_element_type=jnp.float32)
    grad_down = jnp.einsum("tf,td->fd", act, routed_grad, preferred_element_type=jnp.float32)
    grad_gate = jnp.einsum("tf,td->fd", gate_grad, routed, preferred_element_type=jnp.float32)
    grad_up = jnp.einsum("tf,td->fd", up_grad, routed, preferred_element_type=jnp.float32)
    return (produced, sent_back, jnp.stack([grad_gate, grad_up], axis=1), grad_down)


def gather_pair(first, second):
    return (
        lax.all_gather(first.astype(jnp.bfloat16), "grp", axis=1, tiled=True),
        lax.all_gather(second.astype(jnp.bfloat16), "grp", axis=1, tiled=True),
    )


def scatter_pair(first, second):
    return (
        lax.psum_scatter(first.astype(jnp.bfloat16), "grp", scatter_dimension=1, tiled=True).astype(
            jnp.float32
        ),
        lax.psum_scatter(
            second.astype(jnp.bfloat16), "grp", scatter_dimension=1, tiled=True
        ).astype(jnp.float32),
    )


def body(
    layer_input,
    out_grad,
    doc_lengths,
    block_order,
    attn_route,
    ffn_route,
    norm_gains,
    kv_master,
    router_master,
    query_master,
    output_master,
    gate_up_master,
    down_master,
):
    local_rows = layer_input.shape[0]
    width = layer_input.shape[1]
    heads = HEADS
    members = lax.axis_size("exp")
    member = lax.axis_index("exp")
    per_device = query_master.shape[0]
    experts = per_device * members
    capacity = 3 * local_rows // experts
    group_rows = local_rows * members
    key_block = min(512, group_rows)
    slots_all = experts * capacity
    local_slots = per_device * capacity
    start_row = member * local_rows
    gains, kv_weight, route_weight = (
        lax.all_gather(norm_gains.astype(jnp.bfloat16), ("grp", "exp"), axis=0, tiled=True),
        lax.all_gather(kv_master.astype(jnp.bfloat16), ("grp", "exp"), axis=0, tiled=True),
        lax.all_gather(router_master.astype(jnp.bfloat16), ("grp", "exp"), axis=0, tiled=True),
    )
    query_weight, output_weight = gather_pair(query_master, output_master)
    gain_one = gains[:, 0].astype(jnp.float32)
    gain_two = gains[:, 1].astype(jnp.float32)
    route_float = route_weight.astype(jnp.float32)
    anchor, doc, place = layout(doc_lengths[0], block_order[0], group_rows, local_rows // 2)
    own_place = lax.dynamic_slice_in_dim(place, start_row, local_rows)
    inputs = layer_input.astype(jnp.float32)
    inverse_one = lax.rsqrt(jnp.mean(inputs * inputs, axis=1, keepdims=True) + epsilon)
    normed_one = inputs * inverse_one
    hidden_one = (normed_one * gain_one).astype(jnp.bfloat16)
    projected = jnp.dot(hidden_one, kv_weight, preferred_element_type=jnp.float32)
    own_kv = jnp.concatenate(
        [rotate(projected[:, :width], own_place, 1.0, heads), projected[:, width:]], axis=1
    ).astype(jnp.bfloat16)
    full_kv = lax.all_gather(own_kv, "exp", axis=0, tiled=True)
    attn_dest = destinations(attn_route, members, experts, capacity)
    own_attn_dest = lax.dynamic_index_in_dim(attn_dest, member, 0, keepdims=False)
    own_attn_route = lax.dynamic_slice_in_dim(attn_route, start_row, local_rows)
    attn_logits = jnp.dot(hidden_one, route_weight[:, :experts], preferred_element_type=jnp.float32)
    attn_chosen, attn_gates = pick_gates(attn_logits, own_attn_route, experts)
    attn_first, attn_second = dispatch_pair(own_attn_dest, slots_all)
    attn_buffer = jnp.dot(
        attn_first + attn_second, hidden_one, preferred_element_type=jnp.float32
    ).astype(jnp.bfloat16)
    arrived = lax.all_to_all(
        attn_buffer.reshape(experts, capacity, width),
        "exp",
        split_axis=0,
        concat_axis=0,
        tiled=True,
    )
    came_anchor, came_doc, came_place = arrivals(attn_dest, anchor, doc, place, member, local_slots)
    index = 0
    incoming = expert_rows(arrived, members, per_device, index)
    query_anchor = slot_values(came_anchor, per_device, index)
    query_doc = slot_values(came_doc, per_device, index)
    query_place = slot_values(came_place, per_device, index)
    query_pre = jnp.dot(incoming, query_weight[index], preferred_element_type=jnp.float32)
    query = rotate(query_pre, query_place, 1.0, heads).astype(jnp.bfloat16)
    attended, log_total = attend_forward(
        query, full_kv, query_anchor, query_doc, anchor, doc, heads, key_block
    )
    attended_low = attended.astype(jnp.bfloat16)
    mapped = jnp.dot(attended_low, output_weight[index], preferred_element_type=jnp.float32).astype(
        jnp.bfloat16
    )
    saved = [
        (incoming, query, attended, attended_low, log_total, query_anchor, query_doc, query_place)
    ]
    mapped_list = [mapped]
    attn_rows = lax.all_to_all(
        expert_buffer(mapped_list, members, capacity),
        "exp",
        split_axis=0,
        concat_axis=0,
        tiled=True,
    )
    attn_flat = attn_rows.reshape(slots_all, width)
    attn_zero = jnp.take(attn_flat, own_attn_dest[:, 0], axis=0).astype(jnp.float32)
    attn_one = jnp.take(attn_flat, own_attn_dest[:, 1], axis=0).astype(jnp.float32)
    middle = inputs + attn_gates[:, 0:1] * attn_zero + attn_gates[:, 1:2] * attn_one
    inverse_two = lax.rsqrt(jnp.mean(middle * middle, axis=1, keepdims=True) + epsilon)
    normed_two = middle * inverse_two
    hidden_two = (normed_two * gain_two).astype(jnp.bfloat16)
    ffn_dest = destinations(ffn_route, members, experts, capacity)
    own_ffn_dest = lax.dynamic_index_in_dim(ffn_dest, member, 0, keepdims=False)
    own_ffn_route = lax.dynamic_slice_in_dim(ffn_route, start_row, local_rows)
    ffn_logits = jnp.dot(hidden_two, route_weight[:, experts:], preferred_element_type=jnp.float32)
    ffn_chosen, ffn_gates = pick_gates(ffn_logits, own_ffn_route, experts)
    top_grad = out_grad.astype(jnp.float32)
    ffn_first, ffn_second = dispatch_pair(own_ffn_dest, slots_all)
    rows_buffer = jnp.dot(
        ffn_first + ffn_second, hidden_two, preferred_element_type=jnp.float32
    ).astype(jnp.bfloat16)
    grad_zero = (ffn_gates[:, 0:1] * top_grad).astype(jnp.bfloat16)
    grad_one = (ffn_gates[:, 1:2] * top_grad).astype(jnp.bfloat16)
    grads_buffer = jnp.dot(ffn_first, grad_zero, preferred_element_type=jnp.float32) + jnp.dot(
        ffn_second, grad_one, preferred_element_type=jnp.float32
    )
    ffn_rows_in, ffn_grads_in = (
        lax.all_to_all(
            rows_buffer.reshape(experts, capacity, width),
            "exp",
            split_axis=0,
            concat_axis=0,
            tiled=True,
        ),
        lax.all_to_all(
            grads_buffer.astype(jnp.bfloat16).reshape(experts, capacity, width),
            "exp",
            split_axis=0,
            concat_axis=0,
            tiled=True,
        ),
    )
    gate_up, down = gather_pair(gate_up_master, down_master)
    index = 0
    produced, sent_back, grad_pair, grad_down = expert_ffn(
        expert_rows(ffn_rows_in, members, per_device, index),
        expert_rows(ffn_grads_in, members, per_device, index),
        gate_up[index],
        down[index],
    )
    outs_list = [produced.astype(jnp.bfloat16)]
    backs_list = [sent_back.astype(jnp.bfloat16)]
    pair_grads = [grad_pair]
    down_grads = [grad_down]
    ffn_out_buffer = expert_buffer(outs_list, members, capacity)
    ffn_back_buffer = expert_buffer(backs_list, members, capacity)
    gate_up_grad, down_grad = scatter_pair(jnp.stack(pair_grads), jnp.stack(down_grads))
    ffn_result, ffn_input_grad = (
        lax.all_to_all(ffn_out_buffer, "exp", split_axis=0, concat_axis=0, tiled=True),
        lax.all_to_all(ffn_back_buffer, "exp", split_axis=0, concat_axis=0, tiled=True),
    )
    ffn_flat = ffn_result.reshape(slots_all, width)
    ffn_zero = jnp.take(ffn_flat, own_ffn_dest[:, 0], axis=0).astype(jnp.float32)
    ffn_one = jnp.take(ffn_flat, own_ffn_dest[:, 1], axis=0).astype(jnp.float32)
    final = middle + ffn_gates[:, 0:1] * ffn_zero + ffn_gates[:, 1:2] * ffn_one
    back_flat = ffn_input_grad.reshape(slots_all, width)
    back_zero = jnp.take(back_flat, own_ffn_dest[:, 0], axis=0).astype(jnp.float32)
    back_one = jnp.take(back_flat, own_ffn_dest[:, 1], axis=0).astype(jnp.float32)
    ffn_gate_grad = jnp.stack(
        [jnp.sum(top_grad * ffn_zero, axis=1), jnp.sum(top_grad * ffn_one, axis=1)], axis=1
    )
    ffn_logit_grad = logit_grad(ffn_chosen, ffn_gates, ffn_gate_grad)
    ffn_route_grad = jnp.einsum(
        "td,te->de", hidden_two.astype(jnp.float32), ffn_logit_grad, precision=highest
    )
    hidden_two_grad = (
        back_zero
        + back_one
        + jnp.einsum("te,de->td", ffn_logit_grad, route_float[:, experts:], precision=highest)
    )
    middle_part, gain_two_grad = norm_back(hidden_two_grad, normed_two, inverse_two, gain_two)
    middle_grad = top_grad + middle_part
    attn_gate_grad = jnp.stack(
        [jnp.sum(middle_grad * attn_zero, axis=1), jnp.sum(middle_grad * attn_one, axis=1)], axis=1
    )
    attn_logit_grad = logit_grad(attn_chosen, attn_gates, attn_gate_grad)
    mapped_zero = (attn_gates[:, 0:1] * middle_grad).astype(jnp.bfloat16)
    mapped_one = (attn_gates[:, 1:2] * middle_grad).astype(jnp.bfloat16)
    mapped_buffer = jnp.dot(attn_first, mapped_zero, preferred_element_type=jnp.float32) + jnp.dot(
        attn_second, mapped_one, preferred_element_type=jnp.float32
    )
    mapped_in = lax.all_to_all(
        mapped_buffer.astype(jnp.bfloat16).reshape(experts, capacity, width),
        "exp",
        split_axis=0,
        concat_axis=0,
        tiled=True,
    )
    index = 0
    incoming, query, attended, attended_low, log_total, query_anchor, query_doc, query_place = (
        saved[index]
    )
    mapped_grad = expert_rows(mapped_in, members, per_device, index)
    attended_grad = jnp.einsum(
        "td,ed->te", mapped_grad, output_weight[index], preferred_element_type=jnp.float32
    ).astype(jnp.bfloat16)
    output_grads = [
        jnp.einsum("te,td->ed", attended_low, mapped_grad, preferred_element_type=jnp.float32)
    ]
    query_grad, kv_part = attend_backward(
        query,
        full_kv,
        attended_grad,
        attended,
        log_total,
        query_anchor,
        query_doc,
        anchor,
        doc,
        heads,
        key_block,
    )
    pre_grad = rotate(query_grad, query_place, -1.0, heads).astype(jnp.bfloat16)
    query_grads = [jnp.einsum("te,td->ed", incoming, pre_grad, preferred_element_type=jnp.float32)]
    returned = [
        jnp.einsum(
            "td,ed->te", pre_grad, query_weight[index], preferred_element_type=jnp.float32
        ).astype(jnp.bfloat16)
    ]
    query_grad_out, output_grad_out = scatter_pair(jnp.stack(query_grads), jnp.stack(output_grads))
    attn_input_grad = lax.all_to_all(
        expert_buffer(returned, members, capacity), "exp", split_axis=0, concat_axis=0, tiled=True
    )
    own_kv_grad = lax.psum_scatter(
        kv_part.astype(jnp.bfloat16), "exp", scatter_dimension=0, tiled=True
    ).astype(jnp.float32)
    projected_grad = jnp.concatenate(
        [rotate(own_kv_grad[:, :width], own_place, -1.0, heads), own_kv_grad[:, width:]], axis=1
    ).astype(jnp.bfloat16)
    kv_weight_grad = jnp.einsum(
        "td,te->de", hidden_one, projected_grad, preferred_element_type=jnp.float32
    )
    input_flat = attn_input_grad.reshape(slots_all, width)
    hidden_one_grad = jnp.take(input_flat, own_attn_dest[:, 0], axis=0).astype(
        jnp.float32
    ) + jnp.take(input_flat, own_attn_dest[:, 1], axis=0).astype(jnp.float32)
    hidden_one_grad = hidden_one_grad + jnp.einsum(
        "te,de->td", projected_grad, kv_weight, preferred_element_type=jnp.float32
    )
    hidden_one_grad = hidden_one_grad + jnp.einsum(
        "te,de->td", attn_logit_grad, route_float[:, :experts], precision=highest
    )
    attn_route_grad = jnp.einsum(
        "td,te->de", hidden_one.astype(jnp.float32), attn_logit_grad, precision=highest
    )
    input_part, gain_one_grad = norm_back(hidden_one_grad, normed_one, inverse_one, gain_one)
    input_grad = middle_grad + input_part
    gain_grad, kv_grad, router_grad = (
        lax.psum_scatter(
            jnp.stack([gain_one_grad, gain_two_grad], axis=1),
            ("grp", "exp"),
            scatter_dimension=0,
            tiled=True,
        ),
        lax.psum_scatter(kv_weight_grad, ("grp", "exp"), scatter_dimension=0, tiled=True),
        lax.psum_scatter(
            jnp.concatenate([attn_route_grad, ffn_route_grad], axis=1),
            ("grp", "exp"),
            scatter_dimension=0,
            tiled=True,
        ),
    )
    return (
        final.astype(jnp.bfloat16),
        input_grad,
        gain_grad,
        kv_grad,
        router_grad,
        query_grad_out,
        output_grad_out,
        gate_up_grad,
        down_grad,
    )


def solution(mesh):
    in_specs = (
        P(("grp", "exp"), None),
        P(("grp", "exp"), None),
        P("grp", None),
        P("grp", None),
        P("grp", None),
        P("grp", None),
        P(("grp", "exp"), None),
        P(("grp", "exp"), None),
        P(("grp", "exp"), None),
        P("exp", "grp", None),
        P("exp", "grp", None),
        P("exp", "grp", None, None),
        P("exp", "grp", None),
    )
    out_specs = (
        P(("grp", "exp"), None),
        P(("grp", "exp"), None),
        P(("grp", "exp"), None),
        P(("grp", "exp"), None),
        P(("grp", "exp"), None),
        P("exp", "grp", None),
        P("exp", "grp", None),
        P("exp", "grp", None, None),
        P("exp", "grp", None),
    )
    return jax.shard_map(body, mesh=mesh, in_specs=in_specs, out_specs=out_specs, check_vma=False)
```

profile of v0, /device:TPU:22, one launch (start us, length us, event | category | flops | bytes accessed | tf_op | source)
XLA Modules:
  0.0 4064.5 jit_solution(1151985823438111053)
XLA Ops:
  12.3 30.2 all-gather
  49.8 75.8 %all-gather.9.cloned.1.call-done = bf16[2048,4096]{1,0:T(8,128)(2,1)} async-done(((bf16[64,4096]{1,0:T(8,128)(2,1)}), bf16[2048,4096]{1,0:T(8,128)(2,1)}) %all-gather.9.cloned.1.call-update) | async-done | bytes 16777232 | tf_op jit(solution)/shard_map/all_gather | solution.py:297
  177.6 44.2 %all-gather.1 = bf16[32,64,8]{1,2,0:T(8,128)(2,1)S(1)} all-gather(bf16[1,64,8]{1,2,0:T(8,128)(2,1)S(1)} %convert_bitcast_fusion.5), channel_id=1, replica_groups=mesh['grp'=8,'exp'=4] {'grp','exp'}, dimensions={0}, use_global_device_ids=true | all-gather | bytes 33792 | tf_op jit(solution)/shard_map/all_gather | solution.py:298
  224.2 27.5 all-gather.13.cloned.1.call-done
  312.3 101.3 %all-gather.15.cloned.1.call-done = bf16[1,2048,2048]{2,1,0:T(8,128)(2,1)} async-done(((bf16[1,256,2048]{2,1,0:T(8,128)(2,1)}), bf16[1,2048,2048]{2,1,0:T(8,128)(2,1)}) %all-gather.15.cloned.1.call-update) | async-done | bytes 8388624 | tf_op jit(solution)/shard_map/all_gather | solution.py:252
  426.6 18.2 all-to-all-done.1
  449.0 22.5 all_to_all.40
  471.5 816.8 %all-gather.17.cloned.1.call-done = bf16[1,5632,2,2048]{3,1,2,0:T(8,128)(2,1)} async-done(((bf16[1,704,2,2048]{3,1,2,0:T(8,128)(2,1)}), bf16[1,5632,2,2048]{3,1,2,0:T(8,128)(2,1)}) %all-gather.17.cloned.1.call-update) | async-done | bytes 46137360 | tf_op jit(solution)/shard_map/all_gather | solution.py:251
  1304.0 20.3 multiply_convert_fusion.3
  1324.3 406.5 %all-gather.19.cloned.1.call-done = bf16[1,5632,2048]{2,1,0:T(8,128)(2,1)} async-done(((bf16[1,704,2048]{2,1,0:T(8,128)(2,1)}), bf16[1,5632,2048]{2,1,0:T(8,128)(2,1)}) %all-gather.19.cloned.1.call-update) | async-done | bytes 23068688 | tf_op jit(solution)/shard_map/all_gather | solution.py:252
  1773.5 22.5 all_to_all.41
  1796.0 27.9 multiply_convert_fusion.1
  1858.1 18.4 all-to-all-done.5
  1981.7 32.6 all-to-all-done.7
  2059.2 18.8 convert_bitcast_fusion
  2078.3 18.7 convert_bitcast_fusion.1
  2097.0 18.7 convert_bitcast_fusion.2
  2115.7 30.8 pad_maximum_fusion
  2163.4 103.4 %reduce-scatter.27.cloned.1.call-done = f32[64,2]{1,0:T(8,128)} async-done(((f32[2048,2]{1,0:T(8,128)}), f32[64,2]{1,0:T(8,128)}) %reduce-scatter.27.cloned.1.call-update) | async-done | bytes 528
  2268.2 169.5 %reduce-scatter.17.cloned.1.call-done = bf16[1,256,2048]{2,1,0:T(8,128)(2,1)} async-done(((bf16[1,2048,2048]{2,1,0:T(8,128)(2,1)}), bf16[1,256,2048]{2,1,0:T(8,128)(2,1)}) %reduce-scatter.17.cloned.1.call-update) | async-done | bytes 1048592 | tf_op jit(solution)/shard_map/reduce_scatter | solution.py:258
  2440.5 148.9 %reduce-scatter.19.cloned.1.call-done = bf16[1,256,2048]{2,1,0:T(8,128)(2,1)} async-done(((bf16[1,2048,2048]{2,1,0:T(8,128)(2,1)}), bf16[1,256,2048]{2,1,0:T(8,128)(2,1)}) %reduce-scatter.19.cloned.1.call-update) | async-done | bytes 1048592 | tf_op jit(solution)/shard_map/reduce_scatter | solution.py:261
  2592.1 374.4 %reduce-scatter.23.cloned.1.call-done = bf16[1,704,2048]{2,1,0:T(8,128)(2,1)} async-done(((bf16[1,5632,2048]{2,1,0:T(8,128)(2,1)}), bf16[1,704,2048]{2,1,0:T(8,128)(2,1)}) %reduce-scatter.23.cloned.1.call-update) | async-done | bytes 2883600 | tf_op jit(solution)/shard_map/reduce_scatter | solution.py:261
  2971.7 726.4 %reduce-scatter.21.cloned.1.call-done = bf16[1,704,2,2048]{3,1,2,0:T(8,128)(2,1)} async-done(((bf16[1,5632,2,2048]{3,1,2,0:T(8,128)(2,1)}), bf16[1,704,2,2048]{3,1,2,0:T(8,128)(2,1)}) %reduce-scatter.21.cloned.1.call-update) | async-done | bytes 5767184 | tf_op jit(solution)/shard_map/reduce_scatter | solution.py:258
  3710.8 346.8 %reduce-scatter.15.cloned.1.call-done = f32[64,4096]{1,0:T(8,128)} async-done(((f32[2048,4096]{1,0:T(8,128)}), f32[64,4096]{1,0:T(8,128)}) %reduce-scatter.15.cloned.1.call-update) | async-done | bytes 1048592 | tf_op jit(solution)/shard_map/reduce_scatter | solution.py:517
  (389 shorter events, 427.5 us)
Async XLA Ops:
  7.2 118.4 %all-gather.9.cloned.1.call-start = ((), (), s32[]{:S(2)}) async-start(), calls=%async_computation.16 | async-start | bytes 17301504 | tf_op jit(solution)/shard_map/all_gather | solution.py:297
  9.4 242.3 %all-gather.13.cloned.1.call-start = ((), (), s32[]{:S(2)}) async-start(), calls=%async_computation.18 | async-start | bytes 9437184 | tf_op jit(solution)/shard_map/all_gather | solution.py:251
  12.2 275.3 %all-gather.11.cloned.1.call-start = ((), (), s32[]{:S(2)}) async-start(), calls=%async_computation.17 | async-start | bytes 5242880 | tf_op jit(solution)/shard_map/all_gather | solution.py:314
  49.8 397.5 %copy-start.42 = (f32[2048,1]{0,1:T(1,128)}, f32[2048,1]{0,1:T(1,128)S(1)}, u32[]{:S(2)}) copy-start(f32[2048,1]{0,1:T(1,128)S(1)} %get-tuple-element.192) | copy-start | bytes 24580
  136.2 277.3 %all-gather.15.cloned.1.call-start = ((), (), s32[]{:S(2)}) async-start(), calls=%async_computation.19 | async-start | bytes 9437184 | tf_op jit(solution)/shard_map/all_gather | solution.py:252
  139.3 1149.1 %all-gather.17.cloned.1.call-start = ((), (), s32[]{:S(2)}) async-start(), calls=%async_computation.20 | async-start | bytes 51904512 | tf_op jit(solution)/shard_map/all_gather | solution.py:251
  152.5 1578.3 %all-gather.19.cloned.1.call-start = ((), (), s32[]{:S(2)}) async-start(), calls=%async_computation.21 | async-start | bytes 25952256 | tf_op jit(solution)/shard_map/all_gather | solution.py:252
  171.7 92.8 %all-to-all-start = ((bf16[4,96,2048]{2,1,0:T(8,128)(2,1)}), bf16[4,96,2048]{2,1,0:T(8,128)(2,1)S(1)}, u32[]{:S(2)}, u32[]{:S(2)}) async-start(bf16[4,96,2048]{2,1,0:T(8,128)(2,1)} %bitcast.21), calls=%async_computation | async-start | bytes 3145728 | tf_op jit(solution)/shard_map/all_to_all | solution.py:324
  222.0 1658.0 %copy-start.39 = (bf16[2048,8]{0,1:T(8,128)(2,1)}, bf16[2048,8]{0,1:T(8,128)(2,1)S(1)}, u32[]{:S(2)}) copy-start(bf16[2048,8]{0,1:T(8,128)(2,1)S(1)} %reshape.877) | copy-start | bytes 98308
  422.1 22.7 all-to-all-start.1
  448.4 1302.7 %copy-start.9 = (bf16[128,2048]{1,0:T(8,128)(2,1)}, bf16[128,2048]{1,0:T(8,128)(2,1)S(1)}, u32[]{:S(2)}) copy-start(bf16[128,2048]{1,0:T(8,128)(2,1)S(1)} %multiply_convert_fusion.7) | copy-start | bytes 1572868
  471.5 832.5 %copy-start.28 = (bf16[4,96,2048]{2,1,0:T(8,128)(2,1)}, bf16[4,96,2048]{2,1,0:T(8,128)(2,1)S(1)}, u32[]{:S(2)}) copy-start(bf16[4,96,2048]{2,1,0:T(8,128)(2,1)S(1)} %all_to_all.40) | copy-start | bytes 4718596
  1746.5 22.9 all-to-all-start.3
  1852.9 23.6 all-to-all-start.5
  1888.0 24.5 all-to-all-start.6
  1894.0 124.4 %reduce-scatter.25.cloned.1.call-start = ((), (), s32[]{:S(2)}) async-start(), calls=%async_computation.27 | async-start | bytes 5242880
  1973.6 40.7 %all-to-all-start.7 = ((bf16[4,96,2048]{2,1,0:T(8,128)(2,1)}), bf16[4,96,2048]{2,1,0:T(8,128)(2,1)S(1)}, u32[]{:S(2)}, u32[]{:S(2)}) async-start(bf16[4,96,2048]{2,1,0:T(8,128)(2,1)} %bitcast.263), calls=%async_computation.7 | async-start | bytes 3145728 | tf_op jit(solution)/shard_map/all_to_all | solution.py:483
  1979.0 181.5 %reduce-scatter.29.cloned.1.call-start = ((), (), s32[]{:S(2)}) async-start(), calls=%async_computation.29 | async-start | bytes 1081344
  1981.3 285.5 %reduce-scatter.27.cloned.1.call-start = ((), (), s32[]{:S(2)}) async-start(), calls=%async_computation.28 | async-start | bytes 1081344
  2039.3 398.3 %reduce-scatter.17.cloned.1.call-start = ((), (), s32[]{:S(2)}) async-start(), calls=%async_computation.23 | async-start | bytes 9437184 | tf_op jit(solution)/shard_map/reduce_scatter | solution.py:258
  2049.5 539.9 %reduce-scatter.19.cloned.1.call-start = ((), (), s32[]{:S(2)}) async-start(), calls=%async_computation.24 | async-start | bytes 9437184 | tf_op jit(solution)/shard_map/reduce_scatter | solution.py:261
  2059.2 907.4 %reduce-scatter.23.cloned.1.call-start = ((), (), s32[]{:S(2)}) async-start(), calls=%async_computation.26 | async-start | bytes 25952256 | tf_op jit(solution)/shard_map/reduce_scatter | solution.py:261
  2078.0 1620.0 %reduce-scatter.21.cloned.1.call-start = ((), (), s32[]{:S(2)}) async-start(), calls=%async_computation.25 | async-start | bytes 51904512 | tf_op jit(solution)/shard_map/reduce_scatter | solution.py:258
  2146.5 1911.0 %reduce-scatter.15.cloned.1.call-start = ((), (), s32[]{:S(2)}) async-start(), calls=%async_computation.22 | async-start | bytes 34603008 | tf_op jit(solution)/shard_map/reduce_scatter | solution.py:517
  (77 other events, 1578.2 us)
Sparse Core Ops, SparseCore 0:
  11.5 114.0 all-gather.8
  128.3 123.4 all-gather.12
  253.9 33.5 all-gather.10
  289.5 124.0 all-gather.14
  415.5 872.7 all-gather.16
  1289.7 441.0 all-gather.18
  1956.8 61.4 reduce-scatter.24
  2020.7 113.1 reduce-scatter.28
  2136.1 130.6 reduce-scatter.26
  2271.3 166.3 reduce-scatter.16
  2441.3 147.9 reduce-scatter.18
  2593.6 372.9 reduce-scatter.22
  2970.9 727.1 reduce-scatter.20
  3700.8 356.6 reduce-scatter.14
where the time goes:
time: 4070 us; the launch traced here: 4060 us
  waiting for transfers between devices  3420 us (84%)
  matrix products  298 us (7%)
  blocking collectives  120 us (3%)
  local copies, waits for them, and re-layouts  92.6 us (2%)
  other arithmetic  91 us (2%)
    reduce_scatter x2, waiting for transfers between devices, scatter_pair(): lax.psum_scatter(first.astype(jnp.bfloat16), 'grp', scatter_dimension=1,...  896 us
    all_gather x2, waiting for transfers between devices, gather_pair(): lax.all_gather(first.astype(jnp.bfloat16), 'grp', axis=1, tiled=True)  844 us
    reduce_scatter x2, waiting for transfers between devices, scatter_pair(): lax.psum_scatter(second.astype(jnp.bfloat16), 'grp', scatter_dimension=1,...  523 us
    all_gather x2, waiting for transfers between devices, gather_pair(): lax.all_gather(second.astype(jnp.bfloat16), 'grp', axis=1, tiled=True)  508 us
    reduce_scatter x1, waiting for transfers between devices, body(): lax.psum_scatter(kv_weight_grad, ('grp', 'exp'), scatter_dimension=0, til...  347 us
    unnamed x17, waiting for transfers between devices  104 us
  transfers between devices with their start and end apart: 20, of which 18 were waited for; matrix products, arithmetic and copies ran while one was open for 8% of the time, Pallas kernels for 0%

commit v1 on v0

v1 whole, which is shorter than its diff:
```python
import functools
import math

import jax
import jax.numpy as jnp
from jax import lax
from jax.experimental import pallas as pl
from jax.experimental.pallas import tpu as pltpu
from jax.sharding import PartitionSpec as P

HEADS = 16
LANES = 128
MESH = pl.DeviceIdType.MESH
MB = 1024 * 1024

epsilon = 1e-05
negative = -1e30
highest = lax.Precision.HIGHEST
f32 = jnp.float32
bf16 = jnp.bfloat16


def nn(a, b):
    return jnp.dot(a, b, preferred_element_type=f32)


def nt(a, b):
    return lax.dot_general(a, b, (((1,), (1,)), ((), ())), preferred_element_type=f32)


def tn(a, b):
    return lax.dot_general(a, b, (((0,), (0,)), ((), ())), preferred_element_type=f32)


def loop(count, step):
    def run(i, carry):
        step(i)
        return carry

    lax.fori_loop(0, count, run, 0)


def rows_at(i, size):
    return pl.ds(pl.multiple_of(i * size, size), size)


def turn(v, cos, sin):
    return v * cos + pltpu.roll(v, LANES // 2, 1) * sin


def gate_columns(logits, r0, r1, me):
    lane = lax.broadcasted_iota(jnp.int32, logits.shape, 1)
    l0 = jnp.sum(jnp.where(lane == r0, logits, 0.0), axis=1, keepdims=True)
    l1 = jnp.sum(jnp.where(lane == r1, logits, 0.0), axis=1, keepdims=True)
    top = jnp.maximum(l0, l1)
    e0, e1 = jnp.exp(l0 - top), jnp.exp(l1 - top)
    g0, g1 = e0 / (e0 + e1), e1 / (e0 + e1)
    weight = jnp.where(r0 == me, g0, 0.0) + jnp.where(r1 == me, g1, 0.0)
    sign = jnp.where(r0 == me, 1.0, 0.0) - jnp.where(r1 == me, 1.0, 0.0)
    return jnp.where(
        lane == 0,
        weight,
        jnp.where(lane == 1, sign, jnp.where(lane == 2, g0, jnp.where(lane == 3, g1, 0.0))),
    )


def attn_forward_kernel(
    cw, scale, me, tokens, gain, w_all, ow, cos, sin, meta, krow, qkv, att, aux, part, h1, inv
):
    count, width = h1.shape
    heads = cw // LANES
    step_rows = 256

    def normalise(i):
        at = rows_at(i, 64)
        v = tokens[at, :].astype(f32)
        inverse = lax.rsqrt(jnp.mean(v * v, axis=1, keepdims=True) + epsilon)
        inv[at, :] = jnp.broadcast_to(inverse, (64, LANES))
        h1[at, :] = (v * inverse * gain[...]).astype(bf16)

    loop(count // 64, normalise)

    def project(i):
        at = rows_at(i, step_rows)
        y = nn(h1[at, :], w_all[...])
        c, s = cos[at, :], sin[at, :]
        for h in range(2 * heads):
            qkv[at, h * LANES : (h + 1) * LANES] = turn(
                y[:, h * LANES : (h + 1) * LANES], c, s
            ).astype(bf16)
        qkv[at, 2 * cw : 3 * cw] = y[:, 2 * cw : 3 * cw].astype(bf16)
        found = gate_columns(y[:, 3 * cw : 3 * cw + LANES], meta[at, 2:3], meta[at, 3:4], me[0])
        lane = lax.broadcasted_iota(jnp.int32, found.shape, 1)
        aux[at, :] = jnp.where(lane == 4, inv[at, :], found)

    loop(count // step_rows, project)

    for h in range(heads):

        def attend(i, h=h):
            at = rows_at(i, LANES)
            q = qkv[at, h * LANES : (h + 1) * LANES]
            k = qkv[:, cw + h * LANES : cw + (h + 1) * LANES]
            v = qkv[:, 2 * cw + h * LANES : 2 * cw + (h + 1) * LANES]
            ak = krow[0, 0:1, :]
            allowed = (ak <= meta[at, 0:1]) & (ak >= meta[at, 1:2])
            scores = jnp.where(allowed, nt(q, k) * scale, negative)
            top = jnp.max(scores, axis=1, keepdims=True)
            raised = jnp.exp(scores - top)
            total = jnp.sum(raised, axis=1, keepdims=True)
            probs = (raised * (1.0 / total)).astype(bf16)
            att[at, h * LANES : (h + 1) * LANES] = nn(probs, v).astype(bf16)
            old = aux[at, :]
            lane = lax.broadcasted_iota(jnp.int32, old.shape, 1)
            aux[at, :] = jnp.where(lane == 8 + h, top + jnp.log(total), old)

        loop(count // LANES, attend)

    def output(i):
        at = rows_at(i, step_rows)
        scaled = (aux[at, 0:1] * att[at, :].astype(f32)).astype(bf16)
        part[at, :] = nn(scaled, ow[...]).astype(bf16)

    loop(count // step_rows, output)


def attn_backward_kernel(
    cw, scale, dmid, tokens, gain, qkv, att, aux, cos, sin, meta, krow, w_all, ow,
    dh1, dw, do, h1, datt, watt, dqkv, dk_sum, dv_sum,
):
    count, width = h1.shape
    heads = cw // LANES
    step_rows = 256

    @pl.when(pl.program_id(0) == 0)
    def _():
        dw[...] = jnp.zeros_like(dw)
        do[...] = jnp.zeros_like(do)

    def normalise(i):
        at = rows_at(i, 64)
        h1[at, :] = (tokens[at, :].astype(f32) * aux[at, 4:5] * gain[...]).astype(bf16)

    loop(count // 64, normalise)

    def incoming(i):
        at = rows_at(i, step_rows)
        raw = nt(dmid[at, :], ow[...])
        a = att[at, :].astype(f32)
        weight, sign = aux[at, 0:1], aux[at, 1:2]
        share = sign * jnp.sum(raw * a, axis=1, keepdims=True)
        dh1[at, width:] = jnp.broadcast_to(share, (step_rows, LANES)).astype(bf16)
        datt[at, :] = (weight * raw).astype(bf16)
        watt[at, :] = (weight * a).astype(bf16)

    loop(count // step_rows, incoming)

    def out_weight(i):
        at = rows_at(i, 512)
        do[:, at] += tn(watt[...], dmid[:, at])

    loop(width // 512, out_weight)

    for h in range(heads):
        hs = slice(h * LANES, (h + 1) * LANES)
        ks = slice(cw + h * LANES, cw + (h + 1) * LANES)
        vs = slice(2 * cw + h * LANES, 2 * cw + (h + 1) * LANES)
        dk_sum[...] = jnp.zeros_like(dk_sum)
        dv_sum[...] = jnp.zeros_like(dv_sum)

        def back(i, h=h, hs=hs, ks=ks, vs=vs):
            at = rows_at(i, LANES)
            q, k, v = qkv[at, hs], qkv[:, ks], qkv[:, vs]
            ak = krow[0, 0:1, :]
            allowed = (ak <= meta[at, 0:1]) & (ak >= meta[at, 1:2])
            scores = jnp.where(allowed, nt(q, k) * scale, negative)
            probs = jnp.exp(scores - aux[at, 8 + h : 9 + h])
            grad = datt[at, hs]
            dprobs = nt(grad, v)
            inner = jnp.sum(probs * dprobs, axis=1, keepdims=True)
            dscores = (probs * (dprobs - inner)).astype(bf16)
            dqkv[at, hs] = turn(nn(dscores, k) * scale, cos[at, :], -sin[at, :]).astype(bf16)
            dk_sum[...] += tn(dscores, q)
            dv_sum[...] += tn(probs.astype(bf16), grad)

        loop(count // LANES, back)
        dqkv[:, ks] = turn(dk_sum[...] * scale, cos[...], -sin[...]).astype(bf16)
        dqkv[:, vs] = dv_sum[...].astype(bf16)

    def to_hidden(i):
        at = rows_at(i, step_rows)
        dh1[at, :width] = nt(dqkv[at, :], w_all[:, : 3 * cw]).astype(bf16)

    loop(count // step_rows, to_hidden)

    def weights(i):
        at = rows_at(i, 512)
        dw[:, at] += tn(dqkv[...], h1[:, at])

    loop(width // 512, weights)


def whole_block(shape):
    return pl.BlockSpec(shape, lambda i: (0,) * len(shape))


def attn_forward(me, tokens, gain, w_all, ow, cos, sin, meta, krow, groups, scale):
    total = tokens.shape[0]
    cw, width = ow.shape
    count = total // groups
    row = lambda w: pl.BlockSpec((count, w), lambda i: (i, 0))
    shape = lambda w, t: jax.ShapeDtypeStruct((total, w), t)
    return pl.pallas_call(
        functools.partial(attn_forward_kernel, cw, scale),
        grid=(groups,),
        in_specs=[
            pl.BlockSpec(memory_space=pltpu.SMEM), row(width), whole_block(gain.shape),
            whole_block(w_all.shape), whole_block(ow.shape), row(LANES), row(LANES), row(8),
            pl.BlockSpec((1, 8, count), lambda i: (i, 0, 0)),
        ],
        out_specs=[row(3 * cw), row(cw), row(LANES), row(width)],
        out_shape=[shape(3 * cw, bf16), shape(cw, bf16), shape(LANES, f32), shape(width, bf16)],
        scratch_shapes=[pltpu.VMEM((count, width), bf16), pltpu.VMEM((count, LANES), f32)],
        compiler_params=pltpu.CompilerParams(vmem_limit_bytes=60 * MB),
    )(me, tokens, gain, w_all, ow, cos, sin, meta, krow)


def attn_backward(dmid, tokens, gain, qkv, att, aux, cos, sin, meta, krow, w_all, ow, groups, scale):
    total, width = dmid.shape
    cw = ow.shape[0]
    count = total // groups
    row = lambda w: pl.BlockSpec((count, w), lambda i: (i, 0))
    return pl.pallas_call(
        functools.partial(attn_backward_kernel, cw, scale),
        grid=(groups,),
        in_specs=[
            row(width), row(width), whole_block(gain.shape), row(3 * cw), row(cw), row(LANES), row(LANES), row(LANES), row(8),
            pl.BlockSpec((1, 8, count), lambda i: (i, 0, 0)),
            whole_block(w_all.shape), whole_block(ow.shape),
        ],
        out_specs=[row(width + LANES), whole_block((3 * cw, width)), whole_block((cw, width))],
        out_shape=[
            jax.ShapeDtypeStruct((total, width + LANES), bf16),
            jax.ShapeDtypeStruct((3 * cw, width), f32),
            jax.ShapeDtypeStruct((cw, width), f32),
        ],
        scratch_shapes=[
            pltpu.VMEM((count, width), bf16), pltpu.VMEM((count, cw), bf16), pltpu.VMEM((count, cw), bf16), pltpu.VMEM((count, 3 * cw), bf16),
            pltpu.VMEM((count, LANES), f32), pltpu.VMEM((count, LANES), f32),
        ],
        compiler_params=pltpu.CompilerParams(vmem_limit_bytes=60 * MB),
    )(dmid, tokens, gain, qkv, att, aux, cos, sin, meta, krow, w_all, ow)


def pieces(total, size):
    return [(at, min(size, total - at)) for at in range(0, total, size)]


def ffn_kernel(
    cap, me, h2, top, router, meta, posrow, gate_up, down,
    produced, dh2, aux, gate_up_grad, down_grad,
    wg, wu, wd, sg, su, sd, xc, gc, act, dgate, dup, yc, bc, gw, sems,
):
    rows, width = h2.shape
    hidden = wd.shape[0]
    blocks = rows // LANES
    step = pl.program_id(0)

    def masters(back):
        pairs = [(gate_up.at[:, 0, :], sg), (gate_up.at[:, 1, :], su), (down, sd)]
        if back:
            pairs = [(sg, gate_up_grad.at[:, 0, :]), (su, gate_up_grad.at[:, 1, :]), (sd, down_grad)]
        return [pltpu.make_async_copy(a, b, sems.at[i]) for i, (a, b) in enumerate(pairs)]

    @pl.when(step == 0)
    def _():
        copies = masters(False)
        for c in copies:
            c.start()
        for c, a, b in zip(copies, (sg, su, sd), (wg, wu, wd), strict=True):
            c.wait()

            def cast(i, a=a, b=b):
                at = rows_at(i, 32)
                b[at, :] = a[at, :].astype(bf16)
                a[at, :] = jnp.zeros((32, width), f32)

            loop(hidden // 32, cast)

    def gates(i):
        at = rows_at(i, LANES)
        found = gate_columns(nn(h2[at, :], router[...]), meta[at, 0:1], meta[at, 1:2], me[0])
        aux[at, :] = found
        gw[at, :] = (found[:, 0:1] * top[at, :].astype(f32)).astype(bf16)
        slot = lax.broadcasted_iota(jnp.int32, (cap, LANES), 0)
        choose = (slot == posrow[0, pl.ds(i, 1), :]).astype(bf16)
        to = rows_at(i, cap)
        xc[to, :] = nn(choose, h2[at, :]).astype(bf16)
        gc[to, :] = nn(choose, gw[at, :]).astype(bf16)

    loop(blocks, gates)

    for start, size in pieces(hidden, 256):
        fs = slice(start, start + size)
        gate, up, dact = nt(xc[...], wg[fs, :]), nt(xc[...], wu[fs, :]), nt(gc[...], wd[fs, :])
        sigmoid = 1.0 / (1.0 + jnp.exp(-gate))
        silu = gate * sigmoid
        act[:, fs] = (silu * up).astype(bf16)
        dgate[:, fs] = (dact * up * sigmoid * (1.0 + gate * (1.0 - sigmoid))).astype(bf16)
        dup[:, fs] = (dact * silu).astype(bf16)

        def grads(i, fs=fs):
            at = rows_at(i, 512)
            sd[fs, at] += tn(act[:, fs], gc[:, at])
            sg[fs, at] += tn(dgate[:, fs], xc[:, at])
            su[fs, at] += tn(dup[:, fs], xc[:, at])

        loop(width // 512, grads)

    def results(i):
        at = rows_at(i, 512)
        yc[:, at] = nn(act[...], wd[:, at]).astype(bf16)
        bc[:, at] = (nn(dgate[...], wg[:, at]) + nn(dup[...], wu[:, at])).astype(bf16)

    loop(width // 512, results)

    def scatter(i):
        at, of = rows_at(i, LANES), rows_at(i, cap)
        slot = lax.broadcasted_iota(jnp.int32, (cap, LANES), 0)
        choose = (slot == posrow[0, pl.ds(i, 1), :]).astype(bf16)
        found = aux[at, :]
        share = jnp.zeros((LANES, 1), f32)
        for start, size in pieces(width, 512):
            cs = slice(start, start + size)
            y = tn(choose, yc[of, cs])
            share = share + jnp.sum(y * top[at, cs].astype(f32), axis=1, keepdims=True)
            produced[at, cs] = (found[:, 0:1] * y).astype(bf16)
            dh2[at, cs] = tn(choose, bc[of, cs]).astype(bf16)
        dh2[at, width:] = jnp.broadcast_to(found[:, 1:2] * share, (LANES, LANES)).astype(bf16)

    loop(blocks, scatter)

    @pl.when(step == pl.num_programs(0) - 1)
    def _():
        copies = masters(True)
        for c in copies:
            c.start()
        for c in copies:
            c.wait()


def ffn(me, h2, top, router, meta, posrow, gate_up, down, cap):
    total, width = h2.shape
    hidden = down.shape[0]
    tile = posrow.shape[1] * LANES
    few = tile // LANES * cap
    row = lambda w: pl.BlockSpec((tile, w), lambda i: (i, 0))
    hbm = pl.BlockSpec(memory_space=pl.ANY)
    V = pltpu.VMEM
    return pl.pallas_call(
        functools.partial(ffn_kernel, cap),
        grid=(total // tile,),
        in_specs=[
            pl.BlockSpec(memory_space=pltpu.SMEM), row(width), row(width), whole_block(router.shape), row(8),
            pl.BlockSpec((1,) + posrow.shape[1:], lambda i: (i, 0, 0)), hbm, hbm,
        ],
        out_specs=[row(width), row(width + LANES), row(LANES), hbm, hbm],
        out_shape=[
            jax.ShapeDtypeStruct((total, width), bf16),
            jax.ShapeDtypeStruct((total, width + LANES), bf16),
            jax.ShapeDtypeStruct((total, LANES), f32),
            jax.ShapeDtypeStruct(gate_up.shape, f32),
            jax.ShapeDtypeStruct(down.shape, f32),
        ],
        scratch_shapes=[V((hidden, width), bf16)] * 3 + [V((hidden, width), f32)] * 3 + [V((few, width), bf16)] * 2
        + [V((few, hidden), bf16)] * 3 + [V((few, width), bf16)] * 2 + [V((tile, width), bf16), pltpu.SemaphoreType.DMA((3,))],
        compiler_params=pltpu.CompilerParams(vmem_limit_bytes=63 * MB),
    )(me, h2, top, router, meta, posrow, gate_up, down)


def ag_kernel(dims, halves, src, out, local_sem, zs, zr, xs, xr, ys, yr, cs, cr):
    nz, nx, ny = dims
    gi = lax.axis_index("grp"); ei = lax.axis_index("exp")
    z, x = gi // nx, gi % nx
    y, c = ei // 2, ei % 2
    ne = ny * 2
    rows = src.shape[0]
    part = rows // halves
    def dev(z_, x_, y_, c_):
        return (z_ * nx + x_, y_ * 2 + c_)
    def slot(z_, x_, y_, c_):
        return (z_ * nx + x_) * ne + y_ * 2 + c_
    barrier = pltpu.get_barrier_semaphore()
    def sig(d):
        pl.semaphore_signal(barrier, inc=1, device_id=d, device_id_type=MESH)
    sig(dev(z, 1 - x, y, c)); sig(dev(z, x, 1 - y, c)); sig(dev(z, x, y, 1 - c))
    @pl.when(z > 0)
    def _(): sig(dev(z - 1, x, y, c))
    @pl.when(z < nz - 1)
    def _(): sig(dev(z + 1, x, y, c))
    pl.semaphore_wait(barrier, 3 + (z > 0).astype(jnp.int32) + (z < nz - 1).astype(jnp.int32))
    own = pltpu.make_async_copy(src, out.at[slot(z, x, y, c)], local_sem)
    own.start()
    span = 2 * nz - 1
    def piece(sl, h):
        return out.at[sl, pl.ds(h * part, part)]
    def copy(sl, h, is_own, ssem, rsem, d):
        s = src.at[pl.ds(h * part, part)] if is_own else piece(sl, h)
        return pltpu.make_async_remote_copy(src_ref=s, dst_ref=piece(sl, h), send_sem=ssem, recv_sem=rsem, device_id=d, device_id_type=MESH)
    def zcopy(h, delta, direction, arriving):
        zz = z - delta * direction
        k = (h * 2 + (0 if direction > 0 else 1)) * nz
        if arriving:
            return copy(slot(zz, x, y, c), h, False, zs.at[k + delta], zr.at[k + delta], dev(z, x, y, c) if False else dev(z, x, y, 1 - c))
        return copy(slot(zz, x, y, c), h, delta == 0, zs.at[k + delta + 1], zr.at[k + delta + 1], dev(z + direction, x, y, c))
    def valid(delta):
        zz = z + delta
        return (zz >= 0) & (zz < nz)
    def when(cond, f):
        pl.when(cond)(f)
    sends = []
    def order(h):
        return ("x", "y") if h % 2 == 0 else ("y", "x")
    def first(h, delta):
        a = order(h)[0]
        sems = (xs, xr) if a == "x" else (ys, yr)
        k = h * 2 * span + delta + nz - 1
        d = dev(z, 1 - x, y, c) if a == "x" else dev(z, x, 1 - y, c)
        return copy(slot(z + delta, x, y, c), h, delta == 0, sems[0].at[k], sems[1].at[k], d), (
            lambda: copy(slot(z + delta, 1 - x if a == "x" else x, 1 - y if a == "y" else y, c), h, False, sems[0].at[k], sems[1].at[k], d))
    def second(h, delta, rel):
        a0, a = order(h)
        sems = (xs, xr) if a == "x" else (ys, yr)
        k = h * 2 * span + (rel * span) + delta + nz - 1
        d = dev(z, 1 - x, y, c) if a == "x" else dev(z, x, 1 - y, c)
        x0 = (1 - x if rel else x) if a0 == "x" else x
        y0 = (1 - y if rel else y) if a0 == "y" else y
        snd = copy(slot(z + delta, x0, y0, c), h, delta == 0 and rel == 0, sems[0].at[k], sems[1].at[k], d)
        x1 = 1 - x if a == "x" else x0
        y1 = 1 - y if a == "y" else y0
        rcv = copy(slot(z + delta, x1, y1, c), h, False, sems[0].at[k], sems[1].at[k], d)
        return snd, rcv
    def core(h, delta, rx, ry):
        k = h * 4 * span + (rx * 2 + ry) * span + delta + nz - 1
        d = dev(z, x, y, 1 - c)
        xx = 1 - x if rx else x
        yy = 1 - y if ry else y
        return (copy(slot(z + delta, xx, yy, c), h, delta == 0 and not rx and not ry, cs.at[k], cr.at[k], d),
                copy(slot(z + delta, xx, yy, 1 - c), h, False, cs.at[k], cr.at[k], d))
    hs = range(halves)
    def have_z(delta):
        for h in hs:
            if delta <= 0:
                when(z < nz - 1, lambda h=h: zcopy(h, -delta, 1, False).start())
            if delta >= 0:
                when(z > 0, lambda h=h: zcopy(h, delta, -1, False).start())
            first(h, delta)[0].start()
            second(h, delta, 0)[0].start()
            core(h, delta, 0, 0)[0].start()
    have_z(0)
    def get_z(delta):
        def f():
            for h in hs:
                zcopy(h, abs(delta), -1 if delta > 0 else 1, True).wait_recv()
            have_z(delta)
        when(valid(delta), f)
    def get_first(delta):
        def f():
            for h in hs:
                first(h, delta)[1]().wait_recv()
                second(h, delta, 1)[0].start()
                rx = 1 if order(h)[0] == "x" else 0
                core(h, delta, rx, 1 - rx)[0].start()
        when(valid(delta), f)
    def get_second(delta):
        def f():
            for h in hs:
                for rel in range(2):
                    second(h, delta, rel)[1].wait_recv()
                    a0, a = order(h)
                    rx = 1 if a == "x" else (rel if a0 == "x" else 0)
                    ry = 1 if a == "y" else (rel if a0 == "y" else 0)
                    core(h, delta, rx, ry)[0].start()
        when(valid(delta), f)
    for step in range(nz + 2):
        for dist, fn in ((step, get_z), (step - 1, get_first), (step - 2, get_second)):
            if 0 <= dist < nz:
                if dist == 0:
                    if fn is not get_z: fn(0)
                else:
                    fn(-dist); fn(dist)
    own.wait()
    for delta in range(-(nz - 1), nz):
        def f(delta=delta):
            for h in hs:
                for rx in range(2):
                    for ry in range(2):
                        a, b = core(h, delta, rx, ry)
                        b.wait_recv(); a.wait_send()
                first(h, delta)[0].wait_send()
                for rel in range(2):
                    second(h, delta, rel)[0].wait_send()
                if delta <= 0:
                    when(z < nz - 1, lambda h=h: zcopy(h, -delta, 1, False).wait_send())
                if delta >= 0:
                    when(z > 0, lambda h=h: zcopy(h, delta, -1, False).wait_send())
        when(valid(delta), f)

def gather_kernel(v, dims, cid, halves=2):
    nz, nx, ny = dims
    n = nz * nx * ny * 2
    span = 2 * nz - 1
    D = pltpu.SemaphoreType.DMA
    return pl.pallas_call(
        functools.partial(ag_kernel, dims, halves),
        out_shape=jax.ShapeDtypeStruct((n,) + v.shape, v.dtype),
        in_specs=[pl.BlockSpec(memory_space=pl.ANY)],
        out_specs=pl.BlockSpec(memory_space=pl.ANY),
        scratch_shapes=[D] + [D((halves * 2 * (nz + 1),))] * 2 + [D((halves * 2 * span,))] * 4 + [D((halves * 4 * span,))] * 2,
        compiler_params=pltpu.CompilerParams(collective_id=cid, has_side_effects=True),
    )(v)


def rs_kernel(dims, src, out, loc, crv, frv, srv, zrv, lsem, cs, cr, fs, fr, ss, sr, zs, zr):
    nz, nx, ny = dims
    gi = lax.axis_index("grp"); ei = lax.axis_index("exp")
    z, x = gi // nx, gi % nx
    y, c = ei // 2, ei % 2
    ne = ny * 2
    rows, width = out.shape
    part = rows // 2
    span = 2 * nz - 1
    def dev(z_, x_, y_, c_):
        return (z_ * nx + x_, y_ * 2 + c_)
    def slot(z_, x_, y_, c_):
        return (z_ * nx + x_) * ne + y_ * 2 + c_
    barrier = pltpu.get_barrier_semaphore()
    def sig(d):
        pl.semaphore_signal(barrier, inc=1, device_id=d, device_id_type=MESH)
    sig(dev(z, 1 - x, y, c)); sig(dev(z, x, 1 - y, c)); sig(dev(z, x, y, 1 - c))
    @pl.when(z > 0)
    def _(): sig(dev(z - 1, x, y, c))
    @pl.when(z < nz - 1)
    def _(): sig(dev(z + 1, x, y, c))
    pl.semaphore_wait(barrier, 3 + (z > 0).astype(jnp.int32) + (z < nz - 1).astype(jnp.int32))

    def flip(v, r):
        return 1 - v if r else v
    def remote(s, d, a, b, to):
        return pltpu.make_async_remote_copy(src_ref=s, dst_ref=d, send_sem=a, recv_sem=b, device_id=to, device_id_type=MESH)
    deltas = [d for k in range(nz - 1, 0, -1) for d in (k, -k)] + [0]
    def valid(d):
        return (z + d >= 0) & (z + d < nz)
    classes = [(1, 1), (1, 0), (0, 1), (0, 0)]
    def piece(ref, lead, h):
        return ref.at[lead, pl.ds(h * part, part)]
    def load(d, rx, ry):
        i = (z + d) * 4 + rx * 2 + ry
        return pltpu.make_async_copy(src.at[slot(z + d, flip(x, rx), flip(y, ry), c)], loc.at[i], lsem.at[i])
    def core(d, rx, ry, h):
        i = (z + d) * 4 + rx * 2 + ry
        return remote(src.at[slot(z + d, flip(x, rx), flip(y, ry), 1 - c), pl.ds(h * part, part)],
                      piece(crv, i, h), cs.at[i * 2 + h], cr.at[i * 2 + h], dev(z, x, y, 1 - c))
    def first(d, other, h):
        rx, ry = (other, 1) if h == 0 else (1, other)
        i = (z + d) * 4 + rx * 2 + ry
        k = ((z + d) * 2 + other) * 2 + h
        to = dev(z, x, 1 - y, c) if h == 0 else dev(z, 1 - x, y, c)
        return remote(piece(loc, i, h), frv.at[k], fs.at[k], fr.at[k], to)
    def second(d, h):
        rx, ry = (1, 0) if h == 0 else (0, 1)
        i = (z + d) * 4 + rx * 2 + ry
        k = (z + d) * 2 + h
        to = dev(z, 1 - x, y, c) if h == 0 else dev(z, x, 1 - y, c)
        return remote(piece(loc, i, h), srv.at[k], ss.at[k], sr.at[k], to)
    def zcopy(d, h, arriving_from):
        pass
    def zk(way, dist, h):
        return (way * nz + dist) * 2 + h
    def zsend(d, h):
        way = 0 if d > 0 else 1
        i = (z + d) * 4
        k = zk(way, abs(d) - 1, h)
        to = dev(z + (1 if d > 0 else -1), x, y, c)
        return remote(piece(loc, i, h), zrv.at[k], zs.at[k], zr.at[k], to)
    def zwait(way, dist, h):
        k = zk(way, dist, h)
        remote(piece(loc, 0, h), zrv.at[k], zs.at[k], zr.at[k], dev(z, x, y, 1 - c)).wait_recv()
        return zrv.at[k]
    def add(i, h, *others):
        def step(r, _):
            at = pl.ds(pl.multiple_of(r * 16, 16), 16)
            here = pl.ds(pl.multiple_of(h * part + r * 16, 16), 16)
            total = loc[i, here, :].astype(jnp.float32)
            for o in others:
                total = total + o[at, :].astype(jnp.float32)
            loc[i, here, :] = total.astype(loc.dtype)
            return 0
        lax.fori_loop(0, part // 16, step, 0)
    for cl in classes:
        for d in deltas:
            def go(cl=cl, d=d):
                load(d, *cl).start()
                for h in range(2):
                    core(d, *cl, h).start()
            pl.when(valid(d))(go)
    def got_core(d, rx, ry, h, *more):
        i = (z + d) * 4 + rx * 2 + ry
        core(d, rx, ry, h).wait_recv()
        add(i, h, crv.at[i, pl.ds(h * part, part)], *more)
    def each(f):
        for d in deltas:
            pl.when(valid(d))(functools.partial(f, d))
    def c11(d):
        load(d, 1, 1).wait()
        for h in range(2):
            got_core(d, 1, 1, h)
            first(d, 1, h).start()
    each(c11)
    def c_first(d):
        load(d, 0, 1).wait(); load(d, 1, 0).wait()
        got_core(d, 0, 1, 0); first(d, 0, 0).start()
        got_core(d, 1, 0, 1); first(d, 0, 1).start()
    each(c_first)
    def c_second(d):
        first(d, 1, 0).wait_recv()
        got_core(d, 1, 0, 0, frv.at[((z + d) * 2 + 1) * 2 + 0]); second(d, 0).start()
        first(d, 1, 1).wait_recv()
        got_core(d, 0, 1, 1, frv.at[((z + d) * 2 + 1) * 2 + 1]); second(d, 1).start()
    each(c_second)
    def c_last(d):
        load(d, 0, 0).wait()
        for h in range(2):
            first(d, 0, h).wait_recv()
            second(d, h).wait_recv()
            more = [frv.at[((z + d) * 2) * 2 + h], srv.at[(z + d) * 2 + h]]
            got_core(d, 0, 0, h, *more)
            if d != 0:
                way = 0 if d > 0 else 1
                def chained(h=h):
                    add((z + d) * 4, h, zwait(way, abs(d), h))
                pl.when(z > 0 if d > 0 else z < nz - 1)(chained)
                zsend(d, h).start()
    each(c_last)
    for h in range(2):
        def left(h=h): add(z * 4, h, zwait(0, 0, h))
        def right(h=h): add(z * 4, h, zwait(1, 0, h))
        pl.when(z > 0)(left)
        pl.when(z < nz - 1)(right)
    def finish(r, _):
        at = pl.ds(pl.multiple_of(r * 16, 16), 16)
        out[at, :] = loc[z * 4, at, :].astype(out.dtype)
        return 0
    lax.fori_loop(0, rows // 16, finish, 0)
    def drain(d):
        for cl in classes:
            for h in range(2):
                core(d, *cl, h).wait_send()
        for h in range(2):
            first(d, 0, h).wait_send(); first(d, 1, h).wait_send(); second(d, h).wait_send()
            if d != 0:
                zsend(d, h).wait_send()
    each(drain)

def scatter_kernel(p, dims, cid):
    nz, nx, ny = dims
    n, rows, width = p.shape
    D = pltpu.SemaphoreType.DMA
    V = lambda *s: pltpu.VMEM(s, p.dtype)
    return pl.pallas_call(
        functools.partial(rs_kernel, dims),
        out_shape=jax.ShapeDtypeStruct((rows, width), jnp.float32),
        in_specs=[pl.BlockSpec(memory_space=pl.ANY)],
        out_specs=pl.BlockSpec(memory_space=pltpu.VMEM),
        scratch_shapes=[V(nz * 4, rows, width), V(nz * 4, rows, width), V(nz * 4, rows // 2, width), V(nz * 2, rows // 2, width), V(nz * 4, rows // 2, width),
            D((nz * 4,)), D((nz * 8,)), D((nz * 8,)), D((nz * 4,)), D((nz * 4,)), D((nz * 2,)), D((nz * 2,)), D((nz * 4,)), D((nz * 4,))],
        compiler_params=pltpu.CompilerParams(collective_id=cid, has_side_effects=True, vmem_limit_bytes=56 * 1024 * 1024),
    )(p)


def layout(first, order, group_rows, block):
    places = jnp.arange(group_rows, dtype=jnp.int32)
    anchor = jnp.repeat(order, block, axis=1) * block + places % block
    doc = (anchor >= first).astype(jnp.int32)
    return (anchor, anchor - doc * first)


def rotary_tables(place):
    half = LANES // 2
    freq = jnp.exp(jnp.arange(half, dtype=f32) * (-2.0 * math.log(10000.0) / LANES))
    angle = place.astype(f32)[:, None] * freq[None, :]
    cos, sin = jnp.cos(angle), jnp.sin(angle)
    return (jnp.concatenate([cos, cos], axis=1), jnp.concatenate([-sin, sin], axis=1))


def logit_grad(route, gates, difference, experts):
    moved = gates[:, 0:1] * gates[:, 1:2] * difference
    names = jnp.arange(experts, dtype=jnp.int32)[None, :]
    return jnp.where(route[:, 0:1] == names, moved, 0.0) - jnp.where(
        route[:, 1:2] == names, moved, 0.0
    )


def norm_back(grad_hidden, normed, inverse, gain):
    grad_normed = grad_hidden * gain
    gain_grad = jnp.sum(grad_hidden * normed, axis=0)
    mean_term = jnp.mean(grad_normed * normed, axis=1, keepdims=True)
    return (inverse * (grad_normed - normed * mean_term), gain_grad)


def body(
    dims,
    layer_input,
    out_grad,
    doc_lengths,
    block_order,
    attn_route,
    ffn_route,
    norm_gains,
    kv_master,
    router_master,
    query_master,
    output_master,
    gate_up_master,
    down_master,
):
    own_rows, width = layer_input.shape
    members, groups = lax.axis_size("exp"), lax.axis_size("grp")
    member, group = lax.axis_index("exp"), lax.axis_index("grp")
    experts = members
    capacity = 3 * own_rows // experts
    group_rows = own_rows * members
    total = group_rows * groups
    devices = groups * members
    cw = width // groups
    depth = kv_master.shape[0]
    scale = 1.0 / math.sqrt(LANES)
    me = member.reshape(1).astype(jnp.int32)
    both = ("grp", "exp")

    def gather_all(v, cid):
        if dims is None:
            return lax.all_gather(v, both, axis=0, tiled=False)
        return gather_kernel(v, dims, cid)

    def scatter_all(v, cid):
        v = v.reshape(devices, own_rows, v.shape[-1])
        if dims is None:
            return lax.psum_scatter(v, both, scatter_dimension=0, tiled=False).astype(f32)
        return scatter_kernel(v, dims, cid)

    blocks = block_order.shape[1]
    start_row = member * own_rows
    own_attn_route = lax.dynamic_slice_in_dim(attn_route, start_row, own_rows)
    own_ffn_route = lax.dynamic_slice_in_dim(ffn_route, start_row, own_rows)
    tall = lambda v: jnp.pad(v.astype(bf16), ((0, own_rows - v.shape[0]), (0, 0)))
    first_doc = doc_lengths[:, 0]
    small = jnp.concatenate(
        [
            tall(norm_gains),
            tall(router_master),
            own_attn_route.astype(bf16),
            own_ffn_route.astype(bf16),
            tall(jnp.concatenate([first_doc // 16, first_doc % 16, block_order[0]])[:, None]),
        ],
        axis=1,
    )
    at_route = 2 + 2 * experts
    sent = jnp.concatenate([layer_input, jnp.pad(small, ((0, 0), (0, LANES - small.shape[1])))], axis=1)
    tokens = gather_all(sent, 1).reshape(total, width + LANES)
    tops = gather_all(out_grad, 2).reshape(total, width)

    query_low = query_master[0].astype(bf16)
    kv_low = kv_master.astype(bf16).reshape(depth * 2, groups, cw)
    pieces_out = jnp.concatenate(
        [query_low.reshape(query_low.shape[0], groups, cw), kv_low], axis=0
    ).transpose(1, 0, 2)
    pieces_in = lax.all_to_all(pieces_out, "grp", split_axis=0, concat_axis=0, tiled=True)
    query_weight = pieces_in[:, : query_low.shape[0]].reshape(width, cw)
    kv_all = lax.all_gather(pieces_in[:, query_low.shape[0] :], "exp", axis=1, tiled=False)
    kv_weight = kv_all.reshape(width, 2 * cw)
    output_weight = output_master[0].astype(bf16)

    extra = tokens[:, width:]
    tables = extra.reshape(devices, own_rows, LANES)[:, :depth, :at_route].reshape(width, at_route)
    gains = tables[:, :2].astype(f32)
    router = tables[:, 2:]
    router_float = router.astype(f32)
    wide = lambda v: jnp.pad(v, ((0, 0), (0, LANES - v.shape[1])))
    routes = extra[:, at_route : at_route + 4].astype(jnp.int32)
    column = extra.reshape(groups, group_rows, LANES)[:, : blocks + 2, at_route + 4].astype(jnp.int32)
    anchor, place = layout(
        column[:, 0:1] * 16 + column[:, 1:2], column[:, 2:], group_rows, own_rows // 2
    )
    cos, sin = rotary_tables(place.reshape(total))
    zero = jnp.zeros((total, 4), jnp.int32)
    attn_meta = jnp.concatenate(
        [anchor.reshape(total, 1), (anchor - place).reshape(total, 1), routes[:, :2], zero], axis=1
    )
    key_rows = jnp.broadcast_to(anchor[:, None, :], (groups, 8, group_rows))
    gain_one, gain_two = gains[:, 0], gains[:, 1]
    w_all = jnp.concatenate([query_weight, kv_weight, wide(router[:, :experts])], axis=1)

    qkv, att, aux, attn_part = attn_forward(
        me, tokens, gain_one[None], w_all, output_weight, cos, sin, attn_meta, key_rows, groups, scale
    )
    own = (group * members + member) * own_rows
    attn_gates = lax.dynamic_slice(aux, (own, 2), (own_rows, 2))
    inputs = layer_input.astype(f32)
    middle = inputs + scatter_all(attn_part, 3)
    inverse_two = lax.rsqrt(jnp.mean(middle * middle, axis=1, keepdims=True) + epsilon)
    normed_two = middle * inverse_two
    hidden_two = (normed_two * gain_two).astype(bf16)
    h2 = gather_all(hidden_two, 4).reshape(total, width)

    ffn_meta = jnp.concatenate([routes[:, 2:], zero, zero[:, :2]], axis=1)
    named = (routes[:, 2] == member) | (routes[:, 3] == member)
    named = named.reshape(devices, own_rows)
    position = jnp.cumsum(named.astype(jnp.int32), axis=1) - 1
    position = jnp.where(named, position, -1)
    tile_blocks = 4
    produced, dh2, ffn_aux, gate_up_grad, down_grad = ffn(
        me, h2, tops, wide(router[:, experts:]), ffn_meta,
        position.reshape(devices // tile_blocks, tile_blocks, own_rows),
        gate_up_master[0], down_master[0], capacity,
    )
    ffn_gates = lax.dynamic_slice(ffn_aux, (own, 2), (own_rows, 2))
    back = scatter_all(dh2, 5)
    top_grad = out_grad.astype(f32)
    ffn_logit_grad = logit_grad(own_ffn_route, ffn_gates, back[:, width : width + 1], experts)
    hidden_two_grad = back[:, :width] + jnp.einsum(
        "te,de->td", ffn_logit_grad, router_float[:, experts:], precision=highest
    )
    middle_part, gain_two_grad = norm_back(hidden_two_grad, normed_two, inverse_two, gain_two)
    middle_grad = top_grad + middle_part
    dmid = gather_all(middle_grad.astype(bf16), 6).reshape(total, width)

    if dims is None:
        again, dmid = lax.optimization_barrier((layer_input, dmid))
        tokens = gather_all(again, 9).reshape(total, width)
    dh1, dw, do = attn_backward(
        dmid, tokens, gain_one[None], qkv, att, aux, cos, sin, attn_meta, key_rows, w_all, output_weight, groups, scale
    )
    final = middle + scatter_all(produced, 7)
    back = scatter_all(dh1, 8)
    inverse_one = lax.rsqrt(jnp.mean(inputs * inputs, axis=1, keepdims=True) + epsilon)
    normed_one = inputs * inverse_one
    hidden_one = (normed_one * gain_one).astype(bf16)
    attn_logit_grad = logit_grad(own_attn_route, attn_gates, back[:, width : width + 1], experts)
    hidden_one_grad = back[:, :width] + jnp.einsum(
        "te,de->td", attn_logit_grad, router_float[:, :experts], precision=highest
    )
    input_part, gain_one_grad = norm_back(hidden_one_grad, normed_one, inverse_one, gain_one)
    input_grad = middle_grad + input_part
    route_grad = [
        jnp.einsum("td,te->de", a.astype(f32), b, precision=highest)
        for a, b in ((hidden_one, attn_logit_grad), (hidden_two, ffn_logit_grad))
    ]
    sums = jnp.concatenate(
        [gain_one_grad[:, None], gain_two_grad[:, None], route_grad[0], route_grad[1]], axis=1
    )
    sums = lax.psum_scatter(sums, both, scatter_dimension=0, tiled=True)

    kv_part = dw[cw:].reshape(2 * cw, groups, members, depth)
    kv_part = lax.psum_scatter(kv_part.astype(bf16), "exp", scatter_dimension=2, tiled=False)
    query_part = dw[:cw].astype(bf16).reshape(cw, groups, width // groups)
    pieces_out = jnp.concatenate(
        [query_part.transpose(1, 0, 2).reshape(groups, -1), kv_part.transpose(1, 0, 2).reshape(groups, -1)],
        axis=1,
    )
    pieces_in = lax.all_to_all(pieces_out, "grp", split_axis=0, concat_axis=0, tiled=True)
    cut = cw * (width // groups)
    query_grad = pieces_in[:, :cut].reshape(width, width // groups).T.astype(f32)
    kv_grad = (
        pieces_in[:, cut:].reshape(groups, 2, cw, depth).transpose(3, 1, 0, 2).reshape(depth, 2 * width)
    ).astype(f32)
    return (
        final.astype(bf16),
        input_grad,
        sums[:, :2],
        kv_grad,
        sums[:, 2:],
        query_grad[None],
        do[None],
        gate_up_grad[None],
        down_grad[None],
    )


def solution(mesh):
    groups, members = mesh.shape["grp"], mesh.shape["exp"]
    dims = (groups // 2, 2, members // 2) if groups <= 8 and members == 4 else None
    in_specs = (
        P(("grp", "exp"), None),
        P(("grp", "exp"), None),
        P("grp", None),
        P("grp", None),
        P("grp", None),
        P("grp", None),
        P(("grp", "exp"), None),
        P(("grp", "exp"), None),
        P(("grp", "exp"), None),
        P("exp", "grp", None),
        P("exp", "grp", None),
        P("exp", "grp", None, None),
        P("exp", "grp", None),
    )
    out_specs = (
        P(("grp", "exp"), None),
        P(("grp", "exp"), None),
        P(("grp", "exp"), None),
        P(("grp", "exp"), None),
        P(("grp", "exp"), None),
        P("exp", "grp", None),
        P("exp", "grp", None),
        P("exp", "grp", None, None),
        P("exp", "grp", None),
    )
    return jax.shard_map(
        functools.partial(body, dims),
        mesh=mesh,
        in_specs=in_specs,
        out_specs=out_specs,
        check_vma=False,
    )
```

time: 4070 us -> 1380 us (0.34)
  the two profiles are of different devices: /device:TPU:22 before, /device:TPU:0 now
where the time goes in v1:
time: 1380 us; the launch traced here: 1370 us
  Pallas kernels  1140 us (83%)
  waiting for transfers between devices  88.8 us (6%)
  local copies, waits for them, and re-layouts  68.1 us (5%)
  other arithmetic  44.3 us (3%)
  between operations  15 us (1%)
    pallas_call x4, Pallas kernels, scatter_kernel(): pl.pallas_call(functools.partial(rs_kernel, dims), out_shape=jax.ShapeDty...  413 us
    pallas_call x4, Pallas kernels, gather_kernel(): pl.pallas_call(functools.partial(ag_kernel, dims, halves), out_shape=jax....  339 us
    pallas_call x1, Pallas kernels, ffn(): pl.pallas_call(functools.partial(ffn_kernel, cap), grid=(total // tile,),...  192 us
    pallas_call x1, Pallas kernels, attn_backward(): pl.pallas_call(functools.partial(attn_backward_kernel, cw, scale), grid=(...  114 us
    unnamed x5, waiting for transfers between devices  82.4 us
    pallas_call x1, Pallas kernels, attn_forward(): pl.pallas_call(functools.partial(attn_forward_kernel, cw, scale), grid=(g...  80.9 us
    unnamed x63, local copies, waits for them, and re-layouts  29 us
  transfers between devices with their start and end apart: 5, of which 3 were waited for; matrix products, arithmetic and copies ran while one was open for 4% of the time, Pallas kernels for 29%

profile of v1, /device:TPU:0, one launch (start us, length us, event | category | flops | bytes accessed | tf_op | source)
XLA Modules:
  0.0 1374.5 jit_solution(14892066647049965983)
XLA Ops:
  11.8 7.4 all-to-all-start
  21.5 106.4 %shard_map.196 = bf16[32,128,2176]{2,1,0:T(8,128)(2,1)} custom-call(bf16[128,2176]{1,0:T(8,128)(2,1)} %fusion.17.src), custom_call_target="tpu_custom_call" | custom-call | tf_op jit(solution)/shard_map/pallas_call | solution.py:514
  149.1 84.0 %shard_map.200 = bf16[32,128,2048]{2,1,0:T(8,128)(2,1)} custom-call(bf16[128,2048]{1,0:T(8,128)(2,1)} %src.1), custom_call_target="tpu_custom_call" | custom-call | tf_op jit(solution)/shard_map/pallas_call | solution.py:514
  237.5 7.5 fusion.16
  252.2 6.4 all-gather.3.cloned.1.call-done
  261.3 3.1 fusion.1.w_all
  265.0 80.9 %shard_map.197 = (bf16[4096,768]{1,0:T(8,128)(2,1)}, bf16[4096,256]{1,0:T(8,128)(2,1)}, f32[4096,128]{1,0:T(8,128)}, bf16[4096,2048]{1,0:T(8,128)(2,1)}) custom-call(s32[1]{0:T(128)} %bitcast.me, bf16[4096,2176]{1,0:T(8,128)(2,1)} %bitcast.99, f32[1,2048]{1,0:T(1,128)} %bitcast.128, bf16[2048,896]{1,0:T(8,128)(2,1)} %fusion.1.w_all, ...), custom_call_target="tpu_custom_call" | custom-call | tf_op jit(solution)/shard_map/pallas_call | solution.py:213
  345.9 96.6 %shard_map.198 = f32[128,2048]{1,0:T(8,128)} custom-call(bf16[32,128,2048]{2,1,0:T(8,128)(2,1)} %bitcast.111), custom_call_target="tpu_custom_call" | custom-call | tf_op jit(solution)/shard_map/pallas_call | solution.py:670
  445.9 74.6 %shard_map.199 = bf16[32,128,2048]{2,1,0:T(8,128)(2,1)} custom-call(bf16[128,2048]{1,0:T(8,128)(2,1)} %multiply_convert_fusion.src), custom_call_target="tpu_custom_call" | custom-call | tf_op jit(solution)/shard_map/pallas_call | solution.py:514
  520.5 191.7 %shard_map.201 = (bf16[4096,2048]{1,0:T(8,128)(2,1)}, bf16[4096,2176]{1,0:T(8,128)(2,1)}, f32[4096,128]{1,0:T(8,128)}, f32[704,2,2048]{2,1,0:T(2,128)}, f32[704,2048]{1,0:T(8,128)}) custom-call(s32[1]{0:T(128)} %bitcast.me, bf16[4096,2048]{1,0:T(8,128)(2,1)} %bitcast.102, bf16[4096,2048]{1,0:T(8,128)(2,1)} %bitcast.101, bf16[2048,128]{1,0:T(8,128)(2,1)} %pad.28.router, ...), custom_call_target="tpu_custom_call" | custom-call | tf_op jit(solution)/shard_map/pallas_call | solution.py:360
  712.2 101.8 %shard_map.203 = f32[128,2176]{1,0:T(8,128)} custom-call(bf16[32,128,2176]{2,1,0:T(8,128)(2,1)} %bitcast.109), custom_call_target="tpu_custom_call" | custom-call | tf_op jit(solution)/shard_map/pallas_call | solution.py:670
  818.5 74.2 %shard_map.204 = bf16[32,128,2048]{2,1,0:T(8,128)(2,1)} custom-call(bf16[128,2048]{1,0:T(8,128)(2,1)} %fusion.55.src), custom_call_target="tpu_custom_call" | custom-call | tf_op jit(solution)/shard_map/pallas_call | solution.py:514
  892.7 114.3 %shard_map.205 = (bf16[4096,2176]{1,0:T(8,128)(2,1)}, f32[768,2048]{1,0:T(8,128)}, f32[256,2048]{1,0:T(8,128)}) custom-call(bf16[4096,2048]{1,0:T(8,128)(2,1)} %bitcast.103, bf16[4096,2176]{1,0:T(8,128)(2,1)} %bitcast.100, f32[1,2048]{1,0:T(1,128)} %bitcast.129, bf16[4096,768]{1,0:T(8,128)(2,1)} %get-tuple-element.25.qkv, ...), custom_call_target="tpu_custom_call" | custom-call | tf_op jit(solution)/shard_map/pallas_call | solution.py:233
  1007.0 3.3 convert.26
  1013.4 3.9 copy.93
  1019.8 49.8 %all-reduce.9.cloned.1.call-done = bf16[512,8,4,64]{0,3,2,1:T(8,128)(2,1)} async-done(((bf16[512,8,4,64]{0,3,2,1:T(8,128)(2,1)}), bf16[512,8,4,64]{0,3,2,1:T(8,128)(2,1)}) %all-reduce.9.cloned.1.call-update) | async-done | bytes 2097168
  1080.3 3.9 reduce.13
  1084.2 3.9 reshape.335
  1088.1 5.5 all-to-all-start.1
  1093.7 113.0 %shard_map.206 = f32[128,2176]{1,0:T(8,128)} custom-call(bf16[32,128,2176]{2,1,0:T(8,128)(2,1)} %bitcast.108), custom_call_target="tpu_custom_call" | custom-call | tf_op jit(solution)/shard_map/pallas_call | solution.py:670
  1208.8 3.1 fusion.13
  1213.3 101.4 %shard_map.202 = f32[128,2048]{1,0:T(8,128)} custom-call(bf16[32,128,2048]{2,1,0:T(8,128)(2,1)} %bitcast.110), custom_call_target="tpu_custom_call" | custom-call | tf_op jit(solution)/shard_map/pallas_call | solution.py:670
  1317.6 32.6 %reduce-scatter.7.cloned.1.call-done = f32[64,10]{1,0:T(8,128)} async-done(((f32[2048,10]{1,0:T(8,128)}), f32[64,10]{1,0:T(8,128)}) %reduce-scatter.7.cloned.1.call-update) | async-done | bytes 2576
  1353.0 4.7 reshape.336
  (154 shorter events, 85.7 us)
Async XLA Ops:
  11.8 7.5 copy-start.18
  11.8 7.7 copy-start.20
  11.8 7.7 copy-start.17
  11.8 7.7 copy-start.19
  11.8 8.8 copy-start.5
  11.8 222.9 %all-to-all-start = ((bf16[8,384,256]{2,1,0:T(8,128)(2,1)}), bf16[8,384,256]{2,1,0:T(8,128)(2,1)}, u32[]{:S(2)}, u32[]{:S(2)}) async-start(bf16[8,384,256]{2,1,0:T(8,128)(2,1)} %maximum_bitcast_fusion), calls=%async_computation | async-start | bytes 3145728 | tf_op jit(solution)/shard_map/all_to_all | solution.py:778
  19.2 239.4 %all-gather.3.cloned.1.call-start = ((), (), s32[]{:S(2)}) async-start(), calls=%async_computation.3 | async-start | bytes 2621440 | tf_op jit(solution)/shard_map/all_gather | solution.py:780
  129.2 5.3 copy-start.12
  236.6 833.1 %all-reduce.9.cloned.1.call-start = ((), (), s32[]{:S(2)}) async-start(), calls=%async_computation.5 | async-start | bytes 4194304
  246.9 1.9 copy-start.14
  345.8 96.6 %copy-start.6 = (bf16[128,2048]{1,0:T(8,128)(2,1)S(1)}, bf16[128,2048]{1,0:T(8,128)(2,1)}, u32[]{:S(2)}) copy-start(bf16[128,2048]{1,0:T(8,128)(2,1)} %param.13) | copy-start | bytes 1572868
  712.2 102.9 %copy-start.1 = (f32[128,2048]{1,0:T(8,128)S(1)}, f32[128,2048]{1,0:T(8,128)}, u32[]{:S(2)}) copy-start(f32[128,2048]{1,0:T(8,128)} %copy-done) | copy-start | bytes 3145732
  814.0 3.4 copy-start.8
  817.4 75.4 %copy-start.3 = (f32[128,2048]{1,0:T(8,128)}, f32[128,2048]{1,0:T(8,128)S(1)}, u32[]{:S(2)}) copy-start(f32[128,2048]{1,0:T(8,128)S(1)} %get-tuple-element.104) | copy-start | bytes 3145732
  1010.3 1.6 copy-start.2
  1069.7 7.8 copy-start.11
  1088.1 265.0 %all-to-all-start.1 = ((bf16[8,2,49152]{2,1,0:T(2,128)(2,1)}), bf16[8,2,49152]{2,1,0:T(2,128)(2,1)}, u32[]{:S(2)}, u32[]{:S(2)}) async-start(bf16[8,2,49152]{2,1,0:T(2,128)(2,1)} %reshape.335), calls=%async_computation.1 | async-start | bytes 3145728 | tf_op jit(solution)/shard_map/all_to_all | solution.py:871
  1093.6 256.6 %reduce-scatter.7.cloned.1.call-start = ((), (), s32[]{:S(2)}) async-start(), calls=%async_computation.4 | async-start | bytes 1081344
  1093.6 114.2 %copy-start.13 = (bf16[128,2048]{1,0:T(8,128)(2,1)S(1)}, bf16[128,2048]{1,0:T(8,128)(2,1)}, u32[]{:S(2)}) copy-start(bf16[128,2048]{1,0:T(8,128)(2,1)} %multiply_convert_fusion.src) | copy-start | bytes 1572868
  1093.7 114.6 %copy-start.7 = (bf16[128,2048]{1,0:T(8,128)(2,1)S(1)}, bf16[128,2048]{1,0:T(8,128)(2,1)}, u32[]{:S(2)}) copy-start(bf16[128,2048]{1,0:T(8,128)(2,1)} %param.13) | copy-start | bytes 1572868
  1093.7 114.6 %copy-start.16 = (f32[2048]{0:T(1024)S(1)}, f32[2048]{0:T(1024)}, u32[]{:S(2)}) copy-start(f32[2048]{0:T(1024)} %get-tuple-element.74) | copy-start | bytes 24580
  1213.3 101.4 %copy-start.4 = (f32[128,2048]{1,0:T(8,128)S(1)}, f32[128,2048]{1,0:T(8,128)}, u32[]{:S(2)}) copy-start(f32[128,2048]{1,0:T(8,128)} %copy-done.3) | copy-start | bytes 3145732
  1213.3 101.4 %copy-start.9 = (bf16[128,2048]{1,0:T(8,128)(2,1)S(1)}, bf16[128,2048]{1,0:T(8,128)(2,1)}, u32[]{:S(2)}) copy-start(bf16[128,2048]{1,0:T(8,128)(2,1)} %src.1) | copy-start | bytes 1572868
  1213.3 101.4 %copy-start.10 = (f32[128,2048]{1,0:T(8,128)S(1)}, f32[128,2048]{1,0:T(8,128)}, u32[]{:S(2)}) copy-start(f32[128,2048]{1,0:T(8,128)} %get-tuple-element.105) | copy-start | bytes 3145732
  (4 other events, 4.1 us)
Sparse Core Ops, SparseCore 0:
  236.7 21.8 all-gather.2
  1017.5 52.1 all-reduce.8
  1213.4 136.6 reduce-scatter.6

commit v2 on v1

--- a/solution.py
+++ b/solution.py
@@ -42,6 +42,13 @@
 
 def rows_at(i, size):
     return pl.ds(pl.multiple_of(i * size, size), size)
+
+
+def kept(v):
+    def copy(src, dst):
+        dst[...] = src[...]
+
+    return pl.pallas_call(copy, out_shape=jax.ShapeDtypeStruct(v.shape, v.dtype))(v)
 
 
 def turn(v, cos, sin):
@@ -126,7 +133,7 @@
 
 def attn_backward_kernel(
     cw, scale, dmid, tokens, gain, qkv, att, aux, cos, sin, meta, krow, w_all, ow,
-    dh1, dw, do, h1, datt, watt, dqkv, dk_sum, dv_sum,
+    dh1, side, dw, do, h1, datt, watt, dqkv, dk_sum, dv_sum,
 ):
     count, width = h1.shape
     heads = cw // LANES
@@ -149,7 +156,7 @@
         a = att[at, :].astype(f32)
         weight, sign = aux[at, 0:1], aux[at, 1:2]
         share = sign * jnp.sum(raw * a, axis=1, keepdims=True)
-        dh1[at, width:] = jnp.broadcast_to(share, (step_rows, LANES)).astype(bf16)
+        side[at, :] = jnp.broadcast_to(share, (step_rows, LANES)).astype(bf16)
         datt[at, :] = (weight * raw).astype(bf16)
         watt[at, :] = (weight * a).astype(bf16)
 
@@ -204,51 +211,117 @@
     return pl.BlockSpec(shape, lambda i: (0,) * len(shape))
 
 
-def attn_forward(me, tokens, gain, w_all, ow, cos, sin, meta, krow, groups, scale):
+def once(shape):
+    return pl.BlockSpec(shape, lambda i: (0,) * len(shape), pipeline_mode=pl.Buffered(1))
+
+
+def attn_forward_fused(dims, cw, scale, me, tokens, gain, w_all, ow, cos, sin, meta, krow, qkv, att, aux, out, h1, inv, *refs):
+    i = pl.program_id(0)
+    place = Place(dims)
+    sums = Scatter(dims, place, out, refs)
+    pl.when(i == 0)(place.greet)
+
+    @pl.when(i < sums.tiles)
+    def _():
+        attn_forward_kernel(cw, scale, me, tokens, gain, w_all, ow, cos, sin, meta, krow, qkv, att, aux, sums.tile.at[i % 2], h1, inv)
+
+    pl.when(i == 0)(place.greeted)
+    sums.run(i)
+
+
+def attn_forward(dims, cid, me, tokens, gain, w_all, ow, cos, sin, meta, krow, groups, scale):
     total = tokens.shape[0]
     cw, width = ow.shape
     count = total // groups
-    row = lambda w: pl.BlockSpec((count, w), lambda i: (i, 0))
+    at = (lambda i: tile_group(i, dims)) if dims else (lambda i: i)
+    row = lambda w: pl.BlockSpec((count, w), lambda i: (at(i), 0))
     shape = lambda w, t: jax.ShapeDtypeStruct((total, w), t)
+    if dims:
+        own = count // 4
+        kernel = functools.partial(attn_forward_fused, dims, cw, scale)
+        last_spec, last_shape = whole_block((own, width)), jax.ShapeDtypeStruct((own, width), f32)
+        params, more = dict(collective_id=cid, has_side_effects=True), scatter_scratch(dims, own, width)
+    else:
+        kernel = functools.partial(attn_forward_kernel, cw, scale)
+        last_spec, last_shape, params, more = row(width), shape(width, bf16), {}, []
     return pl.pallas_call(
-        functools.partial(attn_forward_kernel, cw, scale),
-        grid=(groups,),
+        kernel,
+        grid=(groups + 2 + dims[0] if dims else groups,),
         in_specs=[
             pl.BlockSpec(memory_space=pltpu.SMEM), row(width), whole_block(gain.shape),
-            whole_block(w_all.shape), whole_block(ow.shape), row(LANES), row(LANES), row(8),
-            pl.BlockSpec((1, 8, count), lambda i: (i, 0, 0)),
+            once(w_all.shape), once(ow.shape), row(LANES), row(LANES), row(8),
+            pl.BlockSpec((1, 8, count), lambda i: (at(i), 0, 0)),
         ],
-        out_specs=[row(3 * cw), row(cw), row(LANES), row(width)],
-        out_shape=[shape(3 * cw, bf16), shape(cw, bf16), shape(LANES, f32), shape(width, bf16)],
-        scratch_shapes=[pltpu.VMEM((count, width), bf16), pltpu.VMEM((count, LANES), f32)],
-        compiler_params=pltpu.CompilerParams(vmem_limit_bytes=60 * MB),
+        out_specs=[row(3 * cw), row(cw), row(LANES), last_spec],
+        out_shape=[shape(3 * cw, bf16), shape(cw, bf16), shape(LANES, f32), last_shape],
+        scratch_shapes=[pltpu.VMEM((count, width), bf16), pltpu.VMEM((count, LANES), f32)] + more,
+        compiler_params=pltpu.CompilerParams(vmem_limit_bytes=60 * MB, **params),
     )(me, tokens, gain, w_all, ow, cos, sin, meta, krow)
 
 
-def attn_backward(dmid, tokens, gain, qkv, att, aux, cos, sin, meta, krow, w_all, ow, groups, scale):
+def attn_backward_plain(cw, scale, dmid, tokens, gain, qkv, att, aux, cos, sin, meta, krow, w_all, ow, dw_hbm, do_hbm, dh1, side, dw, do, sems, *more):
+    attn_backward_kernel(cw, scale, dmid, tokens, gain, qkv, att, aux, cos, sin, meta, krow, w_all, ow, dh1, side, dw, do, *more)
+    pl.when(pl.program_id(0) == pl.num_programs(0) - 1)(lambda: attn_weights_out(dw, do, dw_hbm, do_hbm, sems))
+
+
+def attn_weights_out(dw, do, dw_hbm, do_hbm, sems):
+    copies = [pltpu.make_async_copy(a, b, sems.at[n]) for n, (a, b) in enumerate(((dw, dw_hbm), (do, do_hbm)))]
+    for c in copies:
+        c.start()
+    for c in copies:
+        c.wait()
+
+
+def attn_backward_fused(dims, cw, scale, dmid, tokens, gain, qkv, att, aux, cos, sin, meta, krow, w_all, ow, dw_hbm, do_hbm, out, dw, do, sems, h1, datt, watt, dqkv, dk_sum, dv_sum, *refs):
+    i = pl.program_id(0)
+    place = Place(dims)
+    sums = Scatter(dims, place, out, refs)
+    pl.when(i == 0)(place.greet)
+
+    @pl.when(i < sums.tiles)
+    def _():
+        tile, side = sums.tile.at[i % 2], sums.tile.at[i % 2, :, pl.ds(dmid.shape[1], LANES)]
+        attn_backward_kernel(cw, scale, dmid, tokens, gain, qkv, att, aux, cos, sin, meta, krow, w_all, ow, tile, side, dw, do, h1, datt, watt, dqkv, dk_sum, dv_sum)
+
+    pl.when(i == 0)(place.greeted)
+    sums.run(i)
+    pl.when(i == sums.tiles)(lambda: attn_weights_out(dw, do, dw_hbm, do_hbm, sems))
+
+
+def attn_backward(dims, cid, dmid, tokens, gain, qkv, att, aux, cos, sin, meta, krow, w_all, ow, groups, scale):
     total, width = dmid.shape
     cw = ow.shape[0]
     count = total // groups
-    row = lambda w: pl.BlockSpec((count, w), lambda i: (i, 0))
+    at = (lambda i: tile_group(i, dims)) if dims else (lambda i: i)
+    row = lambda w: pl.BlockSpec((count, w), lambda i: (at(i), 0))
+    wide = width + LANES
+    hbm = pl.BlockSpec(memory_space=pl.ANY)
+    if dims:
+        own = count // 4
+        kernel = functools.partial(attn_backward_fused, dims, cw, scale)
+        last_spec, last_shape = [whole_block((own, wide))], [jax.ShapeDtypeStruct((own, wide), f32)]
+        params, more = dict(collective_id=cid, has_side_effects=True), scatter_scratch(dims, own, wide)
+    else:
+        kernel = functools.partial(attn_backward_plain, cw, scale)
+        last_spec = [row(width), row(LANES)]
+        last_shape = [jax.ShapeDtypeStruct((total, w), bf16) for w in (width, LANES)]
+        params, more = {}, []
     return pl.pallas_call(
-        functools.partial(attn_backward_kernel, cw, scale),
-        grid=(groups,),
+        kernel,
+        grid=(groups + 2 + dims[0] if dims else groups,),
         in_specs=[
             row(width), row(width), whole_block(gain.shape), row(3 * cw), row(cw), row(LANES), row(LANES), row(LANES), row(8),
-            pl.BlockSpec((1, 8, count), lambda i: (i, 0, 0)),
-            whole_block(w_all.shape), whole_block(ow.shape),
+            pl.BlockSpec((1, 8, count), lambda i: (at(i), 0, 0)),
+            once(w_all.shape), once(ow.shape),
         ],
-        out_specs=[row(width + LANES), whole_block((3 * cw, width)), whole_block((cw, width))],
-        out_shape=[
-            jax.ShapeDtypeStruct((total, width + LANES), bf16),
-            jax.ShapeDtypeStruct((3 * cw, width), f32),
-            jax.ShapeDtypeStruct((cw, width), f32),
-        ],
+        out_specs=[hbm, hbm] + last_spec,
+        out_shape=[jax.ShapeDtypeStruct((3 * cw, width), f32), jax.ShapeDtypeStruct((cw, width), f32)] + last_shape,
         scratch_shapes=[
+            pltpu.VMEM((3 * cw, width), f32), pltpu.VMEM((cw, width), f32), pltpu.SemaphoreType.DMA((2,)),
             pltpu.VMEM((count, width), bf16), pltpu.VMEM((count, cw), bf16), pltpu.VMEM((count, cw), bf16), pltpu.VMEM((count, 3 * cw), bf16),
             pltpu.VMEM((count, LANES), f32), pltpu.VMEM((count, LANES), f32),
-        ],
-        compiler_params=pltpu.CompilerParams(vmem_limit_bytes=60 * MB),
+        ] + more,
+        compiler_params=pltpu.CompilerParams(vmem_limit_bytes=62 * MB, **params),
     )(dmid, tokens, gain, qkv, att, aux, cos, sin, meta, krow, w_all, ow)
 
 
@@ -256,49 +329,61 @@
     return [(at, min(size, total - at)) for at in range(0, total, size)]
 
 
-def ffn_kernel(
-    cap, me, h2, top, router, meta, posrow, gate_up, down,
-    produced, dh2, aux, gate_up_grad, down_grad,
-    wg, wu, wd, sg, su, sd, xc, gc, act, dgate, dup, yc, bc, gw, sems,
-):
+def chosen(posrow, i, cap):
+    slot = lax.broadcasted_iota(jnp.int32, (cap, LANES), 0)
+    return (slot == posrow[0, pl.ds(i, 1), :]).astype(bf16)
+
+
+def compact(cap, h2, top, posrow, weight, xc, gc):
+    def block(i):
+        at, to = rows_at(i, LANES), rows_at(i, cap)
+        choose = chosen(posrow, i, cap)
+        w = weight(i, at)
+        for start, size in pieces(h2.shape[1], 512):
+            cs = slice(start, start + size)
+            xc[to, cs] = nn(choose, h2[at, cs]).astype(bf16)
+            gated = (w * top[at, cs].astype(f32)).astype(bf16)
+            gc[to, cs] = nn(choose, gated).astype(bf16)
+
+    loop(h2.shape[0] // LANES, block)
+
+
+def stage_rows(hidden):
+    return max(r for r in range(16, 177, 16) if hidden % r == 0)
+
+
+def load_masters(gate_up, down, wg, wu, wd, stage, sems):
+    hidden, part = wd.shape[0], stage.shape[1]
+    jobs = [
+        (src.at[pl.ds(n * part, part)], dst.at[pl.ds(n * part, part)])
+        for n in range(hidden // part)
+        for src, dst in ((gate_up.at[:, 0, :], wg), (gate_up.at[:, 1, :], wu), (down, wd))
+    ]
+    copies = [pltpu.make_async_copy(job[0], stage.at[n % 2], sems.at[n % 2]) for n, job in enumerate(jobs)]
+    copies[0].start()
+    for n, (_, dst) in enumerate(jobs):
+        if n + 1 < len(jobs):
+            copies[n + 1].start()
+        copies[n].wait()
+
+        def cast(r, dst=dst, n=n):
+            at = rows_at(r, 16)
+            dst[at, :] = stage[n % 2, at, :].astype(bf16)
+
+        loop(part // 16, cast)
+
+
+def ffn_compute(cap, me, h2, top, router, meta, posrow, produced, dh2, side, aux, act, dgate, dup, wg, wu, wd, xc, gc):
     rows, width = h2.shape
     hidden = wd.shape[0]
     blocks = rows // LANES
-    step = pl.program_id(0)
-
-    def masters(back):
-        pairs = [(gate_up.at[:, 0, :], sg), (gate_up.at[:, 1, :], su), (down, sd)]
-        if back:
-            pairs = [(sg, gate_up_grad.at[:, 0, :]), (su, gate_up_grad.at[:, 1, :]), (sd, down_grad)]
-        return [pltpu.make_async_copy(a, b, sems.at[i]) for i, (a, b) in enumerate(pairs)]
-
-    @pl.when(step == 0)
-    def _():
-        copies = masters(False)
-        for c in copies:
-            c.start()
-        for c, a, b in zip(copies, (sg, su, sd), (wg, wu, wd), strict=True):
-            c.wait()
-
-            def cast(i, a=a, b=b):
-                at = rows_at(i, 32)
-                b[at, :] = a[at, :].astype(bf16)
-                a[at, :] = jnp.zeros((32, width), f32)
-
-            loop(hidden // 32, cast)
-
-    def gates(i):
-        at = rows_at(i, LANES)
-        found = gate_columns(nn(h2[at, :], router[...]), meta[at, 0:1], meta[at, 1:2], me[0])
+
+    def weight(i, at):
+        found = gate_columns(nn(h2[at, :], router[...]), meta[at, 4:5], meta[at, 5:6], me[0])
         aux[at, :] = found
-        gw[at, :] = (found[:, 0:1] * top[at, :].astype(f32)).astype(bf16)
-        slot = lax.broadcasted_iota(jnp.int32, (cap, LANES), 0)
-        choose = (slot == posrow[0, pl.ds(i, 1), :]).astype(bf16)
-        to = rows_at(i, cap)
-        xc[to, :] = nn(choose, h2[at, :]).astype(bf16)
-        gc[to, :] = nn(choose, gw[at, :]).astype(bf16)
-
-    loop(blocks, gates)
+        return found[:, 0:1]
+
+    compact(cap, h2, top, posrow, weight, xc, gc)
 
     for start, size in pieces(hidden, 256):
         fs = slice(start, start + size)
@@ -309,13 +394,7 @@
         dgate[:, fs] = (dact * up * sigmoid * (1.0 + gate * (1.0 - sigmoid))).astype(bf16)
         dup[:, fs] = (dact * silu).astype(bf16)
 
-        def grads(i, fs=fs):
-            at = rows_at(i, 512)
-            sd[fs, at] += tn(act[:, fs], gc[:, at])
-            sg[fs, at] += tn(dgate[:, fs], xc[:, at])
-            su[fs, at] += tn(dup[:, fs], xc[:, at])
-
-        loop(width // 512, grads)
+    yc, bc = gc, xc
 
     def results(i):
         at = rows_at(i, 512)
@@ -326,8 +405,7 @@
 
     def scatter(i):
         at, of = rows_at(i, LANES), rows_at(i, cap)
-        slot = lax.broadcasted_iota(jnp.int32, (cap, LANES), 0)
-        choose = (slot == posrow[0, pl.ds(i, 1), :]).astype(bf16)
+        choose = chosen(posrow, i, cap)
         found = aux[at, :]
         share = jnp.zeros((LANES, 1), f32)
         for start, size in pieces(width, 512):
@@ -336,46 +414,188 @@
             share = share + jnp.sum(y * top[at, cs].astype(f32), axis=1, keepdims=True)
             produced[at, cs] = (found[:, 0:1] * y).astype(bf16)
             dh2[at, cs] = tn(choose, bc[of, cs]).astype(bf16)
-        dh2[at, width:] = jnp.broadcast_to(found[:, 1:2] * share, (LANES, LANES)).astype(bf16)
+        side[at, :] = jnp.broadcast_to(found[:, 1:2] * share, (LANES, LANES)).astype(bf16)
 
     loop(blocks, scatter)
 
-    @pl.when(step == pl.num_programs(0) - 1)
+
+def ffn_kernel(cap, me, h2, top, router, meta, posrow, gate_up, down, produced, aux, act, dgate, dup, dh2, side, wg, wu, wd, xc, gc, stage, sems):
+    pl.when(pl.program_id(0) == 0)(lambda: load_masters(gate_up, down, wg, wu, wd, stage, sems))
+    ffn_compute(cap, me, h2, top, router, meta, posrow, produced, dh2, side, aux, act, dgate, dup, wg, wu, wd, xc, gc)
+
+
+def ffn_fused_kernel(dims, cap, me, h2, top, router, meta, posrow, gate_up, down, produced, aux, act, dgate, dup, out, wg, wu, wd, xc, gc, stage, sems, *refs):
+    i = pl.program_id(0)
+    place = Place(dims)
+    sums = Scatter(dims, place, out, refs)
+
+    @pl.when(i == 0)
     def _():
-        copies = masters(True)
+        place.greet()
+        load_masters(gate_up, down, wg, wu, wd, stage, sems)
+
+    @pl.when(i < sums.tiles)
+    def _():
+        tile, side = sums.tile.at[i % 2], sums.tile.at[i % 2, :, pl.ds(h2.shape[1], LANES)]
+        ffn_compute(cap, me, h2, top, router, meta, posrow, produced, tile, side, aux, act, dgate, dup, wg, wu, wd, xc, gc)
+
+    pl.when(i == 0)(place.greeted)
+    sums.run(i)
+
+
+def ffn(dims, cid, me, h2, top, router, meta, posrow, gate_up, down, cap):
+    total, width = h2.shape
+    hidden = down.shape[0]
+    tile = posrow.shape[1] * LANES
+    few = tile // LANES * cap
+    tiles = total // tile
+    at = (lambda i: tile_group(i, dims)) if dims else (lambda i: i)
+    row = lambda w: pl.BlockSpec((tile, w), lambda i: (at(i), 0))
+    some = pl.BlockSpec((few, hidden), lambda i: (at(i), 0))
+    hbm = pl.BlockSpec(memory_space=pl.ANY)
+    V = pltpu.VMEM
+    own = total // (dims[0] * dims[1] * dims[2] * 2) if dims else 0
+    wide = width + LANES
+    if dims:
+        kernel = functools.partial(ffn_fused_kernel, dims, cap)
+        last_spec, last_shape = [whole_block((own, wide))], [jax.ShapeDtypeStruct((own, wide), f32)]
+        params = dict(collective_id=cid, has_side_effects=True)
+    else:
+        kernel = functools.partial(ffn_kernel, cap)
+        last_spec = [row(width), row(LANES)]
+        last_shape = [jax.ShapeDtypeStruct((total, w), bf16) for w in (width, LANES)]
+        params = {}
+    return pl.pallas_call(
+        kernel,
+        grid=(tiles + 2 + dims[0] if dims else tiles,),
+        in_specs=[
+            pl.BlockSpec(memory_space=pltpu.SMEM), row(width), row(width), whole_block(router.shape), row(8),
+            pl.BlockSpec((1,) + posrow.shape[1:], lambda i: (at(i), 0, 0)), hbm, hbm,
+        ],
+        out_specs=[row(width), row(LANES), some, some, some] + last_spec,
+        out_shape=[
+            jax.ShapeDtypeStruct((total, width), bf16),
+            jax.ShapeDtypeStruct((total, LANES), f32),
+        ] + [jax.ShapeDtypeStruct((tiles * few, hidden), bf16)] * 3 + last_shape,
+        scratch_shapes=[V((hidden, width), bf16)] * 3 + [V((few, width), bf16)] * 2
+        + [V((2, stage_rows(hidden), width), f32), pltpu.SemaphoreType.DMA((2,))]
+        + (scatter_scratch(dims, own, wide) if dims else []),
+        compiler_params=pltpu.CompilerParams(vmem_limit_bytes=63 * MB, **params),
+    )(me, h2, top, router, meta, posrow, gate_up, down)
+
+
+def ffn_weights_compute(cap, first, h2, top, aux, posrow, act, dgate, dup, sg, su, sd, xc, gc):
+    width = h2.shape[1]
+    hidden = sd.shape[0]
+
+    @pl.when(first)
+    def _():
+        for s in (sg, su, sd):
+
+            def clear(i, s=s):
+                s[rows_at(i, 32), :] = jnp.zeros((32, width), f32)
+
+            loop(hidden // 32, clear)
+
+    compact(cap, h2, top, posrow, lambda i, at: aux[at, 0:1], xc, gc)
+    for start, size in pieces(hidden, 256):
+        fs = slice(start, start + size)
+
+        def grads(i, fs=fs):
+            at = rows_at(i, 512)
+            sd[fs, at] += tn(act[:, fs], gc[:, at])
+            sg[fs, at] += tn(dgate[:, fs], xc[:, at])
+            su[fs, at] += tn(dup[:, fs], xc[:, at])
+
+        loop(width // 512, grads)
+
+
+def ffn_weights_out(gate_up_grad, down_grad, sg, su, sd, sems):
+    pairs = [(sg, gate_up_grad.at[:, 0, :]), (su, gate_up_grad.at[:, 1, :]), (sd, down_grad)]
+    return [pltpu.make_async_copy(a, b, sems.at[i]) for i, (a, b) in enumerate(pairs)]
+
+
+def ffn_weights_kernel(cap, h2, top, aux, posrow, act, dgate, dup, gate_up_grad, down_grad, sg, su, sd, xc, gc, sems):
+    i = pl.program_id(0)
+    ffn_weights_compute(cap, i == 0, h2, top, aux, posrow, act, dgate, dup, sg, su, sd, xc, gc)
+
+    @pl.when(i == pl.num_programs(0) - 1)
+    def _():
+        copies = ffn_weights_out(gate_up_grad, down_grad, sg, su, sd, sems)
         for c in copies:
             c.start()
         for c in copies:
             c.wait()
 
 
-def ffn(me, h2, top, router, meta, posrow, gate_up, down, cap):
+def ffn_weights_fused(dims, cap, h2, top, aux, posrow, act, dgate, dup, extra, produced, gate_up_grad, down_grad, out, sg, su, sd, xc, gc, sems, load, *refs):
+    i = pl.program_id(0)
+    place = Place(dims)
+    sums = Scatter(dims, place, out, refs)
+    rows, width = h2.shape
+    copies = ffn_weights_out(gate_up_grad, down_grad, sg, su, sd, sems)
+    pl.when(i == 0)(place.greet)
+
+    @pl.when(i < sums.tiles)
+    def _():
+        tile = sums.tile.at[i % 2]
+        fetch = pltpu.make_async_copy(produced.at[rows_at(tile_group(i, dims), rows)], tile.at[:, pl.ds(0, width)], load)
+        fetch.start()
+        tile[:, width:] = extra[...]
+        ffn_weights_compute(cap, i == 0, h2, top, aux, posrow, act, dgate, dup, sg, su, sd, xc, gc)
+        fetch.wait()
+
+    @pl.when(i == sums.tiles)
+    def _():
+        for c in copies:
+            c.start()
+
+    pl.when(i == 0)(place.greeted)
+    sums.run(i)
+
+    @pl.when(i == sums.steps - 1)
+    def _():
+        for c in copies:
+            c.wait()
+
+
+def ffn_weights(dims, cid, h2, top, aux, posrow, act, dgate, dup, extra, produced, cap):
     total, width = h2.shape
-    hidden = down.shape[0]
+    hidden = act.shape[1]
     tile = posrow.shape[1] * LANES
     few = tile // LANES * cap
-    row = lambda w: pl.BlockSpec((tile, w), lambda i: (i, 0))
+    tiles = total // tile
+    at = (lambda i: tile_group(i, dims)) if dims else (lambda i: i)
+    row = lambda w: pl.BlockSpec((tile, w), lambda i: (at(i), 0))
+    some = pl.BlockSpec((few, hidden), lambda i: (at(i), 0))
     hbm = pl.BlockSpec(memory_space=pl.ANY)
     V = pltpu.VMEM
+    scratch = [V((hidden, width), f32)] * 3 + [V((few, width), bf16)] * 2 + [pltpu.SemaphoreType.DMA((3,))]
+    out_specs = [hbm, hbm]
+    out_shape = [jax.ShapeDtypeStruct((hidden, 2, width), f32), jax.ShapeDtypeStruct((hidden, width), f32)]
+    in_specs = [
+        row(width), row(width), row(LANES), pl.BlockSpec((1,) + posrow.shape[1:], lambda i: (at(i), 0, 0)), some, some, some,
+    ]
+    operands = [h2, top, aux, posrow, act, dgate, dup]
+    if dims:
+        own = tile // 4
+        kernel = functools.partial(ffn_weights_fused, dims, cap)
+        wide = width + LANES
+        operands, in_specs = operands + [extra, produced], in_specs + [row(LANES), hbm]
+        out_specs, out_shape = out_specs + [once((own, wide))], out_shape + [jax.ShapeDtypeStruct((own, wide), f32)]
+        scratch = scratch + [pltpu.SemaphoreType.DMA] + scatter_scratch(dims, own, wide)
+        params = dict(collective_id=cid, has_side_effects=True)
+    else:
+        kernel, params = functools.partial(ffn_weights_kernel, cap), {}
     return pl.pallas_call(
-        functools.partial(ffn_kernel, cap),
-        grid=(total // tile,),
-        in_specs=[
-            pl.BlockSpec(memory_space=pltpu.SMEM), row(width), row(width), whole_block(router.shape), row(8),
-            pl.BlockSpec((1,) + posrow.shape[1:], lambda i: (i, 0, 0)), hbm, hbm,
-        ],
-        out_specs=[row(width), row(width + LANES), row(LANES), hbm, hbm],
-        out_shape=[
-            jax.ShapeDtypeStruct((total, width), bf16),
-            jax.ShapeDtypeStruct((total, width + LANES), bf16),
-            jax.ShapeDtypeStruct((total, LANES), f32),
-            jax.ShapeDtypeStruct(gate_up.shape, f32),
-            jax.ShapeDtypeStruct(down.shape, f32),
-        ],
-        scratch_shapes=[V((hidden, width), bf16)] * 3 + [V((hidden, width), f32)] * 3 + [V((few, width), bf16)] * 2
-        + [V((few, hidden), bf16)] * 3 + [V((few, width), bf16)] * 2 + [V((tile, width), bf16), pltpu.SemaphoreType.DMA((3,))],
-        compiler_params=pltpu.CompilerParams(vmem_limit_bytes=63 * MB),
-    )(me, h2, top, router, meta, posrow, gate_up, down)
+        kernel,
+        grid=(tiles + 2 + dims[0] if dims else tiles,),
+        in_specs=in_specs,
+        out_specs=out_specs,
+        out_shape=out_shape,
+        scratch_shapes=scratch,
+        compiler_params=pltpu.CompilerParams(vmem_limit_bytes=63 * MB, **params),
+    )(*operands)
 
 
 def ag_kernel(dims, halves, src, out, local_sem, zs, zr, xs, xr, ys, yr, cs, cr):
@@ -521,160 +741,294 @@
     )(v)
 
 
-def rs_kernel(dims, src, out, loc, crv, frv, srv, zrv, lsem, cs, cr, fs, fr, ss, sr, zs, zr):
-    nz, nx, ny = dims
-    gi = lax.axis_index("grp"); ei = lax.axis_index("exp")
-    z, x = gi // nx, gi % nx
-    y, c = ei // 2, ei % 2
-    ne = ny * 2
-    rows, width = out.shape
-    part = rows // 2
-    span = 2 * nz - 1
-    def dev(z_, x_, y_, c_):
-        return (z_ * nx + x_, y_ * 2 + c_)
-    def slot(z_, x_, y_, c_):
-        return (z_ * nx + x_) * ne + y_ * 2 + c_
-    barrier = pltpu.get_barrier_semaphore()
-    def sig(d):
-        pl.semaphore_signal(barrier, inc=1, device_id=d, device_id_type=MESH)
-    sig(dev(z, 1 - x, y, c)); sig(dev(z, x, 1 - y, c)); sig(dev(z, x, y, 1 - c))
-    @pl.when(z > 0)
-    def _(): sig(dev(z - 1, x, y, c))
-    @pl.when(z < nz - 1)
-    def _(): sig(dev(z + 1, x, y, c))
-    pl.semaphore_wait(barrier, 3 + (z > 0).astype(jnp.int32) + (z < nz - 1).astype(jnp.int32))
-
-    def flip(v, r):
-        return 1 - v if r else v
-    def remote(s, d, a, b, to):
-        return pltpu.make_async_remote_copy(src_ref=s, dst_ref=d, send_sem=a, recv_sem=b, device_id=to, device_id_type=MESH)
-    deltas = [d for k in range(nz - 1, 0, -1) for d in (k, -k)] + [0]
-    def valid(d):
-        return (z + d >= 0) & (z + d < nz)
-    classes = [(1, 1), (1, 0), (0, 1), (0, 0)]
-    def piece(ref, lead, h):
-        return ref.at[lead, pl.ds(h * part, part)]
-    def load(d, rx, ry):
-        i = (z + d) * 4 + rx * 2 + ry
-        return pltpu.make_async_copy(src.at[slot(z + d, flip(x, rx), flip(y, ry), c)], loc.at[i], lsem.at[i])
-    def core(d, rx, ry, h):
-        i = (z + d) * 4 + rx * 2 + ry
-        return remote(src.at[slot(z + d, flip(x, rx), flip(y, ry), 1 - c), pl.ds(h * part, part)],
-                      piece(crv, i, h), cs.at[i * 2 + h], cr.at[i * 2 + h], dev(z, x, y, 1 - c))
-    def first(d, other, h):
-        rx, ry = (other, 1) if h == 0 else (1, other)
-        i = (z + d) * 4 + rx * 2 + ry
-        k = ((z + d) * 2 + other) * 2 + h
-        to = dev(z, x, 1 - y, c) if h == 0 else dev(z, 1 - x, y, c)
-        return remote(piece(loc, i, h), frv.at[k], fs.at[k], fr.at[k], to)
-    def second(d, h):
-        rx, ry = (1, 0) if h == 0 else (0, 1)
-        i = (z + d) * 4 + rx * 2 + ry
-        k = (z + d) * 2 + h
-        to = dev(z, 1 - x, y, c) if h == 0 else dev(z, x, 1 - y, c)
-        return remote(piece(loc, i, h), srv.at[k], ss.at[k], sr.at[k], to)
-    def zcopy(d, h, arriving_from):
-        pass
-    def zk(way, dist, h):
-        return (way * nz + dist) * 2 + h
-    def zsend(d, h):
-        way = 0 if d > 0 else 1
-        i = (z + d) * 4
-        k = zk(way, abs(d) - 1, h)
-        to = dev(z + (1 if d > 0 else -1), x, y, c)
-        return remote(piece(loc, i, h), zrv.at[k], zs.at[k], zr.at[k], to)
-    def zwait(way, dist, h):
-        k = zk(way, dist, h)
-        remote(piece(loc, 0, h), zrv.at[k], zs.at[k], zr.at[k], dev(z, x, y, 1 - c)).wait_recv()
-        return zrv.at[k]
-    def add(i, h, *others):
+def target_order(nz):
+    low, high, order = 0, nz - 1, []
+    while low <= high:
+        order += [low] if low == high else [low, high]
+        low, high = low + 1, high - 1
+    return order
+
+
+def tile_group(i, dims):
+    nz, nx, _ = dims
+    i = jnp.minimum(i, nz * nx - 1)
+    j = i // nx
+    t = jnp.where(j % 2 == 0, j // 2, nz - 1 - j // 2)
+    return t * nx + i % nx
+
+
+class Place:
+    def __init__(self, dims):
+        self.nz, self.nx, self.ny = dims
+        gi, ei = lax.axis_index("grp"), lax.axis_index("exp")
+        self.z, self.x = gi // self.nx, gi % self.nx
+        self.y, self.c = ei // 2, ei % 2
+
+    def device(self, z, x, y, c):
+        return (z * self.nx + x, y * 2 + c)
+
+    def core(self):
+        return self.device(self.z, self.x, self.y, 1 - self.c)
+
+    def along_x(self):
+        return self.device(self.z, 1 - self.x, self.y, self.c)
+
+    def along_y(self):
+        return self.device(self.z, self.x, 1 - self.y, self.c)
+
+    def along_z(self, by):
+        return self.device(self.z + by, self.x, self.y, self.c)
+
+    def greet(self):
+        barrier = pltpu.get_barrier_semaphore()
+
+        def signal(device):
+            pl.semaphore_signal(barrier, inc=1, device_id=device, device_id_type=MESH)
+
+        signal(self.along_x())
+        signal(self.along_y())
+        signal(self.core())
+        pl.when(self.z > 0)(lambda: signal(self.along_z(-1)))
+        pl.when(self.z < self.nz - 1)(lambda: signal(self.along_z(1)))
+
+    def greeted(self):
+        inner = (self.z > 0).astype(jnp.int32) + (self.z < self.nz - 1).astype(jnp.int32)
+        pl.semaphore_wait(pltpu.get_barrier_semaphore(), 3 + inner)
+
+
+def remote(src, dst, sent, came, device):
+    return pltpu.make_async_remote_copy(
+        src_ref=src, dst_ref=dst, send_sem=sent, recv_sem=came, device_id=device, device_id_type=MESH
+    )
+
+
+def scatter_scratch(dims, rows, width):
+    nz, nx, _ = dims
+    tiles, half = nz * nx, rows // 2
+    D, V = pltpu.SemaphoreType.DMA, lambda *s: pltpu.VMEM(s, bf16)
+    return [
+        V(2, 4 * rows, width),
+        V(4, 2, rows, width),
+        V(tiles, 2, rows, width),
+        V(tiles, half, width), V(nz, 2, half, width),
+        V(nz, half, width), V(nz, half, width),
+        V(nz + 1, rows, width),
+        D((tiles * 2,)), D((tiles * 2,)), D((tiles,)), D((tiles,)), D((nz * 2,)), D((nz * 2,)),
+        D((nz,)), D((nz,)), D((nz,)), D((nz,)), D((nz,)), D((nz + 1,)),
+    ]
+
+
+SCATTER_REFS = 20
+
+
+class Scatter:
+    def __init__(self, dims, place, out, refs):
+        self.dims, self.place, self.out = dims, place, out
+        (self.tile, self.crv, self.acc, self.ya, self.xb, self.xa, self.yb, self.zv,
+         self.cs, self.cr, self.yas, self.yar, self.xbs, self.xbr,
+         self.xas, self.xar, self.ybs, self.ybr, self.zs, self.zr) = refs
+        self.rows = out.shape[0]
+        self.half = self.rows // 2
+        self.order = target_order(dims[0])
+        self.tiles = dims[0] * dims[1]
+        self.steps = self.tiles + 2 + dims[0]
+
+    def add(self, into, *others):
         def step(r, _):
-            at = pl.ds(pl.multiple_of(r * 16, 16), 16)
-            here = pl.ds(pl.multiple_of(h * part + r * 16, 16), 16)
-            total = loc[i, here, :].astype(jnp.float32)
-            for o in others:
-                total = total + o[at, :].astype(jnp.float32)
-            loc[i, here, :] = total.astype(loc.dtype)
+            at = rows_at(r, 16)
+            total = others[0][at, :].astype(f32)
+            for o in others[1:]:
+                total = total + o[at, :].astype(f32)
+            into[at, :] = total.astype(into.dtype)
             return 0
-        lax.fori_loop(0, part // 16, step, 0)
-    for cl in classes:
-        for d in deltas:
-            def go(cl=cl, d=d):
-                load(d, *cl).start()
-                for h in range(2):
-                    core(d, *cl, h).start()
-            pl.when(valid(d))(go)
-    def got_core(d, rx, ry, h, *more):
-        i = (z + d) * 4 + rx * 2 + ry
-        core(d, rx, ry, h).wait_recv()
-        add(i, h, crv.at[i, pl.ds(h * part, part)], *more)
-    def each(f):
-        for d in deltas:
-            pl.when(valid(d))(functools.partial(f, d))
-    def c11(d):
-        load(d, 1, 1).wait()
-        for h in range(2):
-            got_core(d, 1, 1, h)
-            first(d, 1, h).start()
-    each(c11)
-    def c_first(d):
-        load(d, 0, 1).wait(); load(d, 1, 0).wait()
-        got_core(d, 0, 1, 0); first(d, 0, 0).start()
-        got_core(d, 1, 0, 1); first(d, 0, 1).start()
-    each(c_first)
-    def c_second(d):
-        first(d, 1, 0).wait_recv()
-        got_core(d, 1, 0, 0, frv.at[((z + d) * 2 + 1) * 2 + 0]); second(d, 0).start()
-        first(d, 1, 1).wait_recv()
-        got_core(d, 0, 1, 1, frv.at[((z + d) * 2 + 1) * 2 + 1]); second(d, 1).start()
-    each(c_second)
-    def c_last(d):
-        load(d, 0, 0).wait()
-        for h in range(2):
-            first(d, 0, h).wait_recv()
-            second(d, h).wait_recv()
-            more = [frv.at[((z + d) * 2) * 2 + h], srv.at[(z + d) * 2 + h]]
-            got_core(d, 0, 0, h, *more)
-            if d != 0:
-                way = 0 if d > 0 else 1
-                def chained(h=h):
-                    add((z + d) * 4, h, zwait(way, abs(d), h))
-                pl.when(z > 0 if d > 0 else z < nz - 1)(chained)
-                zsend(d, h).start()
-    each(c_last)
-    for h in range(2):
-        def left(h=h): add(z * 4, h, zwait(0, 0, h))
-        def right(h=h): add(z * 4, h, zwait(1, 0, h))
-        pl.when(z > 0)(left)
-        pl.when(z < nz - 1)(right)
-    def finish(r, _):
-        at = pl.ds(pl.multiple_of(r * 16, 16), 16)
-        out[at, :] = loc[z * 4, at, :].astype(out.dtype)
-        return 0
-    lax.fori_loop(0, rows // 16, finish, 0)
-    def drain(d):
-        for cl in classes:
-            for h in range(2):
-                core(d, *cl, h).wait_send()
-        for h in range(2):
-            first(d, 0, h).wait_send(); first(d, 1, h).wait_send(); second(d, h).wait_send()
-            if d != 0:
-                zsend(d, h).wait_send()
-    each(drain)
+
+        lax.fori_loop(0, into.shape[0] // 16, step, 0)
+
+    def low(self, k, q):
+        return self.acc.at[k, q, pl.ds(0, self.half)]
+
+    def high(self, k, q):
+        return self.acc.at[k, q, pl.ds(self.half, self.half)]
+
+    def shard(self, k, q, c):
+        return self.tile.at[k % 2, rows_at(q * 2 + c, self.rows)]
+
+    def c_core(self, k, q):
+        p, s = self.place, k * 2 + q
+        return remote(self.shard(k, q, 1 - p.c), self.crv.at[k % 4, q], self.cs.at[s], self.cr.at[s], p.core())
+
+    def c_ya(self, k):
+        p = self.place
+        return remote(self.low(k, 1 - p.y), self.ya.at[k], self.yas.at[k], self.yar.at[k], p.along_y())
+
+    def c_xb(self, k, q):
+        p, j = self.place, k // 2
+        s = j * 2 + q
+        return remote(self.high(k, q), self.xb.at[j, q], self.xbs.at[s], self.xbr.at[s], p.along_x())
+
+    def c_xa(self, k):
+        p, j = self.place, k // 2
+        return remote(self.low(k, p.y), self.xa.at[j], self.xas.at[j], self.xar.at[j], p.along_x())
+
+    def c_yb(self, k):
+        p, j = self.place, k // 2
+        return remote(self.high(k, 1 - p.y), self.yb.at[j], self.ybs.at[j], self.ybr.at[j], p.along_y())
+
+    def c_z(self, k, way):
+        p, t = self.place, self.order[k // 2]
+        slot = t if way > 0 else jnp.where(p.z - 1 == t, self.dims[0], t)
+        return remote(self.acc.at[k, p.y], self.zv.at[slot], self.zs.at[t], self.zr.at[slot], p.along_z(way))
+
+    def z_wait(self, k, slot):
+        remote(self.acc.at[k, self.place.y], self.zv.at[slot], self.zs.at[0], self.zr.at[slot], self.place.core()).wait_recv()
+
+    def phase_s(self, k):
+        for q in range(2):
+            self.c_core(k, q).start()
+
+    def phase_b(self, k):
+        p = self.place
+        for q in range(2):
+            self.c_core(k, q).wait_recv()
+            self.add(self.acc.at[k, q], self.shard(k, q, p.c), self.crv.at[k % 4, q])
+        self.c_ya(k).start()
+
+        def give():
+            for q in range(2):
+                self.c_xb(k, q).start()
+
+        pl.when(p.x != k % 2)(give)
+        for q in range(2):
+            self.c_core(k, q).wait_send()
+
+    def phase_c(self, k):
+        p, j = self.place, k // 2
+
+        def give():
+            self.c_ya(k).wait_recv()
+            self.add(self.low(k, p.y), self.low(k, p.y), self.ya.at[k])
+            self.c_xa(k).start()
+
+        def keep():
+            self.c_xb(k, 1 - p.y).wait_recv()
+            self.add(self.high(k, 1 - p.y), self.high(k, 1 - p.y), self.xb.at[j, 1 - p.y])
+            self.c_yb(k).start()
+
+        pl.when(p.x != k % 2)(give)
+        pl.when(p.x == k % 2)(keep)
+
+    def phase_d(self, k):
+        p, j, t, nz = self.place, k // 2, self.order[k // 2], self.dims[0]
+
+        def keep():
+            self.c_ya(k).wait_recv()
+            self.c_xa(k).wait_recv()
+            self.add(self.low(k, p.y), self.low(k, p.y), self.ya.at[k], self.xa.at[j])
+            self.c_xb(k, p.y).wait_recv()
+            self.c_yb(k).wait_recv()
+            self.add(self.high(k, p.y), self.high(k, p.y), self.xb.at[j, p.y], self.yb.at[j])
+            if t > 0:
+                pl.when(p.z == 0)(lambda: self.c_z(k, 1).start())
+            if t < nz - 1:
+                pl.when(p.z == nz - 1)(lambda: self.c_z(k, -1).start())
+
+        pl.when(p.x == k % 2)(keep)
+
+    def phase_e(self, k, h):
+        p, t, nz = self.place, self.order[k // 2], self.dims[0]
+        mine = p.x == k % 2
+        acc = self.acc.at[k, p.y]
+
+        def pass_on(way):
+            def run():
+                self.z_wait(k, t)
+                self.add(acc, acc, self.zv.at[t])
+                self.c_z(k, way).start()
+
+            return run
+
+        if h < t:
+            pl.when(mine & (p.z == h))(pass_on(1))
+        if nz - 1 - h > t:
+            pl.when(mine & (p.z == nz - 1 - h))(pass_on(-1))
+        if h == max(t, nz - 1 - t):
+
+            def last():
+                others = [acc]
+                for there, slot in ((t > 0, t), (t < nz - 1, nz)):
+                    if there:
+                        self.z_wait(k, slot)
+                        others.append(self.zv.at[slot])
+                self.add(self.out, *others)
+
+            pl.when(mine & (p.z == t))(last)
+
+    def drain(self):
+        p = self.place
+        for k in range(self.tiles):
+            self.c_ya(k).wait_send()
+
+            def give(k=k):
+                self.c_xa(k).wait_send()
+                for q in range(2):
+                    self.c_xb(k, q).wait_send()
+
+            def keep(k=k):
+                self.c_yb(k).wait_send()
+                pl.when(p.z != self.order[k // 2])(lambda: self.c_z(k, 1).wait_send())
+
+            pl.when(p.x != k % 2)(give)
+            pl.when(p.x == k % 2)(keep)
+
+    def run(self, i):
+        for step in range(self.steps):
+
+            def phases(step=step):
+                for lag, phase in enumerate([self.phase_s, self.phase_b, self.phase_c, self.phase_d]):
+                    if 0 <= step - lag < self.tiles:
+                        phase(step - lag)
+                for h in range(1, self.dims[0]):
+                    if 0 <= step - 3 - h < self.tiles:
+                        self.phase_e(step - 3 - h, h)
+                if step == self.steps - 1:
+                    self.drain()
+
+            pl.when(i == step)(phases)
+
+
+def scatter_kernel_body(dims, src, out, *refs):
+    i = pl.program_id(0)
+    place = Place(dims)
+    s = Scatter(dims, place, out, refs)
+
+    @pl.when(i == 0)
+    def _():
+        place.greet()
+        place.greeted()
+
+    @pl.when(i < s.tiles)
+    def _():
+        def copy(r):
+            at = rows_at(r, 64)
+            s.tile[i % 2, at, :] = src[at, :]
+        loop(src.shape[0] // 64, copy)
+
+    s.run(i)
+
 
 def scatter_kernel(p, dims, cid):
     nz, nx, ny = dims
     n, rows, width = p.shape
-    D = pltpu.SemaphoreType.DMA
-    V = lambda *s: pltpu.VMEM(s, p.dtype)
+    groups = nz * nx
+    p = p.reshape(n * rows, width)
     return pl.pallas_call(
-        functools.partial(rs_kernel, dims),
-        out_shape=jax.ShapeDtypeStruct((rows, width), jnp.float32),
-        in_specs=[pl.BlockSpec(memory_space=pl.ANY)],
-        out_specs=pl.BlockSpec(memory_space=pltpu.VMEM),
-        scratch_shapes=[V(nz * 4, rows, width), V(nz * 4, rows, width), V(nz * 4, rows // 2, width), V(nz * 2, rows // 2, width), V(nz * 4, rows // 2, width),
-            D((nz * 4,)), D((nz * 8,)), D((nz * 8,)), D((nz * 4,)), D((nz * 4,)), D((nz * 2,)), D((nz * 2,)), D((nz * 4,)), D((nz * 4,))],
-        compiler_params=pltpu.CompilerParams(collective_id=cid, has_side_effects=True, vmem_limit_bytes=56 * 1024 * 1024),
+        functools.partial(scatter_kernel_body, dims),
+        grid=(groups + 2 + nz,),
+        in_specs=[pl.BlockSpec((4 * rows, width), lambda i: (tile_group(i, dims), 0))],
+        out_specs=whole_block((rows, width)),
+        out_shape=jax.ShapeDtypeStruct((rows, width), f32),
+        scratch_shapes=scatter_scratch(dims, rows, width),
+        compiler_params=pltpu.CompilerParams(collective_id=cid, has_side_effects=True, vmem_limit_bytes=60 * MB),
     )(p)
 
 
@@ -740,7 +1094,7 @@
 
     def gather_all(v, cid):
         if dims is None:
-            return lax.all_gather(v, both, axis=0, tiled=False)
+            return lax.all_gather(kept(v), both, axis=0, tiled=True)
         return gather_kernel(v, dims, cid)
 
     def scatter_all(v, cid):
@@ -748,6 +1102,9 @@
         if dims is None:
             return lax.psum_scatter(v, both, scatter_dimension=0, tiled=False).astype(f32)
         return scatter_kernel(v, dims, cid)
+
+    def summed(parts):
+        return jnp.concatenate([scatter_all(v, 0) for v in parts], axis=1) if dims is None else parts[0]
 
     blocks = block_order.shape[1]
     start_row = member * own_rows
@@ -766,9 +1123,14 @@
         axis=1,
     )
     at_route = 2 + 2 * experts
-    sent = jnp.concatenate([layer_input, jnp.pad(small, ((0, 0), (0, LANES - small.shape[1])))], axis=1)
-    tokens = gather_all(sent, 1).reshape(total, width + LANES)
-    tops = gather_all(out_grad, 2).reshape(total, width)
+    small = jnp.pad(small, ((0, 0), (0, LANES - small.shape[1])))
+    if dims is None:
+        tokens = gather_all(layer_input, 1).reshape(total, width)
+        extra = gather_all(small, 2).reshape(total, LANES)
+    else:
+        sent = jnp.concatenate([layer_input, small], axis=1)
+        tokens = gather_all(sent, 1).reshape(total, width + LANES)
+        extra = tokens[:, width:]
 
     query_low = query_master[0].astype(bf16)
     kv_low = kv_master.astype(bf16).reshape(depth * 2, groups, cw)
@@ -781,7 +1143,6 @@
     kv_weight = kv_all.reshape(width, 2 * cw)
     output_weight = output_master[0].astype(bf16)
 
-    extra = tokens[:, width:]
     tables = extra.reshape(devices, own_rows, LANES)[:, :depth, :at_route].reshape(width, at_route)
     gains = tables[:, :2].astype(f32)
     router = tables[:, 2:]
@@ -789,43 +1150,58 @@
     wide = lambda v: jnp.pad(v, ((0, 0), (0, LANES - v.shape[1])))
     routes = extra[:, at_route : at_route + 4].astype(jnp.int32)
     column = extra.reshape(groups, group_rows, LANES)[:, : blocks + 2, at_route + 4].astype(jnp.int32)
-    anchor, place = layout(
-        column[:, 0:1] * 16 + column[:, 1:2], column[:, 2:], group_rows, own_rows // 2
-    )
-    cos, sin = rotary_tables(place.reshape(total))
-    zero = jnp.zeros((total, 4), jnp.int32)
-    attn_meta = jnp.concatenate(
-        [anchor.reshape(total, 1), (anchor - place).reshape(total, 1), routes[:, :2], zero], axis=1
-    )
-    key_rows = jnp.broadcast_to(anchor[:, None, :], (groups, 8, group_rows))
+
+    def where_rows_stand(column):
+        anchor, place = layout(
+            column[:, 0:1] * 16 + column[:, 1:2], column[:, 2:], group_rows, own_rows // 2
+        )
+        cos, sin = rotary_tables(place.reshape(total))
+        meta = jnp.concatenate(
+            [anchor.reshape(total, 1), (anchor - place).reshape(total, 1), routes, routes[:, :2]], axis=1
+        )
+        return cos, sin, meta, jnp.broadcast_to(anchor[:, None, :], (groups, 8, group_rows))
+
+    cos, sin, meta, key_rows = where_rows_stand(column)
     gain_one, gain_two = gains[:, 0], gains[:, 1]
     w_all = jnp.concatenate([query_weight, kv_weight, wide(router[:, :experts])], axis=1)
 
-    qkv, att, aux, attn_part = attn_forward(
-        me, tokens, gain_one[None], w_all, output_weight, cos, sin, attn_meta, key_rows, groups, scale
+    qkv, att, aux, attn_sum = attn_forward(
+        dims, 3, me, tokens, gain_one[None], w_all, output_weight, cos, sin, meta, key_rows, groups, scale
     )
     own = (group * members + member) * own_rows
     attn_gates = lax.dynamic_slice(aux, (own, 2), (own_rows, 2))
     inputs = layer_input.astype(f32)
-    middle = inputs + scatter_all(attn_part, 3)
+    middle = inputs + summed([attn_sum])
     inverse_two = lax.rsqrt(jnp.mean(middle * middle, axis=1, keepdims=True) + epsilon)
     normed_two = middle * inverse_two
     hidden_two = (normed_two * gain_two).astype(bf16)
+    if dims is None:
+        out_grad, hidden_two = lax.optimization_barrier((out_grad, hidden_two))
     h2 = gather_all(hidden_two, 4).reshape(total, width)
-
-    ffn_meta = jnp.concatenate([routes[:, 2:], zero, zero[:, :2]], axis=1)
+    tops = lax.all_gather(out_grad, both, axis=0, tiled=True)
+
     named = (routes[:, 2] == member) | (routes[:, 3] == member)
     named = named.reshape(devices, own_rows)
     position = jnp.cumsum(named.astype(jnp.int32), axis=1) - 1
     position = jnp.where(named, position, -1)
     tile_blocks = 4
-    produced, dh2, ffn_aux, gate_up_grad, down_grad = ffn(
-        me, h2, tops, wide(router[:, experts:]), ffn_meta,
-        position.reshape(devices // tile_blocks, tile_blocks, own_rows),
+    position = position.reshape(devices // tile_blocks, tile_blocks, own_rows)
+    produced, ffn_aux, act, dgate, dup, *dh2_parts = ffn(
+        dims, 5, me, h2, tops, wide(router[:, experts:]), meta, position,
         gate_up_master[0], down_master[0], capacity,
     )
+    if dims is None:
+        gate_up_grad, down_grad = ffn_weights(
+            dims, 0, h2, tops, ffn_aux, position, act, dgate, dup, None, None, capacity
+        )
+        gate_up_grad, dh2_parts, produced = lax.optimization_barrier((gate_up_grad, dh2_parts, produced))
+        back = summed(dh2_parts)
+        produced, back = lax.optimization_barrier((produced, back))
+        ffn_sum = scatter_all(produced, 0)
+        ffn_sum, back = lax.optimization_barrier((ffn_sum, back))
+    else:
+        back = summed(dh2_parts)
     ffn_gates = lax.dynamic_slice(ffn_aux, (own, 2), (own_rows, 2))
-    back = scatter_all(dh2, 5)
     top_grad = out_grad.astype(f32)
     ffn_logit_grad = logit_grad(own_ffn_route, ffn_gates, back[:, width : width + 1], experts)
     hidden_two_grad = back[:, :width] + jnp.einsum(
@@ -838,11 +1214,12 @@
     if dims is None:
         again, dmid = lax.optimization_barrier((layer_input, dmid))
         tokens = gather_all(again, 9).reshape(total, width)
-    dh1, dw, do = attn_backward(
-        dmid, tokens, gain_one[None], qkv, att, aux, cos, sin, attn_meta, key_rows, w_all, output_weight, groups, scale
-    )
-    final = middle + scatter_all(produced, 7)
-    back = scatter_all(dh1, 8)
+        column, dmid = lax.optimization_barrier((column, dmid))
+        cos, sin, meta, key_rows = where_rows_stand(column)
+    dw, do, *dh1_parts = attn_backward(
+        dims, 8, dmid, tokens, gain_one[None], qkv, att, aux, cos, sin, meta, key_rows, w_all, output_weight, groups, scale
+    )
+    back = summed(dh1_parts)
     inverse_one = lax.rsqrt(jnp.mean(inputs * inputs, axis=1, keepdims=True) + epsilon)
     normed_one = inputs * inverse_one
     hidden_one = (normed_one * gain_one).astype(bf16)
@@ -859,16 +1236,29 @@
     sums = jnp.concatenate(
         [gain_one_grad[:, None], gain_two_grad[:, None], route_grad[0], route_grad[1]], axis=1
     )
-    sums = lax.psum_scatter(sums, both, scatter_dimension=0, tiled=True)
 
     kv_part = dw[cw:].reshape(2 * cw, groups, members, depth)
     kv_part = lax.psum_scatter(kv_part.astype(bf16), "exp", scatter_dimension=2, tiled=False)
+    if dims is None:
+        sums = lax.psum_scatter(sums, both, scatter_dimension=0, tiled=True)
+    else:
+        beside = jnp.pad(
+            sums.astype(bf16).reshape(devices, depth, sums.shape[1]),
+            ((0, 0), (0, own_rows - depth), (0, LANES - sums.shape[1])),
+        ).reshape(total, LANES)
+        gate_up_grad, down_grad, ffn_sum = ffn_weights(
+            dims, 7, h2, tops, ffn_aux, position, act, dgate, dup, beside, produced, capacity
+        )
+        kv_part, ffn_sum = lax.optimization_barrier((kv_part, ffn_sum))
+        sums = ffn_sum[:depth, width : width + sums.shape[1]]
+        ffn_sum = ffn_sum[:, :width]
     query_part = dw[:cw].astype(bf16).reshape(cw, groups, width // groups)
     pieces_out = jnp.concatenate(
         [query_part.transpose(1, 0, 2).reshape(groups, -1), kv_part.transpose(1, 0, 2).reshape(groups, -1)],
         axis=1,
     )
     pieces_in = lax.all_to_all(pieces_out, "grp", split_axis=0, concat_axis=0, tiled=True)
+    final = middle + ffn_sum
     cut = cw * (width // groups)
     query_grad = pieces_in[:, :cut].reshape(width, width // groups).T.astype(f32)
     kv_grad = (

time: 1380 us -> 1130 us (0.82)
  the two profiles are of different devices: /device:TPU:0 before, /device:TPU:22 now
where the time goes in v2:
time: 1130 us; the launch traced here: 1110 us
  Pallas kernels  907 us (80%)
  local copies, waits for them, and re-layouts  71.4 us (6%)
  other arithmetic  43.1 us (4%)
  blocking collectives  39.7 us (4%)
  waiting for transfers between devices  25.8 us (2%)
  between operations  15.1 us (1%)
    pallas_call x3, Pallas kernels, gather_kernel(): pl.pallas_call(functools.partial(ag_kernel, dims, halves), out_shape=jax....  249 us
    pallas_call x1, Pallas kernels, ffn(): pl.pallas_call(kernel, grid=(tiles + 2 + dims[0] if dims else tiles,), in...  195 us
    pallas_call x1, Pallas kernels, attn_backward(): pl.pallas_call(kernel, grid=(groups + 2 + dims[0] if dims else groups,),...  176 us
    pallas_call x1, Pallas kernels, attn_forward(): pl.pallas_call(kernel, grid=(groups + 2 + dims[0] if dims else groups,),...  144 us
    pallas_call x1, Pallas kernels, ffn_weights(): pl.pallas_call(kernel, grid=(tiles + 2 + dims[0] if dims else tiles,), in...  143 us
    unnamed x82, local copies, waits for them, and re-layouts  44.1 us
    all_to_all x1, blocking collectives, body(): lax.all_to_all(pieces_out, 'grp', split_axis=0, concat_axis=0, tiled=True)  39.7 us
    all_to_all x1, waiting for transfers between devices, body(): lax.all_to_all(pieces_out, 'grp', split_axis=0, concat_axis=0, tiled=True)  25.1 us
  transfers between devices with their start and end apart: 4, of which 1 were waited for; matrix products, arithmetic and copies ran while one was open for 6% of the time, Pallas kernels for 42%

profile of v2, /device:TPU:22, one launch (start us, length us, event | category | flops | bytes accessed | tf_op | source)
XLA Modules:
  0.0 1114.3 jit_solution(13095022596433340117)
XLA Ops:
  9.9 39.7 %all_to_all.17 = bf16[8,384,256]{2,1,0:T(8,128)(2,1)S(1)} all-to-all(bf16[8,384,256]{2,1,0:T(8,128)(2,1)S(1)} %maximum_bitcast_fusion), channel_id=1, replica_groups=mesh['grp'=8,'exp'=4] {'grp'}, dimensions={0} | all-to-all | bytes 3145728 | tf_op jit(solution)/shard_map/all_to_all | solution.py:1140
  54.6 102.4 %shard_map.196 = bf16[32,128,2176]{2,1,0:T(8,128)(2,1)} custom-call(bf16[128,2176]{1,0:T(8,128)(2,1)} %fusion.17.src), custom_call_target="tpu_custom_call" | custom-call | tf_op jit(solution)/shard_map/pallas_call | solution.py:734
  158.8 3.4 mul.230
  176.6 7.5 fusion.16
  190.0 3.1 pad_add_fusion.meta
  196.0 2.7 reshape.303
  198.7 3.2 fusion.1.w_all
  202.6 144.1 %shard_map.197 = (bf16[4096,768]{1,0:T(8,128)(2,1)}, bf16[4096,256]{1,0:T(8,128)(2,1)}, f32[4096,128]{1,0:T(8,128)}, f32[128,2048]{1,0:T(8,128)}) custom-call(s32[1]{0:T(128)} %bitcast.me, bf16[4096,2176]{1,0:T(8,128)(2,1)} %bitcast.98, f32[1,2048]{1,0:T(1,128)} %bitcast.131, bf16[2048,896]{1,0:T(8,128)(2,1)} %fusion.1.w_all, ...), custom_call_target="tpu_custom_call" | custom-call | tf_op jit(solution)/shard_map/pallas_call | solution.py:247
  350.1 73.9 %shard_map.198 = bf16[32,128,2048]{2,1,0:T(8,128)(2,1)} custom-call(bf16[128,2048]{1,0:T(8,128)(2,1)} %multiply_convert_fusion.src), custom_call_target="tpu_custom_call" | custom-call | tf_op jit(solution)/shard_map/pallas_call | solution.py:734
  424.1 195.0 %shard_map.199 = (bf16[4096,2048]{1,0:T(8,128)(2,1)}, f32[4096,128]{1,0:T(8,128)}, bf16[3072,704]{1,0:T(8,128)(2,1)}, bf16[3072,704]{1,0:T(8,128)(2,1)}, bf16[3072,704]{1,0:T(8,128)(2,1)}, /*index=5*/f32[128,2176]{1,0:T(8,128)}) custom-call(s32[1]{0:T(128)} %bitcast.me, bf16[4096,2048]{1,0:T(8,128)(2,1)} %bitcast.100, ...), custom_call_target="tpu_custom_call" | custom-call | tf_op jit(solution)/shard_map/pallas_call | solution.py:468
  620.3 2.6 multiply_reduce_fusion
  625.0 72.4 %shard_map.200 = bf16[32,128,2048]{2,1,0:T(8,128)(2,1)} custom-call(bf16[128,2048]{1,0:T(8,128)(2,1)} %fusion.53.src), custom_call_target="tpu_custom_call" | custom-call | tf_op jit(solution)/shard_map/pallas_call | solution.py:734
  697.4 176.0 %shard_map.201 = (f32[768,2048]{1,0:T(8,128)}, f32[256,2048]{1,0:T(8,128)}, f32[128,2176]{1,0:T(8,128)}) custom-call(bf16[4096,2048]{1,0:T(8,128)(2,1)} %bitcast.102, bf16[4096,2176]{1,0:T(8,128)(2,1)} %bitcast.99, f32[1,2048]{1,0:T(1,128)} %bitcast.132, bf16[4096,768]{1,0:T(8,128)(2,1)} %get-tuple-element.30.qkv, bf16[4096,256]{1,0:T(8,128)(2,1)} %get-tuple-element.31.att, ...), custom_call_target="tpu_custom_call" | custom-call | tf_op jit(solution)/shard_map/pallas_call | solution.py:309
  873.4 3.3 convert.42
  878.5 2.5 copy.130
  883.7 3.1 fusion.11
  890.4 142.9 %shard_map.202 = (f32[704,2,2048]{2,1,0:T(2,128)}, f32[704,2048]{1,0:T(8,128)}, f32[128,2176]{1,0:T(8,128)}) custom-call(bf16[4096,2048]{1,0:T(8,128)(2,1)} %bitcast.101, bf16[4096,2048]{1,0:T(8,128)(2,1)} %all-gather.4.cloned.1.call-done.top, f32[4096,128]{1,0:T(8,128)} %get-tuple-element.29.aux, s32[8,4,128]{2,1,0:T(4,128)} %fusion.43.posrow, ...), custom_call_target="tpu_custom_call" | custom-call | tf_op jit(solution)/shard_map/pallas_call | solution.py:590
  1041.5 5.7 all-to-all-start.1
  1050.1 3.2 fusion.14
  1053.3 25.1 %all-to-all-done.1 = bf16[8,2,49152]{2,1,0:T(2,128)(2,1)} async-done(((bf16[8,2,49152]{2,1,0:T(2,128)(2,1)}), bf16[8,2,49152]{2,1,0:T(2,128)(2,1)}, u32[]{:S(2)}, u32[]{:S(2)}) %all-to-all-start.1) | async-done | bytes 1572896 | tf_op jit(solution)/shard_map/all_to_all | solution.py:1260
  1078.4 4.7 reshape.329
  1086.6 2.9 copy.137
  1094.2 10.6 copy.163
  1104.7 2.5 copy.164
  (169 shorter events, 66.8 us)
Async XLA Ops:
  7.2 188.8 %all-gather.6.cloned.1.call-start = ((), (), s32[]{:S(2)}) async-start(), calls=%async_computation.3 | async-start | bytes 2621440 | tf_op jit(solution)/shard_map/all_gather | solution.py:1142
  9.9 42.6 %copy-start.24 = (s32[1,2]{1,0:T(1,128)S(1)}, s32[1,2]{1,0:T(1,128)}, u32[]{:S(2)}) copy-start(s32[1,2]{1,0:T(1,128)} %param.15) | copy-start | bytes 28
  9.9 42.7 %copy-start.25 = (f32[64,2]{0,1:T(2,128)S(1)}, f32[64,2]{0,1:T(2,128)}, u32[]{:S(2)}) copy-start(f32[64,2]{0,1:T(2,128)} %param.19) | copy-start | bytes 1540
  9.9 42.8 %copy-start.23 = (f32[64,8]{0,1:T(8,128)S(1)}, f32[64,8]{0,1:T(8,128)}, u32[]{:S(2)}) copy-start(f32[64,8]{0,1:T(8,128)} %param.21) | copy-start | bytes 6148
  9.9 42.8 %copy-start.26 = (s32[1,8]{1,0:T(1,128)S(1)}, s32[1,8]{1,0:T(1,128)}, u32[]{:S(2)}) copy-start(s32[1,8]{1,0:T(1,128)} %param.16) | copy-start | bytes 100
  9.9 43.8 %copy-start.9 = (bf16[128,2048]{1,0:T(8,128)(2,1)S(1)}, bf16[128,2048]{1,0:T(8,128)(2,1)}, u32[]{:S(2)}) copy-start(bf16[128,2048]{1,0:T(8,128)(2,1)} %param.13) | copy-start | bytes 1572868
  51.6 372.5 %all-gather.4.cloned.1.call-start = ((), (), s32[]{:S(2)}) async-start(), calls=%async_computation.2 | async-start | bytes 17301504 | tf_op jit(solution)/shard_map/all_gather | solution.py:1181
  52.4 980.9 %all-reduce.10.cloned.1.call-start = ((), (), s32[]{:S(2)}) async-start(), calls=%async_computation.4 | async-start | bytes 4194304
  170.7 3.1 copy-start.27
  186.1 3.0 copy-start.7
  186.1 3.6 copy-start.8
  190.0 3.2 copy-start.20
  202.6 144.1 %copy-start.10 = (bf16[128,2048]{1,0:T(8,128)(2,1)S(1)}, bf16[128,2048]{1,0:T(8,128)(2,1)}, u32[]{:S(2)}) copy-start(bf16[128,2048]{1,0:T(8,128)(2,1)} %param.13) | copy-start | bytes 1572868
  619.1 4.8 copy-start.1
  619.1 4.8 copy-start.15
  881.0 2.7 copy-start.22
  1033.3 3.2 copy-start.17
  1041.5 8.6 copy-start.2
  1041.5 8.6 copy-start.5
  1041.5 8.6 copy-start.12
  1041.5 8.6 copy-start.16
  1041.5 36.9 %all-to-all-start.1 = ((bf16[8,2,49152]{2,1,0:T(2,128)(2,1)}), bf16[8,2,49152]{2,1,0:T(2,128)(2,1)}, u32[]{:S(2)}, u32[]{:S(2)}) async-start(bf16[8,2,49152]{2,1,0:T(2,128)(2,1)} %reshape.328), calls=%async_computation.1 | async-start | bytes 3145728 | tf_op jit(solution)/shard_map/all_to_all | solution.py:1260
  1092.8 11.9 %slice-start.1 = ((s8[5767168]{0:T(1024)(128)(4,1)}), s8[4194304]{0:T(1024)(128)(4,1)S(1)}, s32[]{:S(2)}) async-start(s8[5767168]{0:T(1024)(128)(4,1)} %bitcast.117), calls=%async_computation.6 | async-start | bytes 8388608
  1094.2 10.6 slice-start.2
  (11 other events, 18.0 us)
Sparse Core Ops, SparseCore 0:
  51.7 35.1 all-gather.5
  89.8 129.0 all-gather.3
  881.1 76.4 all-reduce.9

commit v3 on v2

--- a/solution.py
+++ b/solution.py
@@ -215,10 +215,17 @@
     return pl.BlockSpec(shape, lambda i: (0,) * len(shape), pipeline_mode=pl.Buffered(1))
 
 
-def attn_forward_fused(dims, cw, scale, me, tokens, gain, w_all, ow, cos, sin, meta, krow, qkv, att, aux, out, h1, inv, *refs):
+def attn_forward_plain(cw, scale, me, tokens, gain, w_all, ow, cos, sin, meta, krow, gate_up, down, qkv, att, aux, wg, wu, wd, part, h1, inv, *more):
+    i = pl.program_id(0)
+    Masters(gate_up, down, wg, wu, wd, *more).step(i, 1, 4)
+    attn_forward_kernel(cw, scale, me, tokens, gain, w_all, ow, cos, sin, meta, krow, qkv, att, aux, part, h1, inv)
+
+
+def attn_forward_fused(dims, cw, scale, me, tokens, gain, w_all, ow, cos, sin, meta, krow, gate_up, down, qkv, att, aux, wg, wu, wd, out, h1, inv, stage, low, sems, out_sems, *refs):
     i = pl.program_id(0)
     place = Place(dims)
     sums = Scatter(dims, place, out, refs)
+    Masters(gate_up, down, wg, wu, wd, stage, low, sems, out_sems).step(i, sums.tiles, 5)
     pl.when(i == 0)(place.greet)
 
     @pl.when(i < sums.tiles)
@@ -229,12 +236,13 @@
     sums.run(i)
 
 
-def attn_forward(dims, cid, me, tokens, gain, w_all, ow, cos, sin, meta, krow, groups, scale):
+def attn_forward(dims, cid, me, tokens, gain, w_all, ow, cos, sin, meta, krow, gate_up, down, groups, scale):
     total = tokens.shape[0]
     cw, width = ow.shape
     count = total // groups
     at = (lambda i: tile_group(i, dims)) if dims else (lambda i: i)
     row = lambda w: pl.BlockSpec((count, w), lambda i: (at(i), 0))
+    hbm = pl.BlockSpec(memory_space=pl.ANY)
     shape = lambda w, t: jax.ShapeDtypeStruct((total, w), t)
     if dims:
         own = count // 4
@@ -242,7 +250,7 @@
         last_spec, last_shape = whole_block((own, width)), jax.ShapeDtypeStruct((own, width), f32)
         params, more = dict(collective_id=cid, has_side_effects=True), scatter_scratch(dims, own, width)
     else:
-        kernel = functools.partial(attn_forward_kernel, cw, scale)
+        kernel = functools.partial(attn_forward_plain, cw, scale)
         last_spec, last_shape, params, more = row(width), shape(width, bf16), {}, []
     return pl.pallas_call(
         kernel,
@@ -250,13 +258,13 @@
         in_specs=[
             pl.BlockSpec(memory_space=pltpu.SMEM), row(width), whole_block(gain.shape),
             once(w_all.shape), once(ow.shape), row(LANES), row(LANES), row(8),
-            pl.BlockSpec((1, 8, count), lambda i: (at(i), 0, 0)),
+            pl.BlockSpec((1, 8, count), lambda i: (at(i), 0, 0)), hbm, hbm,
         ],
-        out_specs=[row(3 * cw), row(cw), row(LANES), last_spec],
-        out_shape=[shape(3 * cw, bf16), shape(cw, bf16), shape(LANES, f32), last_shape],
-        scratch_shapes=[pltpu.VMEM((count, width), bf16), pltpu.VMEM((count, LANES), f32)] + more,
+        out_specs=[row(3 * cw), row(cw), row(LANES), hbm, hbm, hbm, last_spec],
+        out_shape=[shape(3 * cw, bf16), shape(cw, bf16), shape(LANES, f32)] + [jax.ShapeDtypeStruct(down.shape, bf16)] * 3 + [last_shape],
+        scratch_shapes=[pltpu.VMEM((count, width), bf16), pltpu.VMEM((count, LANES), f32)] + masters_scratch(down.shape[0], width) + more,
         compiler_params=pltpu.CompilerParams(vmem_limit_bytes=60 * MB, **params),
-    )(me, tokens, gain, w_all, ow, cos, sin, meta, krow)
+    )(me, tokens, gain, w_all, ow, cos, sin, meta, krow, gate_up, down)
 
 
 def attn_backward_plain(cw, scale, dmid, tokens, gain, qkv, att, aux, cos, sin, meta, krow, w_all, ow, dw_hbm, do_hbm, dh1, side, dw, do, sems, *more):
@@ -334,16 +342,30 @@
     return (slot == posrow[0, pl.ds(i, 1), :]).astype(bf16)
 
 
+def is_dense(cap):
+    return 2 * cap > LANES
+
+
+def chosen_scratch(cap, few, width):
+    return [pltpu.VMEM((16 if is_dense(cap) else few, width), bf16), pltpu.VMEM((few, width), bf16)]
+
+
+def gated(top, weight, at, cs):
+    return (weight * top[at, cs].astype(f32)).astype(bf16)
+
+
 def compact(cap, h2, top, posrow, weight, xc, gc):
     def block(i):
         at, to = rows_at(i, LANES), rows_at(i, cap)
-        choose = chosen(posrow, i, cap)
-        w = weight(i, at)
+        w = weight(at)
+        choose = None if is_dense(cap) else chosen(posrow, i, cap)
         for start, size in pieces(h2.shape[1], 512):
             cs = slice(start, start + size)
-            xc[to, cs] = nn(choose, h2[at, cs]).astype(bf16)
-            gated = (w * top[at, cs].astype(f32)).astype(bf16)
-            gc[to, cs] = nn(choose, gated).astype(bf16)
+            if is_dense(cap):
+                gc[at, cs] = gated(top, w, at, cs)
+            else:
+                xc[to, cs] = nn(choose, h2[at, cs]).astype(bf16)
+                gc[to, cs] = nn(choose, gated(top, w, at, cs)).astype(bf16)
 
     loop(h2.shape[0] // LANES, block)
 
@@ -352,25 +374,60 @@
     return max(r for r in range(16, 177, 16) if hidden % r == 0)
 
 
-def load_masters(gate_up, down, wg, wu, wd, stage, sems):
-    hidden, part = wd.shape[0], stage.shape[1]
-    jobs = [
-        (src.at[pl.ds(n * part, part)], dst.at[pl.ds(n * part, part)])
-        for n in range(hidden // part)
-        for src, dst in ((gate_up.at[:, 0, :], wg), (gate_up.at[:, 1, :], wu), (down, wd))
-    ]
-    copies = [pltpu.make_async_copy(job[0], stage.at[n % 2], sems.at[n % 2]) for n, job in enumerate(jobs)]
-    copies[0].start()
-    for n, (_, dst) in enumerate(jobs):
-        if n + 1 < len(jobs):
-            copies[n + 1].start()
-        copies[n].wait()
-
-        def cast(r, dst=dst, n=n):
-            at = rows_at(r, 16)
-            dst[at, :] = stage[n % 2, at, :].astype(bf16)
-
-        loop(part // 16, cast)
+class Masters:
+    def __init__(self, gate_up, down, wg, wu, wd, stage, low, sems, out_sems):
+        part = stage.shape[1]
+        self.jobs = [
+            (src.at[pl.ds(n * part, part)], dst.at[pl.ds(n * part, part)])
+            for n in range(down.shape[0] // part)
+            for src, dst in ((gate_up.at[:, 0, :], wg), (gate_up.at[:, 1, :], wu), (down, wd))
+        ]
+        self.stage, self.low, self.sems, self.out_sems = stage, low, sems, out_sems
+
+    def load(self, n):
+        return pltpu.make_async_copy(self.jobs[n][0], self.stage.at[n % 2], self.sems.at[n % 2])
+
+    def store(self, n):
+        return pltpu.make_async_copy(self.low.at[n % 2], self.jobs[n][1], self.out_sems.at[n % 2])
+
+    def run(self, first, last):
+        for n in range(first, last):
+            self.load(n).wait()
+            if n >= 2:
+                self.store(n - 2).wait()
+
+            def cast(r, n=n):
+                at = rows_at(r, 16)
+                self.low[n % 2, at, :] = self.stage[n % 2, at, :].astype(bf16)
+
+            loop(self.low.shape[1] // 16, cast)
+            self.store(n).start()
+            if n + 2 < len(self.jobs):
+                self.load(n + 2).start()
+
+    def finish(self):
+        for n in range(max(len(self.jobs) - 2, 0), len(self.jobs)):
+            self.store(n).wait()
+
+    def step(self, i, first_step, steps):
+        count = len(self.jobs)
+
+        @pl.when(i == first_step - 1)
+        def _():
+            for n in range(min(2, count)):
+                self.load(n).start()
+
+        for k in range(steps):
+            pl.when(i == first_step + k)(
+                lambda k=k: self.run(count * k // steps, count * (k + 1) // steps)
+            )
+        pl.when(i == first_step + steps - 1)(self.finish)
+
+
+def masters_scratch(hidden, width):
+    part = stage_rows(hidden)
+    D = pltpu.SemaphoreType.DMA
+    return [pltpu.VMEM((2, part, width), f32), pltpu.VMEM((2, part, width), bf16), D((2,)), D((2,))]
 
 
 def ffn_compute(cap, me, h2, top, router, meta, posrow, produced, dh2, side, aux, act, dgate, dup, wg, wu, wd, xc, gc):
@@ -378,21 +435,29 @@
     hidden = wd.shape[0]
     blocks = rows // LANES
 
-    def weight(i, at):
-        found = gate_columns(nn(h2[at, :], router[...]), meta[at, 4:5], meta[at, 5:6], me[0])
-        aux[at, :] = found
-        return found[:, 0:1]
-
-    compact(cap, h2, top, posrow, weight, xc, gc)
+    aux[...] = gate_columns(nn(h2[...], router[...]), meta[:, 4:5], meta[:, 5:6], me[0])
+    compact(cap, h2, top, posrow, lambda at: aux[at, 0:1], xc, gc)
+    xs = h2 if is_dense(cap) else xc
 
     for start, size in pieces(hidden, 256):
         fs = slice(start, start + size)
-        gate, up, dact = nt(xc[...], wg[fs, :]), nt(xc[...], wu[fs, :]), nt(gc[...], wd[fs, :])
+        gate, up, dact = nt(xs[...], wg[fs, :]), nt(xs[...], wu[fs, :]), nt(gc[...], wd[fs, :])
         sigmoid = 1.0 / (1.0 + jnp.exp(-gate))
         silu = gate * sigmoid
         act[:, fs] = (silu * up).astype(bf16)
         dgate[:, fs] = (dact * up * sigmoid * (1.0 + gate * (1.0 - sigmoid))).astype(bf16)
         dup[:, fs] = (dact * silu).astype(bf16)
+
+    if is_dense(cap):
+        shares = jnp.zeros((rows, 1), f32)
+        for start, size in pieces(width, 512):
+            cs = slice(start, start + size)
+            y = nn(act[...], wd[:, cs])
+            shares = shares + jnp.sum(y * top[:, cs].astype(f32), axis=1, keepdims=True)
+            produced[:, cs] = (aux[:, 0:1] * y).astype(bf16)
+            dh2[:, cs] = (nn(dgate[...], wg[:, cs]) + nn(dup[...], wu[:, cs])).astype(bf16)
+        side[...] = jnp.broadcast_to(aux[:, 1:2] * shares, (rows, LANES)).astype(bf16)
+        return
 
     yc, bc = gc, xc
 
@@ -419,20 +484,16 @@
     loop(blocks, scatter)
 
 
-def ffn_kernel(cap, me, h2, top, router, meta, posrow, gate_up, down, produced, aux, act, dgate, dup, dh2, side, wg, wu, wd, xc, gc, stage, sems):
-    pl.when(pl.program_id(0) == 0)(lambda: load_masters(gate_up, down, wg, wu, wd, stage, sems))
+def ffn_kernel(cap, me, h2, top, router, meta, posrow, wg, wu, wd, produced, aux, act, dgate, dup, dh2, side, xc, gc):
     ffn_compute(cap, me, h2, top, router, meta, posrow, produced, dh2, side, aux, act, dgate, dup, wg, wu, wd, xc, gc)
 
 
-def ffn_fused_kernel(dims, cap, me, h2, top, router, meta, posrow, gate_up, down, produced, aux, act, dgate, dup, out, wg, wu, wd, xc, gc, stage, sems, *refs):
+def ffn_fused_kernel(dims, cap, me, h2, top, router, meta, posrow, wg, wu, wd, produced, aux, act, dgate, dup, out, xc, gc, *refs):
     i = pl.program_id(0)
     place = Place(dims)
     sums = Scatter(dims, place, out, refs)
 
-    @pl.when(i == 0)
-    def _():
-        place.greet()
-        load_masters(gate_up, down, wg, wu, wd, stage, sems)
+    pl.when(i == 0)(place.greet)
 
     @pl.when(i < sums.tiles)
     def _():
@@ -443,17 +504,15 @@
     sums.run(i)
 
 
-def ffn(dims, cid, me, h2, top, router, meta, posrow, gate_up, down, cap):
+def ffn(dims, cid, me, h2, top, router, meta, posrow, wg, wu, wd, cap):
     total, width = h2.shape
-    hidden = down.shape[0]
+    hidden = wd.shape[0]
     tile = posrow.shape[1] * LANES
-    few = tile // LANES * cap
+    few = tile if is_dense(cap) else tile // LANES * cap
     tiles = total // tile
     at = (lambda i: tile_group(i, dims)) if dims else (lambda i: i)
     row = lambda w: pl.BlockSpec((tile, w), lambda i: (at(i), 0))
     some = pl.BlockSpec((few, hidden), lambda i: (at(i), 0))
-    hbm = pl.BlockSpec(memory_space=pl.ANY)
-    V = pltpu.VMEM
     own = total // (dims[0] * dims[1] * dims[2] * 2) if dims else 0
     wide = width + LANES
     if dims:
@@ -470,18 +529,17 @@
         grid=(tiles + 2 + dims[0] if dims else tiles,),
         in_specs=[
             pl.BlockSpec(memory_space=pltpu.SMEM), row(width), row(width), whole_block(router.shape), row(8),
-            pl.BlockSpec((1,) + posrow.shape[1:], lambda i: (at(i), 0, 0)), hbm, hbm,
+            pl.BlockSpec((1,) + posrow.shape[1:], lambda i: (at(i), 0, 0)), once(wg.shape), once(wu.shape), once(wd.shape),
         ],
         out_specs=[row(width), row(LANES), some, some, some] + last_spec,
         out_shape=[
             jax.ShapeDtypeStruct((total, width), bf16),
             jax.ShapeDtypeStruct((total, LANES), f32),
         ] + [jax.ShapeDtypeStruct((tiles * few, hidden), bf16)] * 3 + last_shape,
-        scratch_shapes=[V((hidden, width), bf16)] * 3 + [V((few, width), bf16)] * 2
-        + [V((2, stage_rows(hidden), width), f32), pltpu.SemaphoreType.DMA((2,))]
+        scratch_shapes=chosen_scratch(cap, few, width)
         + (scatter_scratch(dims, own, wide) if dims else []),
         compiler_params=pltpu.CompilerParams(vmem_limit_bytes=63 * MB, **params),
-    )(me, h2, top, router, meta, posrow, gate_up, down)
+    )(me, h2, top, router, meta, posrow, wg, wu, wd)
 
 
 def ffn_weights_compute(cap, first, h2, top, aux, posrow, act, dgate, dup, sg, su, sd, xc, gc):
@@ -497,15 +555,16 @@
 
             loop(hidden // 32, clear)
 
-    compact(cap, h2, top, posrow, lambda i, at: aux[at, 0:1], xc, gc)
+    compact(cap, h2, top, posrow, lambda at: aux[at, 0:1], xc, gc)
+    xs = h2 if is_dense(cap) else xc
     for start, size in pieces(hidden, 256):
         fs = slice(start, start + size)
 
         def grads(i, fs=fs):
             at = rows_at(i, 512)
             sd[fs, at] += tn(act[:, fs], gc[:, at])
-            sg[fs, at] += tn(dgate[:, fs], xc[:, at])
-            su[fs, at] += tn(dup[:, fs], xc[:, at])
+            sg[fs, at] += tn(dgate[:, fs], xs[:, at])
+            su[fs, at] += tn(dup[:, fs], xs[:, at])
 
         loop(width // 512, grads)
 
@@ -528,13 +587,95 @@
             c.wait()
 
 
-def ffn_weights_fused(dims, cap, h2, top, aux, posrow, act, dgate, dup, extra, produced, gate_up_grad, down_grad, out, sg, su, sd, xc, gc, sems, load, *refs):
+class GradExchange:
+    def __init__(self, dims, place, q_src, kv_src, q_out, kv_out, other_out, own, landed, along, refs):
+        groups = dims[0] * dims[1]
+        qs, qr, ql, ks, kr, kl, self.ls, self.ss, self.sr = refs
+        self.place, self.kv_src, self.kv_out, self.other_out = place, kv_src, kv_out, other_out
+        self.own, self.landed, self.along = own, landed, along
+        self.query = Exchange(groups, q_src, q_out, qs, qr, ql)
+        self.kv = Exchange(groups, own.at[place.y], kv_out, ks, kr, kl)
+
+    def load(self):
+        return pltpu.make_async_copy(self.kv_src.at[self.place.c], self.own, self.ls)
+
+    def c_core(self):
+        p = self.place
+        return remote(self.kv_src.at[1 - p.c], self.landed, self.ss.at[0], self.sr.at[0], p.core())
+
+    def c_y(self):
+        p = self.place
+        return remote(self.own.at[1 - p.y], self.along, self.ss.at[1], self.sr.at[1], p.along_y())
+
+    def c_last(self):
+        return remote(self.kv_out, self.other_out, self.ss.at[2], self.sr.at[2], self.place.core())
+
+    def add(self, into, other):
+        groups, rows, _ = into.shape
+
+        def step(n):
+            at = rows_at(n % (rows // 64), 64)
+            g = n // (rows // 64)
+            into[g, at, :] = (into[g, at, :].astype(f32) + other[g, at, :].astype(f32)).astype(bf16)
+
+        loop(groups * (rows // 64), step)
+
+    def step(self, i, last):
+        @pl.when(i == 0)
+        def _():
+            self.c_core().start()
+            self.load().start()
+            self.query.start()
+
+        @pl.when(i == 1)
+        def _():
+            self.load().wait()
+            self.c_core().wait_recv()
+            for n in range(2):
+                self.add(self.own.at[n], self.landed.at[n])
+            self.c_y().start()
+
+        @pl.when(i == 3)
+        def _():
+            self.c_y().wait_recv()
+            self.add(self.own.at[self.place.y], self.along)
+            self.kv.start()
+
+        @pl.when(i == 7)
+        def _():
+            self.kv.wait_came()
+            self.c_last().start()
+
+        @pl.when(i == last)
+        def _():
+            self.query.wait_came()
+            self.c_last().wait_recv()
+            for c in (self.c_core(), self.c_y(), self.c_last()):
+                c.wait_send()
+            self.query.wait_sent()
+            self.kv.wait_sent()
+
+
+def grad_exchange_scratch(groups, cw):
+    D = pltpu.SemaphoreType.DMA
+    V = lambda *s: pltpu.VMEM(s + (groups, cw, LANES), bf16)
+    return [V(2), V(2), V()], exchange_scratch(groups) * 2 + [D, D((3,)), D((3,))]
+
+
+def ffn_weights_fused(dims, cap, h2, top, aux, posrow, act, dgate, dup, extra, produced, q_src, kv_src, gate_up_grad, down_grad, out, q_out, kv_out, other_out, sg, su, sd, xc, gc, sems, load, own, landed, along, *refs):
     i = pl.program_id(0)
     place = Place(dims)
-    sums = Scatter(dims, place, out, refs)
+    sums = Scatter(dims, place, out, refs[:SCATTER_REFS])
+    grads = GradExchange(dims, place, q_src, kv_src, q_out, kv_out, other_out, own, landed, along, refs[SCATTER_REFS:])
     rows, width = h2.shape
     copies = ffn_weights_out(gate_up_grad, down_grad, sg, su, sd, sems)
-    pl.when(i == 0)(place.greet)
+
+    @pl.when(i == 0)
+    def _():
+        place.greet_plane()
+        place.greeted_plane()
+
+    grads.step(i, sums.steps - 1)
 
     @pl.when(i < sums.tiles)
     def _():
@@ -550,7 +691,6 @@
         for c in copies:
             c.start()
 
-    pl.when(i == 0)(place.greeted)
     sums.run(i)
 
     @pl.when(i == sums.steps - 1)
@@ -559,18 +699,18 @@
             c.wait()
 
 
-def ffn_weights(dims, cid, h2, top, aux, posrow, act, dgate, dup, extra, produced, cap):
+def ffn_weights(dims, cid, h2, top, aux, posrow, act, dgate, dup, extra, produced, q_src, kv_src, cap):
     total, width = h2.shape
     hidden = act.shape[1]
     tile = posrow.shape[1] * LANES
-    few = tile // LANES * cap
+    few = tile if is_dense(cap) else tile // LANES * cap
     tiles = total // tile
     at = (lambda i: tile_group(i, dims)) if dims else (lambda i: i)
     row = lambda w: pl.BlockSpec((tile, w), lambda i: (at(i), 0))
     some = pl.BlockSpec((few, hidden), lambda i: (at(i), 0))
     hbm = pl.BlockSpec(memory_space=pl.ANY)
     V = pltpu.VMEM
-    scratch = [V((hidden, width), f32)] * 3 + [V((few, width), bf16)] * 2 + [pltpu.SemaphoreType.DMA((3,))]
+    scratch = [V((hidden, width), f32)] * 3 + chosen_scratch(cap, few, width) + [pltpu.SemaphoreType.DMA((3,))]
     out_specs = [hbm, hbm]
     out_shape = [jax.ShapeDtypeStruct((hidden, 2, width), f32), jax.ShapeDtypeStruct((hidden, width), f32)]
     in_specs = [
@@ -581,9 +721,13 @@
         own = tile // 4
         kernel = functools.partial(ffn_weights_fused, dims, cap)
         wide = width + LANES
-        operands, in_specs = operands + [extra, produced], in_specs + [row(LANES), hbm]
-        out_specs, out_shape = out_specs + [once((own, wide))], out_shape + [jax.ShapeDtypeStruct((own, wide), f32)]
-        scratch = scratch + [pltpu.SemaphoreType.DMA] + scatter_scratch(dims, own, wide)
+        operands, in_specs = operands + [extra, produced, q_src, kv_src], in_specs + [row(LANES), hbm, hbm, hbm]
+        groups, cw = q_src.shape[:2]
+        out_specs = out_specs + [once((own, wide)), hbm, hbm, hbm]
+        out_shape = out_shape + [jax.ShapeDtypeStruct((own, wide), f32), jax.ShapeDtypeStruct(q_src.shape, bf16)]
+        out_shape = out_shape + [jax.ShapeDtypeStruct((groups, cw, LANES), bf16)] * 2
+        buffers, marks = grad_exchange_scratch(groups, cw)
+        scratch = scratch + [pltpu.SemaphoreType.DMA] + buffers + scatter_scratch(dims, own, wide) + marks
         params = dict(collective_id=cid, has_side_effects=True)
     else:
         kernel, params = functools.partial(ffn_weights_kernel, cap), {}
@@ -598,7 +742,51 @@
     )(*operands)
 
 
-def ag_kernel(dims, halves, src, out, local_sem, zs, zr, xs, xr, ys, yr, cs, cr):
+class Exchange:
+    def __init__(self, groups, src, dst, sent, came, local):
+        self.groups, self.src, self.dst, self.sent, self.came, self.local = groups, src, dst, sent, came, local
+        self.gi, self.ei = lax.axis_index("grp"), lax.axis_index("exp")
+
+    def peers(self):
+        return [((self.gi + r) % self.groups, self.ei) for r in range(1, self.groups)]
+
+    def copy(self, r, arriving=False):
+        to, of = (self.gi + r) % self.groups, (self.gi + self.groups - r) % self.groups
+        return pltpu.make_async_remote_copy(
+            src_ref=self.src.at[to], dst_ref=self.dst.at[of if arriving else self.gi],
+            send_sem=self.sent.at[r], recv_sem=self.came.at[r], device_id=(to, self.ei), device_id_type=MESH,
+        )
+
+    def own(self):
+        return pltpu.make_async_copy(self.src.at[self.gi], self.dst.at[self.gi], self.local)
+
+    def start(self):
+        self.own().start()
+        for r in range(1, self.groups):
+            self.copy(r).start()
+
+    def wait_came(self):
+        self.own().wait()
+        for r in range(1, self.groups):
+            self.copy(r, True).wait_recv()
+
+    def wait_sent(self):
+        for r in range(1, self.groups):
+            self.copy(r).wait_send()
+
+
+def exchange_scratch(groups):
+    D = pltpu.SemaphoreType.DMA
+    return [D((groups,)), D((groups,)), D]
+
+
+def ag_kernel(dims, halves, shared_rows, *refs):
+    if shared_rows:
+        src, ex_src, out, ex_out, shared, local_sem, zs, zr, xs, xr, ys, yr, cs, cr, exs, exr, exl, shs, shr, shl = refs
+        ex = Exchange(dims[0] * dims[1], ex_src, ex_out, exs, exr, exl)
+    else:
+        src, out, local_sem, zs, zr, xs, xr, ys, yr, cs, cr = refs
+        ex = None
     nz, nx, ny = dims
     gi = lax.axis_index("grp"); ei = lax.axis_index("exp")
     z, x = gi // nx, gi % nx
@@ -613,12 +801,17 @@
     barrier = pltpu.get_barrier_semaphore()
     def sig(d):
         pl.semaphore_signal(barrier, inc=1, device_id=d, device_id_type=MESH)
-    sig(dev(z, 1 - x, y, c)); sig(dev(z, x, 1 - y, c)); sig(dev(z, x, y, 1 - c))
-    @pl.when(z > 0)
-    def _(): sig(dev(z - 1, x, y, c))
-    @pl.when(z < nz - 1)
-    def _(): sig(dev(z + 1, x, y, c))
-    pl.semaphore_wait(barrier, 3 + (z > 0).astype(jnp.int32) + (z < nz - 1).astype(jnp.int32))
+    sig(dev(z, x, 1 - y, c))
+    sig(dev(z, x, y, 1 - c))
+    if ex is None:
+        sig(dev(z, 1 - x, y, c))
+        pl.when(z > 0)(lambda: sig(dev(z - 1, x, y, c)))
+        pl.when(z < nz - 1)(lambda: sig(dev(z + 1, x, y, c)))
+        pl.semaphore_wait(barrier, 3 + (z > 0).astype(jnp.int32) + (z < nz - 1).astype(jnp.int32))
+    else:
+        for peer in ex.peers():
+            sig(peer)
+        pl.semaphore_wait(barrier, 2 + len(ex.peers()))
     own = pltpu.make_async_copy(src, out.at[slot(z, x, y, c)], local_sem)
     own.start()
     span = 2 * nz - 1
@@ -678,6 +871,25 @@
             second(h, delta, 0)[0].start()
             core(h, delta, 0, 0)[0].start()
     have_z(0)
+    def share(n):
+        part = ex_out.at[:, pl.ds(ex_out.shape[1] - shared_rows, shared_rows)]
+        number = (1 - y if n == 2 else y) * 2 + c
+        return pltpu.make_async_remote_copy(
+            src_ref=shared.at[number] if n == 2 else part, dst_ref=shared.at[number],
+            send_sem=shs.at[n], recv_sem=shr.at[n],
+            device_id=dev(z, x, 1 - y, c) if n == 0 else dev(z, x, y, 1 - c), device_id_type=MESH,
+        )
+    def share_own():
+        part = ex_out.at[:, pl.ds(ex_out.shape[1] - shared_rows, shared_rows)]
+        return pltpu.make_async_copy(part, shared.at[y * 2 + c], shl)
+    def shared_came(n):
+        number = ((1 - y) * 2 + c, y * 2 + 1 - c, (1 - y) * 2 + 1 - c)[n]
+        return pltpu.make_async_remote_copy(
+            src_ref=shared.at[number], dst_ref=shared.at[number], send_sem=shs.at[n], recv_sem=shr.at[n],
+            device_id=dev(z, x, y, 1 - c), device_id_type=MESH,
+        )
+    if ex is not None:
+        ex.start()
     def get_z(delta):
         def f():
             for h in hs:
@@ -709,7 +921,22 @@
                     if fn is not get_z: fn(0)
                 else:
                     fn(-dist); fn(dist)
+        if ex is not None and step == nz - 1:
+            ex.wait_came()
+            share_own().start()
+            share(0).start()
+            share(1).start()
+        if ex is not None and step == nz + 1:
+            shared_came(0).wait_recv()
+            share(2).start()
     own.wait()
+    if ex is not None:
+        shared_came(1).wait_recv()
+        shared_came(2).wait_recv()
+        share_own().wait()
+        for n in range(3):
+            share(n).wait_send()
+        ex.wait_sent()
     for delta in range(-(nz - 1), nz):
         def f(delta=delta):
             for h in hs:
@@ -726,19 +953,27 @@
                     when(z > 0, lambda h=h: zcopy(h, delta, -1, False).wait_send())
         when(valid(delta), f)
 
-def gather_kernel(v, dims, cid, halves=2):
+def gather_kernel(v, dims, cid, exchanged=None, shared_rows=0, halves=2):
     nz, nx, ny = dims
     n = nz * nx * ny * 2
     span = 2 * nz - 1
     D = pltpu.SemaphoreType.DMA
-    return pl.pallas_call(
-        functools.partial(ag_kernel, dims, halves),
-        out_shape=jax.ShapeDtypeStruct((n,) + v.shape, v.dtype),
-        in_specs=[pl.BlockSpec(memory_space=pl.ANY)],
-        out_specs=pl.BlockSpec(memory_space=pl.ANY),
-        scratch_shapes=[D] + [D((halves * 2 * (nz + 1),))] * 2 + [D((halves * 2 * span,))] * 4 + [D((halves * 4 * span,))] * 2,
+    hbm = pl.BlockSpec(memory_space=pl.ANY)
+    operands, out_shape, more = [v], [jax.ShapeDtypeStruct((n,) + v.shape, v.dtype)], []
+    if shared_rows:
+        e = exchanged
+        operands += [e]
+        out_shape += [jax.ShapeDtypeStruct(e.shape, e.dtype), jax.ShapeDtypeStruct((ny * 2, e.shape[0], shared_rows, e.shape[2]), e.dtype)]
+        more = exchange_scratch(nz * nx) + [D((3,)), D((3,)), D]
+    out = pl.pallas_call(
+        functools.partial(ag_kernel, dims, halves, shared_rows),
+        out_shape=out_shape,
+        in_specs=[hbm] * len(operands),
+        out_specs=[hbm] * len(out_shape),
+        scratch_shapes=[D] + [D((halves * 2 * (nz + 1),))] * 2 + [D((halves * 2 * span,))] * 4 + [D((halves * 4 * span,))] * 2 + more,
         compiler_params=pltpu.CompilerParams(collective_id=cid, has_side_effects=True),
-    )(v)
+    )(*operands)
+    return out if shared_rows else out[0]
 
 
 def target_order(nz):
@@ -791,6 +1026,17 @@
         pl.when(self.z > 0)(lambda: signal(self.along_z(-1)))
         pl.when(self.z < self.nz - 1)(lambda: signal(self.along_z(1)))
 
+    def greet_plane(self):
+        barrier = pltpu.get_barrier_semaphore()
+        groups = self.nz * self.nx
+        gi, ei = lax.axis_index("grp"), lax.axis_index("exp")
+        peers = [((gi + r) % groups, ei) for r in range(1, groups)] + [self.along_y(), self.core()]
+        for device in peers:
+            pl.semaphore_signal(barrier, inc=1, device_id=device, device_id_type=MESH)
+
+    def greeted_plane(self):
+        pl.semaphore_wait(pltpu.get_barrier_semaphore(), self.nz * self.nx + 1)
+
     def greeted(self):
         inner = (self.z > 0).astype(jnp.int32) + (self.z < self.nz - 1).astype(jnp.int32)
         pl.semaphore_wait(pltpu.get_barrier_semaphore(), 3 + inner)
@@ -808,13 +1054,13 @@
     D, V = pltpu.SemaphoreType.DMA, lambda *s: pltpu.VMEM(s, bf16)
     return [
         V(2, 4 * rows, width),
-        V(4, 2, rows, width),
+        V(2, 2, rows, width),
         V(tiles, 2, rows, width),
         V(tiles, half, width), V(nz, 2, half, width),
         V(nz, half, width), V(nz, half, width),
         V(nz + 1, rows, width),
         D((tiles * 2,)), D((tiles * 2,)), D((tiles,)), D((tiles,)), D((nz * 2,)), D((nz * 2,)),
-        D((nz,)), D((nz,)), D((nz,)), D((nz,)), D((nz,)), D((nz + 1,)),
+        D((nz,)), D((nz,)), D((nz,)), D((nz,)), D((nz * 2,)), D((nz * 2 + 2,)),
     ]
 
 
@@ -855,7 +1101,7 @@
 
     def c_core(self, k, q):
         p, s = self.place, k * 2 + q
-        return remote(self.shard(k, q, 1 - p.c), self.crv.at[k % 4, q], self.cs.at[s], self.cr.at[s], p.core())
+        return remote(self.shard(k, q, 1 - p.c), self.crv.at[k % 2, q], self.cs.at[s], self.cr.at[s], p.core())
 
     def c_ya(self, k):
         p = self.place
@@ -874,13 +1120,19 @@
         p, j = self.place, k // 2
         return remote(self.high(k, 1 - p.y), self.yb.at[j], self.ybs.at[j], self.ybr.at[j], p.along_y())
 
-    def c_z(self, k, way):
+    def own_half(self, k, h):
+        return self.acc.at[k, self.place.y, pl.ds(h * self.half, self.half)]
+
+    def z_half(self, slot, h):
+        return self.zv.at[slot, pl.ds(h * self.half, self.half)]
+
+    def c_z(self, k, way, h):
         p, t = self.place, self.order[k // 2]
         slot = t if way > 0 else jnp.where(p.z - 1 == t, self.dims[0], t)
-        return remote(self.acc.at[k, p.y], self.zv.at[slot], self.zs.at[t], self.zr.at[slot], p.along_z(way))
-
-    def z_wait(self, k, slot):
-        remote(self.acc.at[k, self.place.y], self.zv.at[slot], self.zs.at[0], self.zr.at[slot], self.place.core()).wait_recv()
+        return remote(self.own_half(k, h), self.z_half(slot, h), self.zs.at[t * 2 + h], self.zr.at[slot * 2 + h], p.along_z(way))
+
+    def z_wait(self, k, slot, h):
+        remote(self.own_half(k, h), self.z_half(slot, h), self.zs.at[h], self.zr.at[slot * 2 + h], self.place.core()).wait_recv()
 
     def phase_s(self, k):
         for q in range(2):
@@ -888,16 +1140,13 @@
 
     def phase_b(self, k):
         p = self.place
-        for q in range(2):
+        away = p.x != k % 2
+        for q in (1 - p.y, p.y):
             self.c_core(k, q).wait_recv()
-            self.add(self.acc.at[k, q], self.shard(k, q, p.c), self.crv.at[k % 4, q])
-        self.c_ya(k).start()
-
-        def give():
-            for q in range(2):
-                self.c_xb(k, q).start()
-
-        pl.when(p.x != k % 2)(give)
+            self.add(self.acc.at[k, q], self.shard(k, q, p.c), self.crv.at[k % 2, q])
+            if q is not p.y:
+                self.c_ya(k).start()
+            pl.when(away)(lambda q=q: self.c_xb(k, q).start())
         for q in range(2):
             self.c_core(k, q).wait_send()
 
@@ -920,46 +1169,51 @@
     def phase_d(self, k):
         p, j, t, nz = self.place, k // 2, self.order[k // 2], self.dims[0]
 
+        def ends(h):
+            if t > 0:
+                pl.when(p.z == 0)(lambda: self.c_z(k, 1, h).start())
+            if t < nz - 1:
+                pl.when(p.z == nz - 1)(lambda: self.c_z(k, -1, h).start())
+
         def keep():
             self.c_ya(k).wait_recv()
             self.c_xa(k).wait_recv()
             self.add(self.low(k, p.y), self.low(k, p.y), self.ya.at[k], self.xa.at[j])
+            ends(0)
             self.c_xb(k, p.y).wait_recv()
             self.c_yb(k).wait_recv()
             self.add(self.high(k, p.y), self.high(k, p.y), self.xb.at[j, p.y], self.yb.at[j])
-            if t > 0:
-                pl.when(p.z == 0)(lambda: self.c_z(k, 1).start())
-            if t < nz - 1:
-                pl.when(p.z == nz - 1)(lambda: self.c_z(k, -1).start())
+            ends(1)
 
         pl.when(p.x == k % 2)(keep)
 
-    def phase_e(self, k, h):
+    def phase_e(self, k, hop):
         p, t, nz = self.place, self.order[k // 2], self.dims[0]
         mine = p.x == k % 2
-        acc = self.acc.at[k, p.y]
 
         def pass_on(way):
             def run():
-                self.z_wait(k, t)
-                self.add(acc, acc, self.zv.at[t])
-                self.c_z(k, way).start()
+                for h in range(2):
+                    self.z_wait(k, t, h)
+                    self.add(self.own_half(k, h), self.own_half(k, h), self.z_half(t, h))
+                    self.c_z(k, way, h).start()
 
             return run
 
-        if h < t:
-            pl.when(mine & (p.z == h))(pass_on(1))
-        if nz - 1 - h > t:
-            pl.when(mine & (p.z == nz - 1 - h))(pass_on(-1))
-        if h == max(t, nz - 1 - t):
+        if hop < t:
+            pl.when(mine & (p.z == hop))(pass_on(1))
+        if nz - 1 - hop > t:
+            pl.when(mine & (p.z == nz - 1 - hop))(pass_on(-1))
+        if hop == max(t, nz - 1 - t):
 
             def last():
-                others = [acc]
-                for there, slot in ((t > 0, t), (t < nz - 1, nz)):
-                    if there:
-                        self.z_wait(k, slot)
-                        others.append(self.zv.at[slot])
-                self.add(self.out, *others)
+                for h in range(2):
+                    others = [self.own_half(k, h)]
+                    for there, slot in ((t > 0, t), (t < nz - 1, nz)):
+                        if there:
+                            self.z_wait(k, slot, h)
+                            others.append(self.z_half(slot, h))
+                    self.add(self.out.at[pl.ds(h * self.half, self.half)], *others)
 
             pl.when(mine & (p.z == t))(last)
 
@@ -975,7 +1229,12 @@
 
             def keep(k=k):
                 self.c_yb(k).wait_send()
-                pl.when(p.z != self.order[k // 2])(lambda: self.c_z(k, 1).wait_send())
+
+                def along(k=k):
+                    for h in range(2):
+                        self.c_z(k, 1, h).wait_send()
+
+                pl.when(p.z != self.order[k // 2])(along)
 
             pl.when(p.x != k % 2)(give)
             pl.when(p.x == k % 2)(keep)
@@ -984,7 +1243,7 @@
         for step in range(self.steps):
 
             def phases(step=step):
-                for lag, phase in enumerate([self.phase_s, self.phase_b, self.phase_c, self.phase_d]):
+                for lag, phase in ((1, self.phase_b), (0, self.phase_s), (2, self.phase_c), (3, self.phase_d)):
                     if 0 <= step - lag < self.tiles:
                         phase(step - lag)
                 for h in range(1, self.dims[0]):
@@ -1124,23 +1383,26 @@
     )
     at_route = 2 + 2 * experts
     small = jnp.pad(small, ((0, 0), (0, LANES - small.shape[1])))
+
+    query_low = query_master[0].astype(bf16)
+    kv_low = kv_master.astype(bf16).reshape(depth * 2, groups, cw)
+    query_rows = query_low.shape[0]
+    pieces_out = jnp.concatenate([query_low.reshape(query_rows, groups, cw), kv_low], axis=0).transpose(1, 0, 2)
     if dims is None:
         tokens = gather_all(layer_input, 1).reshape(total, width)
         extra = gather_all(small, 2).reshape(total, LANES)
+        pieces_in = lax.all_to_all(pieces_out, "grp", split_axis=0, concat_axis=0, tiled=True)
+        kv_all = lax.all_gather(pieces_in[:, query_rows:], "exp", axis=1, tiled=False)
     else:
         sent = jnp.concatenate([layer_input, small], axis=1)
-        tokens = gather_all(sent, 1).reshape(total, width + LANES)
+        tokens, pieces_in, kv_all = gather_kernel(sent, dims, 1, pieces_out, 2 * depth)
+        tokens = tokens.reshape(total, width + LANES)
+        tokens, late_grad = lax.optimization_barrier((tokens, out_grad))
         extra = tokens[:, width:]
-
-    query_low = query_master[0].astype(bf16)
-    kv_low = kv_master.astype(bf16).reshape(depth * 2, groups, cw)
-    pieces_out = jnp.concatenate(
-        [query_low.reshape(query_low.shape[0], groups, cw), kv_low], axis=0
-    ).transpose(1, 0, 2)
-    pieces_in = lax.all_to_all(pieces_out, "grp", split_axis=0, concat_axis=0, tiled=True)
-    query_weight = pieces_in[:, : query_low.shape[0]].reshape(width, cw)
-    kv_all = lax.all_gather(pieces_in[:, query_low.shape[0] :], "exp", axis=1, tiled=False)
+        kv_all = kv_all.transpose(1, 0, 2, 3)
+    query_weight = pieces_in[:, :query_rows].reshape(width, cw)
     kv_weight = kv_all.reshape(width, 2 * cw)
+
     output_weight = output_master[0].astype(bf16)
 
     tables = extra.reshape(devices, own_rows, LANES)[:, :depth, :at_route].reshape(width, at_route)
@@ -1165,8 +1427,9 @@
     gain_one, gain_two = gains[:, 0], gains[:, 1]
     w_all = jnp.concatenate([query_weight, kv_weight, wide(router[:, :experts])], axis=1)
 
-    qkv, att, aux, attn_sum = attn_forward(
-        dims, 3, me, tokens, gain_one[None], w_all, output_weight, cos, sin, meta, key_rows, groups, scale
+    qkv, att, aux, wg, wu, wd, attn_sum = attn_forward(
+        dims, 3, me, tokens, gain_one[None], w_all, output_weight, cos, sin, meta, key_rows,
+        gate_up_master[0], down_master[0], groups, scale,
     )
     own = (group * members + member) * own_rows
     attn_gates = lax.dynamic_slice(aux, (own, 2), (own_rows, 2))
@@ -1176,9 +1439,9 @@
     normed_two = middle * inverse_two
     hidden_two = (normed_two * gain_two).astype(bf16)
     if dims is None:
-        out_grad, hidden_two = lax.optimization_barrier((out_grad, hidden_two))
+        late_grad, hidden_two = lax.optimization_barrier((out_grad, hidden_two))
     h2 = gather_all(hidden_two, 4).reshape(total, width)
-    tops = lax.all_gather(out_grad, both, axis=0, tiled=True)
+    tops = lax.all_gather(late_grad, both, axis=0, tiled=True)
 
     named = (routes[:, 2] == member) | (routes[:, 3] == member)
     named = named.reshape(devices, own_rows)
@@ -1188,11 +1451,11 @@
     position = position.reshape(devices // tile_blocks, tile_blocks, own_rows)
     produced, ffn_aux, act, dgate, dup, *dh2_parts = ffn(
         dims, 5, me, h2, tops, wide(router[:, experts:]), meta, position,
-        gate_up_master[0], down_master[0], capacity,
+        wg, wu, wd, capacity,
     )
     if dims is None:
         gate_up_grad, down_grad = ffn_weights(
-            dims, 0, h2, tops, ffn_aux, position, act, dgate, dup, None, None, capacity
+            dims, 0, h2, tops, ffn_aux, position, act, dgate, dup, None, None, None, None, capacity
         )
         gate_up_grad, dh2_parts, produced = lax.optimization_barrier((gate_up_grad, dh2_parts, produced))
         back = summed(dh2_parts)
@@ -1237,33 +1500,39 @@
         [gain_one_grad[:, None], gain_two_grad[:, None], route_grad[0], route_grad[1]], axis=1
     )
 
-    kv_part = dw[cw:].reshape(2 * cw, groups, members, depth)
-    kv_part = lax.psum_scatter(kv_part.astype(bf16), "exp", scatter_dimension=2, tiled=False)
     if dims is None:
         sums = lax.psum_scatter(sums, both, scatter_dimension=0, tiled=True)
+        kv_part = dw[cw:].reshape(2 * cw, groups, members, depth)
+        kv_part = lax.psum_scatter(kv_part.astype(bf16), "exp", scatter_dimension=2, tiled=False)
+        query_part = dw[:cw].astype(bf16).reshape(cw, groups, width // groups)
+        pieces_out = jnp.concatenate(
+            [query_part.transpose(1, 0, 2).reshape(groups, -1), kv_part.transpose(1, 0, 2).reshape(groups, -1)],
+            axis=1,
+        )
+        pieces_in = lax.all_to_all(pieces_out, "grp", split_axis=0, concat_axis=0, tiled=True)
+        cut = cw * (width // groups)
+        query_part = pieces_in[:, :cut].reshape(width, width // groups)
+        kv_part = pieces_in[:, cut:].reshape(groups, 2, cw, depth).transpose(1, 0, 2, 3)
     else:
         beside = jnp.pad(
             sums.astype(bf16).reshape(devices, depth, sums.shape[1]),
             ((0, 0), (0, own_rows - depth), (0, LANES - sums.shape[1])),
         ).reshape(total, LANES)
-        gate_up_grad, down_grad, ffn_sum = ffn_weights(
-            dims, 7, h2, tops, ffn_aux, position, act, dgate, dup, beside, produced, capacity
+        low = dw.astype(bf16)
+        query_part = low[:cw].reshape(cw, groups, width // groups).transpose(1, 0, 2)
+        kv_part = low[cw:].reshape(2, cw, groups, members // 2, LANES).transpose(0, 3, 2, 1, 4)
+        gate_up_grad, down_grad, ffn_sum, query_part, kv_own, kv_other = ffn_weights(
+            dims, 7, h2, tops, ffn_aux, position, act, dgate, dup, beside, produced, query_part, kv_part, capacity
         )
-        kv_part, ffn_sum = lax.optimization_barrier((kv_part, ffn_sum))
         sums = ffn_sum[:depth, width : width + sums.shape[1]]
         ffn_sum = ffn_sum[:, :width]
-    query_part = dw[:cw].astype(bf16).reshape(cw, groups, width // groups)
-    pieces_out = jnp.concatenate(
-        [query_part.transpose(1, 0, 2).reshape(groups, -1), kv_part.transpose(1, 0, 2).reshape(groups, -1)],
-        axis=1,
-    )
-    pieces_in = lax.all_to_all(pieces_out, "grp", split_axis=0, concat_axis=0, tiled=True)
+        query_part = query_part.reshape(width, width // groups)
+        core = member % 2
+        kv_part = jnp.where(core == 0, jnp.stack([kv_own, kv_other]), jnp.stack([kv_other, kv_own]))
+        kv_part = lax.dynamic_slice_in_dim(kv_part, core * depth, depth, axis=3)
     final = middle + ffn_sum
-    cut = cw * (width // groups)
-    query_grad = pieces_in[:, :cut].reshape(width, width // groups).T.astype(f32)
-    kv_grad = (
-        pieces_in[:, cut:].reshape(groups, 2, cw, depth).transpose(3, 1, 0, 2).reshape(depth, 2 * width)
-    ).astype(f32)
+    query_grad = query_part.T.astype(f32)
+    kv_grad = kv_part.reshape(2 * width, depth).T.astype(f32)
     return (
         final.astype(bf16),
         input_grad,

time: 1130 us -> 1030 us (0.912)
  blocking collectives: 39.7 us -> 0 us
  waiting for transfers between devices: 25.8 us -> 0.02 us
  Pallas kernels: 907 us -> 890 us
    all_to_all x1 -> x0, blocking collectives: 39.7 us -> none  [body(): lax.all_to_all(pieces_out, 'grp', split_axis=0, concat_axis=0, tiled=True)]
    pallas_call x1, Pallas kernels: 195 us -> 165 us  [ffn(): pl.pallas_call(kernel, grid=(tiles + 2 + dims[0] if dims else tiles,), in...]
    all_to_all x1 -> x0, waiting for transfers between devices: 25.1 us -> none  [body(): lax.all_to_all(pieces_out, 'grp', split_axis=0, concat_axis=0, tiled=True)]
    pallas_call x1, Pallas kernels: 144 us -> 163 us  [attn_forward(): pl.pallas_call(kernel, grid=(groups + 2 + dims[0] if dims else groups,),...]
    unnamed x82 -> x63, local copies, waits for them, and re-layouts: 44.1 us -> 27.8 us
    pallas_call x1, Pallas kernels: 176 us -> 162 us  [attn_backward(): pl.pallas_call(kernel, grid=(groups + 2 + dims[0] if dims else groups,),...]
  transfers between devices with their start and end apart: 4 -> 1, of which waited for: 1 -> 0; matrix products, arithmetic and copies ran while one was open for 6% -> 5% of each run, Pallas kernels for 42% -> 23%
where the time goes in v3:
time: 1030 us; the launch traced here: 1020 us
  Pallas kernels  890 us (86%)
  local copies, waits for them, and re-layouts  63.6 us (6%)
  other arithmetic  46.3 us (4%)
  between operations  17.6 us (2%)
    pallas_call x3, Pallas kernels, gather_kernel(): pl.pallas_call(functools.partial(ag_kernel, dims, halves, shared_rows), o...  260 us
    pallas_call x1, Pallas kernels, ffn(): pl.pallas_call(kernel, grid=(tiles + 2 + dims[0] if dims else tiles,), in...  165 us
    pallas_call x1, Pallas kernels, attn_forward(): pl.pallas_call(kernel, grid=(groups + 2 + dims[0] if dims else groups,),...  163 us
    pallas_call x1, Pallas kernels, attn_backward(): pl.pallas_call(kernel, grid=(groups + 2 + dims[0] if dims else groups,),...  162 us
    pallas_call x1, Pallas kernels, ffn_weights(): pl.pallas_call(kernel, grid=(tiles + 2 + dims[0] if dims else tiles,), in...  139 us
    unnamed x63, local copies, waits for them, and re-layouts  27.8 us
  transfers between devices with their start and end apart: 1, of which 0 were waited for; matrix products, arithmetic and copies ran while one was open for 5% of the time, Pallas kernels for 23%

profile of v3, /device:TPU:22, one launch (start us, length us, event | category | flops | bytes accessed | tf_op | source)
XLA Modules:
  0.0 1024.8 jit_solution(14670640980400905710)
XLA Ops:
  19.1 108.6 %shard_map.196 = (bf16[32,128,2176]{2,1,0:T(8,128)(2,1)}, bf16[8,384,256]{2,1,0:T(8,128)(2,1)}, bf16[4,8,128,256]{3,2,1,0:T(8,128)(2,1)}) custom-call(bf16[128,2176]{1,0:T(8,128)(2,1)} %fusion.18.refs_0_, bf16[8,384,256]{2,1,0:T(8,128)(2,1)} %maximum_bitcast_fusion.refs_1_), custom_call_target="tpu_custom_call" | custom-call | tf_op jit(solution)/shard_map/pallas_call | solution.py:968
  129.6 3.4 mul.234
  133.4 2.3 slice.116
  146.5 3.1 copy.89
  149.6 4.1 reshape.293
  155.7 2.0 fusion.1.w_all
  157.7 7.5 fusion.17
  171.1 3.1 pad_add_fusion.meta
  176.0 163.4 %shard_map.197 = (bf16[4096,768]{1,0:T(8,128)(2,1)}, bf16[4096,256]{1,0:T(8,128)(2,1)}, f32[4096,128]{1,0:T(8,128)}, bf16[704,2048]{1,0:T(8,128)(2,1)}, bf16[704...) custom-call(s32[1]{0:T(128)} %bitcast.me, bf16[4096,2176]{1,0:T(8,128)(2,1)} %bitcast.87, ...), custom_call_target="tpu_custom_call" | custom-call | tf_op jit(solution)/shard_map/pallas_call | solution.py:255
  342.9 75.2 %shard_map.198 = bf16[32,128,2048]{2,1,0:T(8,128)(2,1)} custom-call(bf16[128,2048]{1,0:T(8,128)(2,1)} %multiply_convert_fusion.refs_0_), custom_call_target="tpu_custom_call" | custom-call | tf_op jit(solution)/shard_map/pallas_call | solution.py:968
  418.8 165.5 %shard_map.199 = (bf16[4096,2048]{1,0:T(8,128)(2,1)}, f32[4096,128]{1,0:T(8,128)}, bf16[4096,704]{1,0:T(8,128)(2,1)}, bf16[4096,704]{1,0:T(8,128)(2,1)}, bf16[4096,704]{1,0:T(8,128)(2,1)}, /*index=5*/f32[128,2176]{1,0:T(8,128)}) custom-call(s32[1]{0:T(128)} %bitcast.me, bf16[4096,2048]{1,0:T(8,128)(2,1)} %bitcast.83, ...), custom_call_target="tpu_custom_call" | custom-call | tf_op jit(solution)/shard_map/pallas_call | solution.py:527
  587.0 2.6 multiply_reduce_fusion
  591.7 75.9 %shard_map.200 = bf16[32,128,2048]{2,1,0:T(8,128)(2,1)} custom-call(bf16[128,2048]{1,0:T(8,128)(2,1)} %fusion.54.refs_0_), custom_call_target="tpu_custom_call" | custom-call | tf_op jit(solution)/shard_map/pallas_call | solution.py:968
  667.7 161.8 %shard_map.201 = (f32[768,2048]{1,0:T(8,128)}, f32[256,2048]{1,0:T(8,128)}, f32[128,2176]{1,0:T(8,128)}) custom-call(bf16[4096,2048]{1,0:T(8,128)(2,1)} %bitcast.89, bf16[4096,2176]{1,0:T(8,128)(2,1)} %bitcast.88, f32[1,2048]{1,0:T(1,128)} %bitcast.116, bf16[4096,768]{1,0:T(8,128)(2,1)} %get-tuple-element.50.qkv, bf16[4096,256]{1,0:T(8,128)(2,1)} %get-tuple-element.51.att, ...), custom_call_target="tpu_custom_call" | custom-call | tf_op jit(solution)/shard_map/pallas_call | solution.py:317
  831.1 3.1 fusion.11
  834.2 3.3 convert_element_type.135
  841.1 2.7 reshape.299
  843.8 3.5 copy.117
  849.1 139.1 %shard_map.202 = (f32[704,2,2048]{2,1,0:T(2,128)}, f32[704,2048]{1,0:T(8,128)}, f32[128,2176]{1,0:T(8,128)}, bf16[8,256,256]{2,1,0:T(8,128)(2,1)}, bf16[8,256,12...) custom-call(bf16[4096,2048]{1,0:T(8,128)(2,1)} %bitcast.84, bf16[4096,2048]{1,0:T(8,128)(2,1)} %all-gather.2.cloned.1.call-done.top, ...), custom_call_target="tpu_custom_call" | custom-call | tf_op jit(solution)/shard_map/pallas_call | solution.py:734
  991.1 2.3 fusion.16
  996.7 3.0 copy.102
  999.8 3.3 fusion.14
  1004.4 10.6 %copy.122 = f32[1,704,2,2048]{3,2,1,0:T(2,128)} copy(f32[1,704,2,2048]{3,2,1,0:T(2,128)} %bitcast.96) | data formatting | bytes 23068672
  1015.0 2.5 copy.123
  (138 shorter events, 55.4 us)
Async XLA Ops:
  7.2 411.6 %all-gather.2.cloned.1.call-start = ((), (), s32[]{:S(2)}) async-start(), calls=%async_computation | async-start | bytes 17301504 | tf_op jit(solution)/shard_map/all_gather | solution.py:1444
  14.6 2.4 copy-start.10
  153.7 1.6 copy-start.9
  153.7 1.9 copy-start.16
  153.7 2.0 copy-start.17
  167.1 1.9 copy-start.6
  167.1 3.0 copy-start.7
  167.1 3.6 copy-start.8
  171.1 3.2 copy-start.18
  176.0 163.4 %copy-start.11 = (bf16[128,2048]{1,0:T(8,128)(2,1)S(1)}, bf16[128,2048]{1,0:T(8,128)(2,1)}, u32[]{:S(2)}) copy-start(bf16[128,2048]{1,0:T(8,128)(2,1)} %param.13) | copy-start | bytes 1572868
  585.4 5.2 copy-start.1
  585.4 5.2 copy-start.14
  667.6 162.9 %copy-start.12 = (bf16[128,2048]{1,0:T(8,128)(2,1)S(1)}, bf16[128,2048]{1,0:T(8,128)(2,1)}, u32[]{:S(2)}) copy-start(bf16[128,2048]{1,0:T(8,128)(2,1)} %param.13) | copy-start | bytes 1572868
  667.6 162.9 %copy-start.21 = (f32[2048]{0:T(1024)S(1)}, f32[2048]{0:T(1024)}, u32[]{:S(2)}) copy-start(f32[2048]{0:T(1024)} %get-tuple-element.104) | copy-start | bytes 24580
  837.5 1.7 copy-start.3
  839.1 1.9 slice-start.1
  843.8 3.5 slice-start
  996.7 3.0 copy-start.2
  996.7 3.0 copy-start.5
  996.7 3.1 copy-start.13
  996.7 3.1 copy-start.15
  999.8 3.3 copy-start.19
  1003.1 11.9 %slice-start.2 = ((s8[5767168]{0:T(1024)(128)(4,1)}), s8[4194304]{0:T(1024)(128)(4,1)S(1)}, s32[]{:S(2)}) async-start(s8[5767168]{0:T(1024)(128)(4,1)} %bitcast.99), calls=%async_computation.3 | async-start | bytes 8388608
  1004.4 10.6 %slice-start.3 = ((s8[5767168]{0:T(1024)(128)(4,1)}), s8[1572864]{0:T(1024)(128)(4,1)S(1)}, s32[]{:S(2)}) async-start(s8[5767168]{0:T(1024)(128)(4,1)} %bitcast.99), calls=%async_computation.4 | async-start | bytes 3145728
  (3 other events, 3.5 us)
Sparse Core Ops, SparseCore 0:
  127.8 148.5 all-gather.1

commit v4 on v3

--- a/solution.py
+++ b/solution.py
@@ -12,6 +12,7 @@
 LANES = 128
 MESH = pl.DeviceIdType.MESH
 MB = 1024 * 1024
+UNROLL = 4
 
 epsilon = 1e-05
 negative = -1e30
@@ -76,7 +77,7 @@
 ):
     count, width = h1.shape
     heads = cw // LANES
-    step_rows = 256
+    step_rows = min(512, count)
 
     def normalise(i):
         at = rows_at(i, 64)
@@ -102,26 +103,26 @@
 
     loop(count // step_rows, project)
 
-    for h in range(heads):
-
-        def attend(i, h=h):
-            at = rows_at(i, LANES)
+    def attend(i):
+        at = rows_at(i, LANES)
+        ak = krow[0, 0:1, :]
+        allowed = (ak <= meta[at, 0:1]) & (ak >= meta[at, 1:2])
+        old = aux[at, :]
+        lane = lax.broadcasted_iota(jnp.int32, old.shape, 1)
+        for h in range(heads):
             q = qkv[at, h * LANES : (h + 1) * LANES]
             k = qkv[:, cw + h * LANES : cw + (h + 1) * LANES]
             v = qkv[:, 2 * cw + h * LANES : 2 * cw + (h + 1) * LANES]
-            ak = krow[0, 0:1, :]
-            allowed = (ak <= meta[at, 0:1]) & (ak >= meta[at, 1:2])
             scores = jnp.where(allowed, nt(q, k) * scale, negative)
             top = jnp.max(scores, axis=1, keepdims=True)
             raised = jnp.exp(scores - top)
             total = jnp.sum(raised, axis=1, keepdims=True)
             probs = (raised * (1.0 / total)).astype(bf16)
             att[at, h * LANES : (h + 1) * LANES] = nn(probs, v).astype(bf16)
-            old = aux[at, :]
-            lane = lax.broadcasted_iota(jnp.int32, old.shape, 1)
-            aux[at, :] = jnp.where(lane == 8 + h, top + jnp.log(total), old)
-
-        loop(count // LANES, attend)
+            old = jnp.where(lane == 8 + h, top + jnp.log(total), old)
+        aux[at, :] = old
+
+    lax.fori_loop(0, count // LANES, lambda i, c: (attend(i), c)[1], 0, unroll=UNROLL)
 
     def output(i):
         at = rows_at(i, step_rows)
@@ -137,7 +138,7 @@
 ):
     count, width = h1.shape
     heads = cw // LANES
-    step_rows = 256
+    step_rows = min(512, count)
 
     @pl.when(pl.program_id(0) == 0)
     def _():
@@ -168,18 +169,16 @@
 
     loop(width // 512, out_weight)
 
-    for h in range(heads):
-        hs = slice(h * LANES, (h + 1) * LANES)
-        ks = slice(cw + h * LANES, cw + (h + 1) * LANES)
-        vs = slice(2 * cw + h * LANES, 2 * cw + (h + 1) * LANES)
-        dk_sum[...] = jnp.zeros_like(dk_sum)
-        dv_sum[...] = jnp.zeros_like(dv_sum)
-
-        def back(i, h=h, hs=hs, ks=ks, vs=vs):
-            at = rows_at(i, LANES)
-            q, k, v = qkv[at, hs], qkv[:, ks], qkv[:, vs]
-            ak = krow[0, 0:1, :]
-            allowed = (ak <= meta[at, 0:1]) & (ak >= meta[at, 1:2])
+    dk_sum[...] = jnp.zeros_like(dk_sum)
+    dv_sum[...] = jnp.zeros_like(dv_sum)
+
+    def back(i):
+        at = rows_at(i, LANES)
+        ak = krow[0, 0:1, :]
+        allowed = (ak <= meta[at, 0:1]) & (ak >= meta[at, 1:2])
+        for h in range(heads):
+            hs = slice(h * LANES, (h + 1) * LANES)
+            q, k, v = qkv[at, hs], qkv[:, cw + h * LANES : cw + (h + 1) * LANES], qkv[:, 2 * cw + h * LANES : 2 * cw + (h + 1) * LANES]
             scores = jnp.where(allowed, nt(q, k) * scale, negative)
             probs = jnp.exp(scores - aux[at, 8 + h : 9 + h])
             grad = datt[at, hs]
@@ -187,12 +186,14 @@
             inner = jnp.sum(probs * dprobs, axis=1, keepdims=True)
             dscores = (probs * (dprobs - inner)).astype(bf16)
             dqkv[at, hs] = turn(nn(dscores, k) * scale, cos[at, :], -sin[at, :]).astype(bf16)
-            dk_sum[...] += tn(dscores, q)
-            dv_sum[...] += tn(probs.astype(bf16), grad)
-
-        loop(count // LANES, back)
-        dqkv[:, ks] = turn(dk_sum[...] * scale, cos[...], -sin[...]).astype(bf16)
-        dqkv[:, vs] = dv_sum[...].astype(bf16)
+            dk_sum[:, hs] += tn(dscores, q)
+            dv_sum[:, hs] += tn(probs.astype(bf16), grad)
+
+    lax.fori_loop(0, count // LANES, lambda i, c: (back(i), c)[1], 0, unroll=UNROLL)
+    for h in range(heads):
+        hs = slice(h * LANES, (h + 1) * LANES)
+        dqkv[:, cw + h * LANES : cw + (h + 1) * LANES] = turn(dk_sum[:, hs] * scale, cos[...], -sin[...]).astype(bf16)
+        dqkv[:, 2 * cw + h * LANES : 2 * cw + (h + 1) * LANES] = dv_sum[:, hs].astype(bf16)
 
     def to_hidden(i):
         at = rows_at(i, step_rows)
@@ -327,7 +328,7 @@
         scratch_shapes=[
             pltpu.VMEM((3 * cw, width), f32), pltpu.VMEM((cw, width), f32), pltpu.SemaphoreType.DMA((2,)),
             pltpu.VMEM((count, width), bf16), pltpu.VMEM((count, cw), bf16), pltpu.VMEM((count, cw), bf16), pltpu.VMEM((count, 3 * cw), bf16),
-            pltpu.VMEM((count, LANES), f32), pltpu.VMEM((count, LANES), f32),
+            pltpu.VMEM((count, cw), f32), pltpu.VMEM((count, cw), f32),
         ] + more,
         compiler_params=pltpu.CompilerParams(vmem_limit_bytes=62 * MB, **params),
     )(dmid, tokens, gain, qkv, att, aux, cos, sin, meta, krow, w_all, ow)
@@ -875,17 +876,17 @@
         part = ex_out.at[:, pl.ds(ex_out.shape[1] - shared_rows, shared_rows)]
         number = (1 - y if n == 2 else y) * 2 + c
         return pltpu.make_async_remote_copy(
-            src_ref=shared.at[number] if n == 2 else part, dst_ref=shared.at[number],
+            src_ref=shared.at[:, number] if n == 2 else part, dst_ref=shared.at[:, number],
             send_sem=shs.at[n], recv_sem=shr.at[n],
             device_id=dev(z, x, 1 - y, c) if n == 0 else dev(z, x, y, 1 - c), device_id_type=MESH,
         )
     def share_own():
         part = ex_out.at[:, pl.ds(ex_out.shape[1] - shared_rows, shared_rows)]
-        return pltpu.make_async_copy(part, shared.at[y * 2 + c], shl)
+        return pltpu.make_async_copy(part, shared.at[:, y * 2 + c], shl)
     def shared_came(n):
         number = ((1 - y) * 2 + c, y * 2 + 1 - c, (1 - y) * 2 + 1 - c)[n]
         return pltpu.make_async_remote_copy(
-            src_ref=shared.at[number], dst_ref=shared.at[number], send_sem=shs.at[n], recv_sem=shr.at[n],
+            src_ref=shared.at[:, number], dst_ref=shared.at[:, number], send_sem=shs.at[n], recv_sem=shr.at[n],
             device_id=dev(z, x, y, 1 - c), device_id_type=MESH,
         )
     if ex is not None:
@@ -963,7 +964,7 @@
     if shared_rows:
         e = exchanged
         operands += [e]
-        out_shape += [jax.ShapeDtypeStruct(e.shape, e.dtype), jax.ShapeDtypeStruct((ny * 2, e.shape[0], shared_rows, e.shape[2]), e.dtype)]
+        out_shape += [jax.ShapeDtypeStruct(e.shape, e.dtype), jax.ShapeDtypeStruct((e.shape[0], ny * 2, shared_rows, e.shape[2]), e.dtype)]
         more = exchange_scratch(nz * nx) + [D((3,)), D((3,)), D]
     out = pl.pallas_call(
         functools.partial(ag_kernel, dims, halves, shared_rows),
@@ -1291,19 +1292,26 @@
     )(p)
 
 
-def layout(first, order, group_rows, block):
-    places = jnp.arange(group_rows, dtype=jnp.int32)
-    anchor = jnp.repeat(order, block, axis=1) * block + places % block
-    doc = (anchor >= first).astype(jnp.int32)
-    return (anchor, anchor - doc * first)
-
-
-def rotary_tables(place):
+def layout(first, order, block):
+    groups, blocks = order.shape
+    rows = groups * blocks * block
+    step = jnp.arange(block, dtype=jnp.int32)
+    anchor = order[:, :, None] * block + step
+    late = anchor >= first[:, :, None]
+    place = anchor - jnp.where(late, first[:, :, None], 0)
     half = LANES // 2
     freq = jnp.exp(jnp.arange(half, dtype=f32) * (-2.0 * math.log(10000.0) / LANES))
-    angle = place.astype(f32)[:, None] * freq[None, :]
-    cos, sin = jnp.cos(angle), jnp.sin(angle)
-    return (jnp.concatenate([cos, cos], axis=1), jnp.concatenate([-sin, sin], axis=1))
+    freq = jnp.concatenate([freq, freq])
+    sign = jnp.where(jnp.arange(LANES) < half, -1.0, 1.0)
+    inner = step.astype(f32)[:, None] * freq
+    start = (order * block).astype(f32)[:, :, None, None] * freq
+    moved = (order * block - first).astype(f32)[:, :, None, None] * freq
+    chosen_cos = jnp.where(late[..., None], jnp.cos(moved), jnp.cos(start))
+    chosen_sin = jnp.where(late[..., None], jnp.sin(moved), jnp.sin(start))
+    cos = jnp.cos(inner) * chosen_cos - jnp.sin(inner) * chosen_sin
+    sin = (jnp.sin(inner) * chosen_cos + jnp.cos(inner) * chosen_sin) * sign
+    flat = lambda v: v.reshape(groups, blocks * block)
+    return (flat(anchor), flat(place), cos.reshape(rows, LANES), sin.reshape(rows, LANES))
 
 
 def logit_grad(route, gates, difference, experts):
@@ -1385,7 +1393,7 @@
     small = jnp.pad(small, ((0, 0), (0, LANES - small.shape[1])))
 
     query_low = query_master[0].astype(bf16)
-    kv_low = kv_master.astype(bf16).reshape(depth * 2, groups, cw)
+    kv_low = kv_master.astype(bf16).reshape(depth, 2, groups, cw).transpose(1, 0, 2, 3).reshape(2 * depth, groups, cw)
     query_rows = query_low.shape[0]
     pieces_out = jnp.concatenate([query_low.reshape(query_rows, groups, cw), kv_low], axis=0).transpose(1, 0, 2)
     if dims is None:
@@ -1399,9 +1407,8 @@
         tokens = tokens.reshape(total, width + LANES)
         tokens, late_grad = lax.optimization_barrier((tokens, out_grad))
         extra = tokens[:, width:]
-        kv_all = kv_all.transpose(1, 0, 2, 3)
     query_weight = pieces_in[:, :query_rows].reshape(width, cw)
-    kv_weight = kv_all.reshape(width, 2 * cw)
+    key_weight, value_weight = (kv_all[:, :, at : at + depth].reshape(width, cw) for at in (0, depth))
 
     output_weight = output_master[0].astype(bf16)
 
@@ -1414,10 +1421,8 @@
     column = extra.reshape(groups, group_rows, LANES)[:, : blocks + 2, at_route + 4].astype(jnp.int32)
 
     def where_rows_stand(column):
-        anchor, place = layout(
-            column[:, 0:1] * 16 + column[:, 1:2], column[:, 2:], group_rows, own_rows // 2
-        )
-        cos, sin = rotary_tables(place.reshape(total))
+        first = column[:, 0:1] * 16 + column[:, 1:2]
+        anchor, place, cos, sin = layout(first, column[:, 2:], own_rows // 2)
         meta = jnp.concatenate(
             [anchor.reshape(total, 1), (anchor - place).reshape(total, 1), routes, routes[:, :2]], axis=1
         )
@@ -1425,7 +1430,7 @@
 
     cos, sin, meta, key_rows = where_rows_stand(column)
     gain_one, gain_two = gains[:, 0], gains[:, 1]
-    w_all = jnp.concatenate([query_weight, kv_weight, wide(router[:, :experts])], axis=1)
+    w_all = jnp.concatenate([query_weight, key_weight, value_weight, wide(router[:, :experts])], axis=1)
 
     qkv, att, aux, wg, wu, wd, attn_sum = attn_forward(
         dims, 3, me, tokens, gain_one[None], w_all, output_weight, cos, sin, meta, key_rows,
@@ -1443,10 +1448,11 @@
     h2 = gather_all(hidden_two, 4).reshape(total, width)
     tops = lax.all_gather(late_grad, both, axis=0, tiled=True)
 
-    named = (routes[:, 2] == member) | (routes[:, 3] == member)
-    named = named.reshape(devices, own_rows)
-    position = jnp.cumsum(named.astype(jnp.int32), axis=1) - 1
-    position = jnp.where(named, position, -1)
+    if is_dense(capacity):
+        position = jnp.zeros((devices, own_rows), jnp.int32)
+    else:
+        named = ((routes[:, 2] == member) | (routes[:, 3] == member)).reshape(devices, own_rows)
+        position = jnp.where(named, jnp.cumsum(named.astype(jnp.int32), axis=1) - 1, -1)
     tile_blocks = 4
     position = position.reshape(devices // tile_blocks, tile_blocks, own_rows)
     produced, ffn_aux, act, dgate, dup, *dh2_parts = ffn(

time: 1030 us -> 997 us (0.968)
  other arithmetic: 46.3 us -> 29.5 us
  local copies, waits for them, and re-layouts: 63.6 us -> 52.2 us
    pallas_call x1, Pallas kernels: 162 us -> 151 us  [attn_backward(): pl.pallas_call(kernel, grid=(groups + 2 + dims[0] if dims else groups,),...]
    unnamed x63 -> x50, local copies, waits for them, and re-layouts: 27.8 us -> 22.7 us
  transfers between devices with their start and end apart: 1 -> 1, of which waited for: 0 -> 0; matrix products, arithmetic and copies ran while one was open for 5% -> 2% of each run, Pallas kernels for 23% -> 25%
where the time goes in v4:
time: 997 us; the launch traced here: 992 us
  Pallas kernels  885 us (89%)
  local copies, waits for them, and re-layouts  52.2 us (5%)
  other arithmetic  29.5 us (3%)
  between operations  17.4 us (2%)
    pallas_call x3, Pallas kernels, gather_kernel(): pl.pallas_call(functools.partial(ag_kernel, dims, halves, shared_rows), o...  257 us
    pallas_call x1, Pallas kernels, attn_forward(): pl.pallas_call(kernel, grid=(groups + 2 + dims[0] if dims else groups,),...  172 us
    pallas_call x1, Pallas kernels, ffn(): pl.pallas_call(kernel, grid=(tiles + 2 + dims[0] if dims else tiles,), in...  169 us
    pallas_call x1, Pallas kernels, attn_backward(): pl.pallas_call(kernel, grid=(groups + 2 + dims[0] if dims else groups,),...  151 us
    pallas_call x1, Pallas kernels, ffn_weights(): pl.pallas_call(kernel, grid=(tiles + 2 + dims[0] if dims else tiles,), in...  136 us
    unnamed x50, local copies, waits for them, and re-layouts  22.7 us
  transfers between devices with their start and end apart: 1, of which 0 were waited for; matrix products, arithmetic and copies ran while one was open for 2% of the time, Pallas kernels for 25%

profile of v4, /device:TPU:22, one launch (start us, length us, event | category | flops | bytes accessed | tf_op | source)
XLA Modules:
  0.0 991.7 jit_solution(6415586858625134647)
XLA Ops:
  14.5 1.8 copy.62
  19.0 108.6 %shard_map.196 = (bf16[32,128,2176]{2,1,0:T(8,128)(2,1)}, bf16[8,384,256]{2,1,0:T(8,128)(2,1)}, bf16[8,4,128,256]{3,2,1,0:T(8,128)(2,1)}) custom-call(bf16[128,2176]{1,0:T(8,128)(2,1)} %fusion.18.refs_0_, bf16[8,384,256]{2,1,0:T(8,128)(2,1)} %maximum_bitcast_fusion.refs_1_), custom_call_target="tpu_custom_call" | custom-call | tf_op jit(solution)/shard_map/pallas_call | solution.py:969
  129.7 1.6 slice.124
  136.0 1.9 copy.67.meta
  138.6 2.6 fusion.4
  143.0 2.1 fusion.1.w_all
  147.7 172.0 %shard_map.197 = (bf16[4096,768]{1,0:T(8,128)(2,1)}, bf16[4096,256]{1,0:T(8,128)(2,1)}, f32[4096,128]{1,0:T(8,128)}, bf16[704,2048]{1,0:T(8,128)(2,1)}, bf16[704...) custom-call(s32[1]{0:T(128)} %bitcast.me, bf16[4096,2176]{1,0:T(8,128)(2,1)} %bitcast.121, ...), custom_call_target="tpu_custom_call" | custom-call | tf_op jit(solution)/shard_map/pallas_call | solution.py:256
  323.2 74.1 %shard_map.198 = bf16[32,128,2048]{2,1,0:T(8,128)(2,1)} custom-call(bf16[128,2048]{1,0:T(8,128)(2,1)} %multiply_convert_fusion.refs_0_), custom_call_target="tpu_custom_call" | custom-call | tf_op jit(solution)/shard_map/pallas_call | solution.py:969
  398.0 168.9 %shard_map.199 = (bf16[4096,2048]{1,0:T(8,128)(2,1)}, f32[4096,128]{1,0:T(8,128)}, bf16[4096,704]{1,0:T(8,128)(2,1)}, bf16[4096,704]{1,0:T(8,128)(2,1)}, bf16[4096,704]{1,0:T(8,128)(2,1)}, /*index=5*/f32[128,2176]{1,0:T(8,128)}) custom-call(s32[1]{0:T(128)} %bitcast.me, bf16[4096,2048]{1,0:T(8,128)(2,1)} %bitcast.117, ...), custom_call_target="tpu_custom_call" | custom-call | tf_op jit(solution)/shard_map/pallas_call | solution.py:528
  568.0 1.6 convolution_convert_fusion
  569.6 2.6 multiply_reduce_fusion
  574.3 73.8 %shard_map.200 = bf16[32,128,2048]{2,1,0:T(8,128)(2,1)} custom-call(bf16[128,2048]{1,0:T(8,128)(2,1)} %fusion.49.refs_0_), custom_call_target="tpu_custom_call" | custom-call | tf_op jit(solution)/shard_map/pallas_call | solution.py:969
  648.2 150.9 %shard_map.201 = (f32[768,2048]{1,0:T(8,128)}, f32[256,2048]{1,0:T(8,128)}, f32[128,2176]{1,0:T(8,128)}) custom-call(bf16[4096,2048]{1,0:T(8,128)(2,1)} %bitcast.123, bf16[4096,2176]{1,0:T(8,128)(2,1)} %bitcast.122, f32[1,2048]{1,0:T(1,128)} %bitcast.153, bf16[4096,768]{1,0:T(8,128)(2,1)} %get-tuple-element.50.qkv, bf16[4096,256]{1,0:T(8,128)(2,1)} %get-tuple-element.51.att, ...), custom_call_target="tpu_custom_call" | custom-call | tf_op jit(solution)/shard_map/pallas_call | solution.py:318
  800.7 3.1 fusion.12
  803.8 3.3 convert_element_type.137
  807.1 1.7 copy-done.3
  810.7 2.9 reshape.388
  813.6 3.5 copy.84
  818.9 136.4 %shard_map.202 = (f32[704,2,2048]{2,1,0:T(2,128)}, f32[704,2048]{1,0:T(8,128)}, f32[128,2176]{1,0:T(8,128)}, bf16[8,256,256]{2,1,0:T(8,128)(2,1)}, bf16[8,256,12...) custom-call(bf16[4096,2048]{1,0:T(8,128)(2,1)} %bitcast.118, bf16[4096,2048]{1,0:T(8,128)(2,1)} %all-gather.2.cloned.1.call-done.top, ...), custom_call_target="tpu_custom_call" | custom-call | tf_op jit(solution)/shard_map/pallas_call | solution.py:735
  958.3 2.2 fusion.17
  963.8 3.0 copy.75
  966.9 3.3 fusion.15
  971.5 10.6 %copy.89 = f32[1,704,2,2048]{3,2,1,0:T(2,128)} copy(f32[1,704,2,2048]{3,2,1,0:T(2,128)} %bitcast.129) | data formatting | bytes 23068672
  982.1 2.5 copy.90
  (129 shorter events, 39.3 us)
Async XLA Ops:
  7.2 390.2 %all-gather.2.cloned.1.call-start = ((), (), s32[]{:S(2)}) async-start(), calls=%async_computation | async-start | bytes 17301504 | tf_op jit(solution)/shard_map/all_gather | solution.py:1449
  14.5 2.4 copy-start.6
  128.9 2.9 copy-start.11
  141.2 1.6 copy-start.13
  143.0 2.9 copy-start.12
  321.3 1.0 copy-start
  568.0 5.2 copy-start.1
  568.0 5.2 copy-start.9
  572.2 1.0 copy-start.4
  648.1 152.0 %copy-start.7 = (bf16[128,2048]{1,0:T(8,128)(2,1)S(1)}, bf16[128,2048]{1,0:T(8,128)(2,1)}, u32[]{:S(2)}) copy-start(bf16[128,2048]{1,0:T(8,128)(2,1)} %param.13) | copy-start | bytes 1572868
  648.1 152.0 %copy-start.16 = (f32[2048]{0:T(1024)S(1)}, f32[2048]{0:T(1024)}, u32[]{:S(2)}) copy-start(f32[2048]{0:T(1024)} %get-tuple-element.95) | copy-start | bytes 24580
  807.1 1.7 copy-start.3
  808.7 1.9 slice-start.1
  813.5 3.6 slice-start
  960.7 1.6 copy-start.15
  963.8 3.0 copy-start.2
  963.8 3.0 copy-start.5
  963.8 3.1 copy-start.8
  963.8 3.1 copy-start.10
  966.9 3.3 copy-start.14
  970.2 11.9 %slice-start.2 = ((s8[5767168]{0:T(1024)(128)(4,1)}), s8[4194304]{0:T(1024)(128)(4,1)S(1)}, s32[]{:S(2)}) async-start(s8[5767168]{0:T(1024)(128)(4,1)} %bitcast.132), calls=%async_computation.3 | async-start | bytes 8388608
  971.5 10.6 %slice-start.3 = ((s8[5767168]{0:T(1024)(128)(4,1)}), s8[1572864]{0:T(1024)(128)(4,1)S(1)}, s32[]{:S(2)}) async-start(s8[5767168]{0:T(1024)(128)(4,1)} %bitcast.132), calls=%async_computation.4 | async-start | bytes 3145728
Sparse Core Ops, SparseCore 0:
  127.7 173.9 all-gather.1

commit v5 on v4

--- a/solution.py
+++ b/solution.py
@@ -562,12 +562,12 @@
         fs = slice(start, start + size)
 
         def grads(i, fs=fs):
-            at = rows_at(i, 512)
+            at = rows_at(i, 1024)
             sd[fs, at] += tn(act[:, fs], gc[:, at])
             sg[fs, at] += tn(dgate[:, fs], xs[:, at])
             su[fs, at] += tn(dup[:, fs], xs[:, at])
 
-        loop(width // 512, grads)
+        loop(width // 1024, grads)
 
 
 def ffn_weights_out(gate_up_grad, down_grad, sg, su, sd, sems):

time: 997 us -> 991 us (level)
  no operation moved by 1% of the time
where the time goes in v5:
time: 991 us; the launch traced here: 985 us
  Pallas kernels  878 us (89%)
  local copies, waits for them, and re-layouts  52.2 us (5%)
  other arithmetic  29.5 us (3%)
  between operations  17.4 us (2%)
    pallas_call x3, Pallas kernels, gather_kernel(): pl.pallas_call(functools.partial(ag_kernel, dims, halves, shared_rows), o...  257 us
    pallas_call x1, Pallas kernels, attn_forward(): pl.pallas_call(kernel, grid=(groups + 2 + dims[0] if dims else groups,),...  172 us
    pallas_call x1, Pallas kernels, ffn(): pl.pallas_call(kernel, grid=(tiles + 2 + dims[0] if dims else tiles,), in...  169 us
    pallas_call x1, Pallas kernels, attn_backward(): pl.pallas_call(kernel, grid=(groups + 2 + dims[0] if dims else groups,),...  151 us
    pallas_call x1, Pallas kernels, ffn_weights(): pl.pallas_call(kernel, grid=(tiles + 2 + dims[0] if dims else tiles,), in...  130 us
    unnamed x50, local copies, waits for them, and re-layouts  22.7 us
  transfers between devices with their start and end apart: 1, of which 0 were waited for; matrix products, arithmetic and copies ran while one was open for 2% of the time, Pallas kernels for 25%

profile of v5, /device:TPU:22, one launch (start us, length us, event | category | flops | bytes accessed | tf_op | source)
XLA Modules:
  0.0 985.3 jit_solution(13513938334640467620)
XLA Ops:
  14.5 1.8 copy.62
  19.0 108.6 %shard_map.196 = (bf16[32,128,2176]{2,1,0:T(8,128)(2,1)}, bf16[8,384,256]{2,1,0:T(8,128)(2,1)}, bf16[8,4,128,256]{3,2,1,0:T(8,128)(2,1)}) custom-call(bf16[128,2176]{1,0:T(8,128)(2,1)} %fusion.18.refs_0_, bf16[8,384,256]{2,1,0:T(8,128)(2,1)} %maximum_bitcast_fusion.refs_1_), custom_call_target="tpu_custom_call" | custom-call | tf_op jit(solution)/shard_map/pallas_call | solution.py:969
  129.7 1.6 slice.124
  136.0 1.9 copy.67.meta
  138.6 2.6 fusion.4
  143.0 2.1 fusion.1.w_all
  147.7 172.0 %shard_map.197 = (bf16[4096,768]{1,0:T(8,128)(2,1)}, bf16[4096,256]{1,0:T(8,128)(2,1)}, f32[4096,128]{1,0:T(8,128)}, bf16[704,2048]{1,0:T(8,128)(2,1)}, bf16[704...) custom-call(s32[1]{0:T(128)} %bitcast.me, bf16[4096,2176]{1,0:T(8,128)(2,1)} %bitcast.121, ...), custom_call_target="tpu_custom_call" | custom-call | tf_op jit(solution)/shard_map/pallas_call | solution.py:256
  323.2 74.1 %shard_map.198 = bf16[32,128,2048]{2,1,0:T(8,128)(2,1)} custom-call(bf16[128,2048]{1,0:T(8,128)(2,1)} %multiply_convert_fusion.refs_0_), custom_call_target="tpu_custom_call" | custom-call | tf_op jit(solution)/shard_map/pallas_call | solution.py:969
  398.0 168.9 %shard_map.199 = (bf16[4096,2048]{1,0:T(8,128)(2,1)}, f32[4096,128]{1,0:T(8,128)}, bf16[4096,704]{1,0:T(8,128)(2,1)}, bf16[4096,704]{1,0:T(8,128)(2,1)}, bf16[4096,704]{1,0:T(8,128)(2,1)}, /*index=5*/f32[128,2176]{1,0:T(8,128)}) custom-call(s32[1]{0:T(128)} %bitcast.me, bf16[4096,2048]{1,0:T(8,128)(2,1)} %bitcast.117, ...), custom_call_target="tpu_custom_call" | custom-call | tf_op jit(solution)/shard_map/pallas_call | solution.py:528
  568.0 1.6 convolution_convert_fusion
  569.6 2.6 multiply_reduce_fusion
  574.3 73.8 %shard_map.200 = bf16[32,128,2048]{2,1,0:T(8,128)(2,1)} custom-call(bf16[128,2048]{1,0:T(8,128)(2,1)} %fusion.49.refs_0_), custom_call_target="tpu_custom_call" | custom-call | tf_op jit(solution)/shard_map/pallas_call | solution.py:969
  648.2 150.9 %shard_map.201 = (f32[768,2048]{1,0:T(8,128)}, f32[256,2048]{1,0:T(8,128)}, f32[128,2176]{1,0:T(8,128)}) custom-call(bf16[4096,2048]{1,0:T(8,128)(2,1)} %bitcast.123, bf16[4096,2176]{1,0:T(8,128)(2,1)} %bitcast.122, f32[1,2048]{1,0:T(1,128)} %bitcast.153, bf16[4096,768]{1,0:T(8,128)(2,1)} %get-tuple-element.50.qkv, bf16[4096,256]{1,0:T(8,128)(2,1)} %get-tuple-element.51.att, ...), custom_call_target="tpu_custom_call" | custom-call | tf_op jit(solution)/shard_map/pallas_call | solution.py:318
  800.7 3.1 fusion.12
  803.8 3.3 convert_element_type.137
  807.1 1.7 copy-done.3
  810.7 2.9 reshape.388
  813.6 3.5 copy.84
  818.9 130.1 %shard_map.202 = (f32[704,2,2048]{2,1,0:T(2,128)}, f32[704,2048]{1,0:T(8,128)}, f32[128,2176]{1,0:T(8,128)}, bf16[8,256,256]{2,1,0:T(8,128)(2,1)}, bf16[8,256,12...) custom-call(bf16[4096,2048]{1,0:T(8,128)(2,1)} %bitcast.118, bf16[4096,2048]{1,0:T(8,128)(2,1)} %all-gather.2.cloned.1.call-done.top, ...), custom_call_target="tpu_custom_call" | custom-call | tf_op jit(solution)/shard_map/pallas_call | solution.py:735
  951.9 2.2 fusion.17
  957.5 3.0 copy.75
  960.5 3.3 fusion.15
  965.1 10.6 %copy.89 = f32[1,704,2,2048]{3,2,1,0:T(2,128)} copy(f32[1,704,2,2048]{3,2,1,0:T(2,128)} %bitcast.129) | data formatting | bytes 23068672
  975.7 2.5 copy.90
  (129 shorter events, 39.3 us)
Async XLA Ops:
  7.2 390.2 %all-gather.2.cloned.1.call-start = ((), (), s32[]{:S(2)}) async-start(), calls=%async_computation | async-start | bytes 17301504 | tf_op jit(solution)/shard_map/all_gather | solution.py:1449
  14.5 2.4 copy-start.6
  128.9 2.9 copy-start.11
  141.2 1.6 copy-start.13
  143.0 2.9 copy-start.12
  321.3 1.0 copy-start
  568.0 5.2 copy-start.1
  568.0 5.2 copy-start.9
  572.2 1.0 copy-start.4
  648.1 152.0 %copy-start.7 = (bf16[128,2048]{1,0:T(8,128)(2,1)S(1)}, bf16[128,2048]{1,0:T(8,128)(2,1)}, u32[]{:S(2)}) copy-start(bf16[128,2048]{1,0:T(8,128)(2,1)} %param.13) | copy-start | bytes 1572868
  648.1 152.0 %copy-start.16 = (f32[2048]{0:T(1024)S(1)}, f32[2048]{0:T(1024)}, u32[]{:S(2)}) copy-start(f32[2048]{0:T(1024)} %get-tuple-element.95) | copy-start | bytes 24580
  807.1 1.7 copy-start.3
  808.7 1.9 slice-start.1
  813.5 3.6 slice-start
  954.3 1.6 copy-start.15
  957.4 3.0 copy-start.2
  957.4 3.0 copy-start.5
  957.4 3.1 copy-start.8
  957.5 3.1 copy-start.10
  960.5 3.3 copy-start.14
  963.8 11.9 %slice-start.2 = ((s8[5767168]{0:T(1024)(128)(4,1)}), s8[4194304]{0:T(1024)(128)(4,1)S(1)}, s32[]{:S(2)}) async-start(s8[5767168]{0:T(1024)(128)(4,1)} %bitcast.132), calls=%async_computation.3 | async-start | bytes 8388608
  965.1 10.6 %slice-start.3 = ((s8[5767168]{0:T(1024)(128)(4,1)}), s8[1572864]{0:T(1024)(128)(4,1)S(1)}, s32[]{:S(2)}) async-start(s8[5767168]{0:T(1024)(128)(4,1)} %bitcast.132), calls=%async_computation.4 | async-start | bytes 3145728
Sparse Core Ops, SparseCore 0:
  127.7 173.9 all-gather.1
